TPU v7x, 32 devices: a whole 2x2x4 slice. The times are simulated.
32 devices in a mesh: gx: 2 (over x), gy: 4 (over y, core), ta: 4 (over z).
Axes of the slice: x: 2, y: 2, z: 4, core: 2. Of those that a mesh axis runs over, the one named last changes fastest.
Arguments:
- frames: bfloat16 [32, 16, 256, 128], P('ta', 'gx', 'gy'), may hold values from -6 to 6
- in_weight: bfloat16 [3, 3, 128, 128], replicated, may hold values from -0.1875 to 0.1875
- out_weight: bfloat16 [3, 3, 128, 128], replicated, may hold values from -0.1875 to 0.1875
- decays: float32 [32, 128], P('ta'), may hold values from 0.05 to 0.999, as said below
Outputs:
- mixed_frames: bfloat16 [32, 16, 256, 128], P('ta', 'gx', 'gy')
Inputs may be any that keep to these rules, and one draw needn't show every extreme that they name: `decays`: every factor lies strictly between 0 and 1.
All inputs are finite; a program needn't handle non-finite values.
Results may differ from a plain program's by a relative error of at most 0.0031.
Values may be sent and summed in bfloat16 or wider, within the bound.
No kernel may reach another device: no remote copies, remote signals or barrier semaphores. Data moves between devices by JAX's collectives and lax.ppermute only.
A program may use at most 64 MiB of HBM per device.

v0:
```python
import jax
import jax.numpy as jnp
from jax import lax
from jax.sharding import PartitionSpec as P


def padded_2(cells, sides, width):
    for axis, dim in sides:
        count = lax.axis_size(axis)
        ends = count - 1
        head = lax.slice_in_dim(cells, 0, width, axis=dim)
        tail = lax.slice_in_dim(cells, cells.shape[dim] - width, cells.shape[dim], axis=dim)
        cells = jnp.concatenate(
            [
                lax.ppermute(tail, axis, [(i, (i + 1) % count) for i in range(ends)]),
                cells,
                lax.ppermute(head, axis, [((i + 1) % count, i) for i in range(ends)]),
            ],
            axis=dim,
        )
    return cells


def entering(value, axis, join, neutral):
    count, mine = (lax.axis_size(axis), lax.axis_index(axis))
    pieces = jax.tree.map(lambda part: lax.all_gather(part, axis), value)
    so_far = jax.tree.map(
        lambda part, zero: jnp.full_like(part, 0) + jnp.asarray(zero, part.dtype), value, neutral
    )

    def step(position, so_far):
        longer = join(so_far, jax.tree.map(lambda part: part[position], pieces))
        return jax.tree.map(lambda new, old: jnp.where(position < mine, new, old), longer, so_far)

    return lax.fori_loop(0, count - 1, step, so_far)


def convolve(padded, weight, height, across):
    summed = None
    for row_off in range(3):
        for col_off in range(3):
            partial_term = jnp.einsum(
                "fhwc,cp->fhwp",
                padded[:, row_off : row_off + height, col_off : col_off + across, :],
                weight[row_off, col_off],
                preferred_element_type=jnp.float32,
            )
            summed = partial_term if summed is None else summed + partial_term
    return summed


def chain_step(earlier, latter):
    return (earlier[0] * latter[0], latter[0] * earlier[1] + latter[1])


def advance(carry, inputs):
    running, current = carry
    factors, drive = inputs
    running = running * factors
    current = factors * current + drive
    return ((running, current), (running, current))


def on_device(frames, in_weight, out_weight, decays):
    height = frames.shape[1]
    across = frames.shape[2]
    padded = padded_2(frames, (("gx", 1), ("gy", 2)), 1)
    driven = convolve(padded, in_weight, height, across)
    scaled = jnp.sqrt(1.0 - decays * decays)[:, None, None, :] * driven
    start_carry = (
        jnp.ones((decays.shape[1],), jnp.float32),
        jnp.zeros(scaled.shape[1:], jnp.float32),
    )
    running, partial_states = lax.scan(advance, start_carry, (decays, scaled))[1]
    incoming = entering((running[-1], partial_states[-1]), "ta", chain_step, start_carry)
    states = partial_states + running[:, None, None, :] * incoming[1][None]
    rounded = states.astype(jnp.bfloat16)
    state_pad = padded_2(rounded, (("gx", 1), ("gy", 2)), 1)
    mixed = convolve(state_pad, out_weight, height, across)
    return (frames.astype(jnp.float32) + jax.nn.gelu(mixed)).astype(jnp.bfloat16)


def solution(mesh):
    placed = (P("ta", "gx", "gy", None), P(), P(), P("ta", None))
    return jax.shard_map(
        on_device, mesh=mesh, in_specs=placed, out_specs=P("ta", "gx", "gy", None), check_vma=False
    )
```

profile of v0, /device:TPU:1, one launch (start us, length us, event | category | flops | bytes accessed | tf_op | source)
XLA Modules:
  0.0 113.9 jit_solution(15263736830823109384)
XLA Ops:
  6.5 1.8 %fusion.109 = (bf16[8,1,64,128]{3,2,1,0:T(8,128)(2,1)}, bf16[8,1,64,128]{3,2,1,0:T(8,128)(2,1)}) fusion(bf16[8,8,64,128]{3,2,1,0:T(8,128)(2,1)} %param.8), kind=kLoop, calls=%fused_computation.132 | loop fusion | bytes 524288 | tf_op jit(solution)/shard_map/slice | solution.py:12
  8.3 3.9 %collective-permute-start = (bf16[8,1,64,128]{3,2,1,0:T(8,128)(2,1)}, bf16[8,1,64,128]{3,2,1,0:T(8,128)(2,1)S(1)}, u32[]{:S(2)}, u32[]{:S(2)}) collective-permute-start(bf16[8,1,64,128]{3,2,1,0:T(8,128)(2,1)} %get-tuple-element.218), channel_id=1, source_target_pairs={{0,16},{1,17},{2,18},{3,19},{4,20},{5,21},{6,22},{7,23},{8,24},{9,... | collective-permute-start | bytes 393224 | tf_op jit(solution)/shard_map/ppermute | solution.py:15
  12.3 1.3 %collective-permute-start.1 = (bf16[8,1,64,128]{3,2,1,0:T(8,128)(2,1)}, bf16[8,1,64,128]{3,2,1,0:T(8,128)(2,1)}, u32[]{:S(2)}, u32[]{:S(2)}) collective-permute-start(bf16[8,1,64,128]{3,2,1,0:T(8,128)(2,1)} %get-tuple-element.219), channel_id=1, source_target_pairs={{16,0},{17,1},{18,2},{19,3},{20,4},{21,5},{22,6},{23,7},{24,8},{25... | collective-permute-start | bytes 393224 | tf_op jit(solution)/shard_map/ppermute | solution.py:17
  13.6 1.6 %fusion.72 = f32[8,8,64,128]{3,2,1,0:T(8,128)S(1)} fusion(bf16[8,8,64,128]{3,2,1,0:T(8,128)(2,1)} %param.8, bf16[3,3,128,128]{3,2,1,0:T(8,128)(2,1)} %param.9), kind=kOutput, calls=%fused_computation.91 | convolution fusion | flops 134217728 | bytes 3178496 | tf_op jit(solution)/shard_map/fhwc,cp->fhwp/dot_general | solution.py:42
  15.5 2.8 %collective-permute-done.1 = bf16[8,1,64,128]{3,2,1,0:T(8,128)(2,1)} collective-permute-done((bf16[8,1,64,128]{3,2,1,0:T(8,128)(2,1)}, bf16[8,1,64,128]{3,2,1,0:T(8,128)(2,1)}, u32[]{:S(2)}, u32[]{:S(2)}) %collective-permute-start.1) | collective-permute-done | bytes 131104 | tf_op jit(solution)/shard_map/ppermute | solution.py:17
  18.3 0.9 constant_dynamic-update-slice_fusion
  19.3 4.0 %collective-permute-start.3 = (bf16[8,10,1,128]{3,2,1,0:T(2,128)(2,1)S(1)}, bf16[8,10,1,128]{3,2,1,0:T(2,128)(2,1)S(1)}, u32[]{:S(2)}, u32[]{:S(2)}) collective-permute-start(bf16[8,10,1,128]{3,2,1,0:T(2,128)(2,1)S(1)} %get-tuple-element.214), channel_id=1, source_target_pairs={{4,0},{8,4},{12,8},{5,1},{9,5},{13,9},{6,2},{10,6},{14,10},{7,3},{... | collective-permute-start | bytes 61448 | tf_op jit(solution)/shard_map/ppermute | solution.py:17
  23.3 3.0 %collective-permute-start.2 = (bf16[8,10,1,128]{3,2,1,0:T(2,128)(2,1)S(1)}, bf16[8,10,1,128]{3,2,1,0:T(2,128)(2,1)S(1)}, u32[]{:S(2)}, u32[]{:S(2)}) collective-permute-start(bf16[8,10,1,128]{3,2,1,0:T(2,128)(2,1)S(1)} %get-tuple-element.215), channel_id=1, source_target_pairs={{0,4},{4,8},{8,12},{1,5},{5,9},{9,13},{2,6},{6,10},{10,14},{3,7},{... | collective-permute-start | bytes 61448 | tf_op jit(solution)/shard_map/ppermute | solution.py:15
  26.4 0.4 fusion.12
  26.8 1.3 %fusion.16 = f32[8,8,64,128]{3,2,1,0:T(8,128)S(1)} fusion(bf16[8,1,64,128]{3,2,1,0:T(8,128)(2,1)} %collective-permute-done.1, bf16[8,8,64,128]{3,2,1,0:T(8,128)(2,1)S(1)} %copy-done, bf16[3,3,128,128]{3,2,1,0:T(8,128)(2,1)S(1)} %copy-done.1), kind=kOutput, calls=%fused_computation.36 | convolution fusion | flops 136577024 | bytes 3309568 | tf_op jit(solution)/shard_map/fhwc,cp->fhwp/dot_general | solution.py:42
  28.1 0.4 fusion.29
  28.6 0.4 fusion.32
  29.0 0.4 fusion.35
  29.5 0.4 fusion.38
  29.9 0.4 fusion.56
  30.4 2.6 %add_multiply_fusion = f32[8,8,64,128]{3,2,1,0:T(8,128)} fusion(f32[8,8,64,128]{3,2,1,0:T(8,128)S(1)} %fusion.16, f32[8,8,64,128]{3,2,1,0:T(8,128)S(1)} %fusion.56, f32[8,8,64,128]{3,2,1,0:T(8,128)S(1)} %fusion.29, f32[8,8,64,128]{3,2,1,0:T(8,128)S(1)} %fusion.72, f32[8,8,64,128]{3,2,1,0:T(8,128)S(1)} %fusion.35, f32[8,8,64,128]{3,2,1,0:T(8,128)S(1)} %fusion.32, ...), kind=kOutput, calls=%fused_computation.21 | convolution fusion | flops 141033472 | bytes 20262912 | tf_op jit(solution)/shard_map/fhwc,cp->fhwp/dot_general | solution.py:42
  32.9 14.5 %while.31 = (s32[]{:T(128)}, f32[128]{0:T(128)S(1)}, f32[8,64,128]{2,1,0:T(8,128)S(1)}, f32[8,128]{1,0:T(8,128)S(1)}, f32[8,8,64,128]{3,2,1,0:T(8,128)}, /*index...) while((s32[]{:T(128)}, f32[128]{0:T(128)S(1)}, ...), condition=%wide.region_1.2_spmd.clone, body=%wide.region_0.1_spmd.clone.sunk | while | flops 196867 | bytes 1052784 | solution.py:74
  32.9 1.8 %bitcast_dynamic-update-slice_fusion.2 = (f32[8,8,64,128]{3,2,1,0:T(8,128)}, f32[8,64,128]{2,1,0:T(8,128)S(1)}) fusion(f32[8,8,64,128]{3,2,1,0:T(8,128)} %get-tuple-element.315, s32[]{:T(128)} %get-tuple-element.311, f32[8,8,64,128]{3,2,1,0:T(8,128)} %get-tuple-element.326, f32[8,64,128]{2,1,0:T(8,128)S(1)} %get-tuple-element.313, pred[]{:T(512)S(6)} %compare.6, ...), kind=kLoop, calls=%fused_computation.clone.1 | loop fusion | flops 196608 | bytes 1049601 | tf_op jit(solution)/shard_map/while/body/jit(dynamic_update_index_in_dim)/dynamic_update_slice | solution.py:74
  34.8 1.8 %bitcast_dynamic-update-slice_fusion.2 = (f32[8,8,64,128]{3,2,1,0:T(8,128)}, f32[8,64,128]{2,1,0:T(8,128)S(1)}) fusion(f32[8,8,64,128]{3,2,1,0:T(8,128)} %get-tuple-element.315, s32[]{:T(128)} %get-tuple-element.311, f32[8,8,64,128]{3,2,1,0:T(8,128)} %get-tuple-element.326, f32[8,64,128]{2,1,0:T(8,128)S(1)} %get-tuple-element.313, pred[]{:T(512)S(6)} %compare.6, ...), kind=kLoop, calls=%fused_computation.clone.1 | loop fusion | flops 196608 | bytes 1049601 | tf_op jit(solution)/shard_map/while/body/jit(dynamic_update_index_in_dim)/dynamic_update_slice | solution.py:74
  36.6 1.8 %bitcast_dynamic-update-slice_fusion.2 = (f32[8,8,64,128]{3,2,1,0:T(8,128)}, f32[8,64,128]{2,1,0:T(8,128)S(1)}) fusion(f32[8,8,64,128]{3,2,1,0:T(8,128)} %get-tuple-element.315, s32[]{:T(128)} %get-tuple-element.311, f32[8,8,64,128]{3,2,1,0:T(8,128)} %get-tuple-element.326, f32[8,64,128]{2,1,0:T(8,128)S(1)} %get-tuple-element.313, pred[]{:T(512)S(6)} %compare.6, ...), kind=kLoop, calls=%fused_computation.clone.1 | loop fusion | flops 196608 | bytes 1049601 | tf_op jit(solution)/shard_map/while/body/jit(dynamic_update_index_in_dim)/dynamic_update_slice | solution.py:74
  38.4 1.8 %bitcast_dynamic-update-slice_fusion.2 = (f32[8,8,64,128]{3,2,1,0:T(8,128)}, f32[8,64,128]{2,1,0:T(8,128)S(1)}) fusion(f32[8,8,64,128]{3,2,1,0:T(8,128)} %get-tuple-element.315, s32[]{:T(128)} %get-tuple-element.311, f32[8,8,64,128]{3,2,1,0:T(8,128)} %get-tuple-element.326, f32[8,64,128]{2,1,0:T(8,128)S(1)} %get-tuple-element.313, pred[]{:T(512)S(6)} %compare.6, ...), kind=kLoop, calls=%fused_computation.clone.1 | loop fusion | flops 196608 | bytes 1049601 | tf_op jit(solution)/shard_map/while/body/jit(dynamic_update_index_in_dim)/dynamic_update_slice | solution.py:74
  40.2 1.8 %bitcast_dynamic-update-slice_fusion.2 = (f32[8,8,64,128]{3,2,1,0:T(8,128)}, f32[8,64,128]{2,1,0:T(8,128)S(1)}) fusion(f32[8,8,64,128]{3,2,1,0:T(8,128)} %get-tuple-element.315, s32[]{:T(128)} %get-tuple-element.311, f32[8,8,64,128]{3,2,1,0:T(8,128)} %get-tuple-element.326, f32[8,64,128]{2,1,0:T(8,128)S(1)} %get-tuple-element.313, pred[]{:T(512)S(6)} %compare.6, ...), kind=kLoop, calls=%fused_computation.clone.1 | loop fusion | flops 196608 | bytes 1049601 | tf_op jit(solution)/shard_map/while/body/jit(dynamic_update_index_in_dim)/dynamic_update_slice | solution.py:74
  42.0 1.8 %bitcast_dynamic-update-slice_fusion.2 = (f32[8,8,64,128]{3,2,1,0:T(8,128)}, f32[8,64,128]{2,1,0:T(8,128)S(1)}) fusion(f32[8,8,64,128]{3,2,1,0:T(8,128)} %get-tuple-element.315, s32[]{:T(128)} %get-tuple-element.311, f32[8,8,64,128]{3,2,1,0:T(8,128)} %get-tuple-element.326, f32[8,64,128]{2,1,0:T(8,128)S(1)} %get-tuple-element.313, pred[]{:T(512)S(6)} %compare.6, ...), kind=kLoop, calls=%fused_computation.clone.1 | loop fusion | flops 196608 | bytes 1049601 | tf_op jit(solution)/shard_map/while/body/jit(dynamic_update_index_in_dim)/dynamic_update_slice | solution.py:74
  43.9 1.8 %bitcast_dynamic-update-slice_fusion.2 = (f32[8,8,64,128]{3,2,1,0:T(8,128)}, f32[8,64,128]{2,1,0:T(8,128)S(1)}) fusion(f32[8,8,64,128]{3,2,1,0:T(8,128)} %get-tuple-element.315, s32[]{:T(128)} %get-tuple-element.311, f32[8,8,64,128]{3,2,1,0:T(8,128)} %get-tuple-element.326, f32[8,64,128]{2,1,0:T(8,128)S(1)} %get-tuple-element.313, pred[]{:T(512)S(6)} %compare.6, ...), kind=kLoop, calls=%fused_computation.clone.1 | loop fusion | flops 196608 | bytes 1049601 | tf_op jit(solution)/shard_map/while/body/jit(dynamic_update_index_in_dim)/dynamic_update_slice | solution.py:74
  45.7 1.8 %bitcast_dynamic-update-slice_fusion.2 = (f32[8,8,64,128]{3,2,1,0:T(8,128)}, f32[8,64,128]{2,1,0:T(8,128)S(1)}) fusion(f32[8,8,64,128]{3,2,1,0:T(8,128)} %get-tuple-element.315, s32[]{:T(128)} %get-tuple-element.311, f32[8,8,64,128]{3,2,1,0:T(8,128)} %get-tuple-element.326, f32[8,64,128]{2,1,0:T(8,128)S(1)} %get-tuple-element.313, pred[]{:T(512)S(6)} %compare.6, ...), kind=kLoop, calls=%fused_computation.clone.1 | loop fusion | flops 196608 | bytes 1049601 | tf_op jit(solution)/shard_map/while/body/jit(dynamic_update_index_in_dim)/dynamic_update_slice | solution.py:74
  47.5 1.7 %slice.170 = f32[1,8,64,128]{3,2,1,0:T(8,128)} slice(f32[8,8,64,128]{3,2,1,0:T(8,128)} %get-tuple-element.137), slice={[7:8], [0:8], [0:64], [0:128]} | slice | bytes 524288 | tf_op jit(solution)/shard_map/slice | solution.py:75
  49.2 9.1 %all-gather = f32[4,1,128]{2,1,0:T(1,128)S(1)} all-gather(f32[1,1,128]{2,1,0:T(1,128)S(1)} %slice_bitcast_fusion), channel_id=1, replica_groups=mesh['gx'=2,'gy'=4,'ta'=4] {'ta'}, dimensions={0}, use_global_device_ids=true | all-gather | bytes 2560 | tf_op jit(solution)/shard_map/all_gather | solution.py:26
  58.3 18.1 %all-gather.3.cloned.1.call-done = f32[4,8,64,128]{3,2,1,0:T(8,128)} async-done(((f32[1,8,64,128]{3,2,1,0:T(8,128)}), f32[4,8,64,128]{3,2,1,0:T(8,128)}) %all-gather.3.cloned.1.call-update) | async-done | bytes 1048592 | tf_op jit(solution)/shard_map/all_gather | solution.py:26
  76.4 3.5 %while.32 = (s32[]{:T(128)}, f32[8,64,128]{2,1,0:T(8,128)S(1)}, s32[]{:T(128)}, f32[4,128]{1,0:T(4,128)S(1)}, f32[4,8,64,128]{3,2,1,0:T(8,128)}, /*index=5*/s32[]{:T(128)}, s32[]{:T(128)}) while((s32[]{:T(128)}, f32[8,64,128]{2,1,0:T(8,128)S(1)}, s32[]{:T(128)}, f32[4,128]{1,0:T(4,128)S(1)}, f32[4,8,64,128]{3,2,1,0:T(8,128)}, ...), condition=%wide.region_3.4_spmd.clone, body=%wide.region_2.3_spmd.clone.sunk | while | flops 262148 | bytes 788073 | solution.py:35
  76.4 1.1 %fusion.115 = f32[8,64,128]{2,1,0:T(8,128)S(1)} fusion(f32[4,8,64,128]{3,2,1,0:T(8,128)} %get-tuple-element.347, s32[]{:T(128)} %get-tuple-element.336, f32[8,64,128]{2,1,0:T(8,128)S(1)} %get-tuple-element.337, f32[128]{0:T(128)S(1)} %dynamic-slice_bitcast_fusion.2, pred[]{:T(512)S(6)} %compare.7, pred[]{:T(512)S(6)} %lt.27), kind=kLoop, calls=%fused_computation.8.clone.1 | loop fusion | flops 262144 | bytes 786950 | tf_op jit(solution)/shard_map/while/body/eval_jaxpr/jit(_where)/select_n | solution.py:33
  77.6 1.2 %fusion.115 = f32[8,64,128]{2,1,0:T(8,128)S(1)} fusion(f32[4,8,64,128]{3,2,1,0:T(8,128)} %get-tuple-element.347, s32[]{:T(128)} %get-tuple-element.336, f32[8,64,128]{2,1,0:T(8,128)S(1)} %get-tuple-element.337, f32[128]{0:T(128)S(1)} %dynamic-slice_bitcast_fusion.2, pred[]{:T(512)S(6)} %compare.7, pred[]{:T(512)S(6)} %lt.27), kind=kLoop, calls=%fused_computation.8.clone.1 | loop fusion | flops 262144 | bytes 786950 | tf_op jit(solution)/shard_map/while/body/eval_jaxpr/jit(_where)/select_n | solution.py:33
  78.8 1.2 %fusion.115 = f32[8,64,128]{2,1,0:T(8,128)S(1)} fusion(f32[4,8,64,128]{3,2,1,0:T(8,128)} %get-tuple-element.347, s32[]{:T(128)} %get-tuple-element.336, f32[8,64,128]{2,1,0:T(8,128)S(1)} %get-tuple-element.337, f32[128]{0:T(128)S(1)} %dynamic-slice_bitcast_fusion.2, pred[]{:T(512)S(6)} %compare.7, pred[]{:T(512)S(6)} %lt.27), kind=kLoop, calls=%fused_computation.8.clone.1 | loop fusion | flops 262144 | bytes 786950 | tf_op jit(solution)/shard_map/while/body/eval_jaxpr/jit(_where)/select_n | solution.py:33
  79.9 1.9 %add_convert_fusion = bf16[8,8,64,128]{3,2,1,0:T(8,128)(2,1)S(1)} fusion(f32[8,8,64,128]{3,2,1,0:T(8,128)} %get-tuple-element.137, f32[8,64,128]{2,1,0:T(8,128)S(1)} %get-tuple-element.139, f32[8,128]{1,0:T(8,128)S(1)} %get-tuple-element.138), kind=kLoop, calls=%fused_computation.20 | loop fusion | flops 1572864 | bytes 3411968 | tf_op jit(solution)/shard_map/convert_element_type | solution.py:77
  81.9 3.1 %collective-permute-start.4 = (bf16[8,1,64,128]{3,2,1,0:T(8,128)(2,1)S(1)}, bf16[8,1,64,128]{3,2,1,0:T(8,128)(2,1)S(1)}, u32[]{:S(2)}, u32[]{:S(2)}) collective-permute-start(bf16[8,1,64,128]{3,2,1,0:T(8,128)(2,1)S(1)} %get-tuple-element.216), channel_id=1, source_target_pairs={{0,16},{1,17},{2,18},{3,19},{4,20},{5,21},{6,22},{7,23},{8,24},{9,... | collective-permute-start | bytes 393224 | tf_op jit(solution)/shard_map/ppermute | solution.py:15
  85.0 1.3 %collective-permute-start.5 = (bf16[8,1,64,128]{3,2,1,0:T(8,128)(2,1)S(1)}, bf16[8,1,64,128]{3,2,1,0:T(8,128)(2,1)S(1)}, u32[]{:S(2)}, u32[]{:S(2)}) collective-permute-start(bf16[8,1,64,128]{3,2,1,0:T(8,128)(2,1)S(1)} %get-tuple-element.217), channel_id=1, source_target_pairs={{16,0},{17,1},{18,2},{19,3},{20,4},{21,5},{22,6},{23,7},{24,8},{25... | collective-permute-start | bytes 393224 | tf_op jit(solution)/shard_map/ppermute | solution.py:17
  86.3 0.4 fusion.62
  86.9 3.8 %collective-permute-done.5 = bf16[8,1,64,128]{3,2,1,0:T(8,128)(2,1)S(1)} collective-permute-done((bf16[8,1,64,128]{3,2,1,0:T(8,128)(2,1)S(1)}, bf16[8,1,64,128]{3,2,1,0:T(8,128)(2,1)S(1)}, u32[]{:S(2)}, u32[]{:S(2)}) %collective-permute-start.5) | collective-permute-done | bytes 131104 | tf_op jit(solution)/shard_map/ppermute | solution.py:17
  90.8 5.2 %collective-permute-start.6 = (bf16[8,10,1,128]{3,2,1,0:T(2,128)(2,1)S(1)}, bf16[8,10,1,128]{3,2,1,0:T(2,128)(2,1)S(1)}, u32[]{:S(2)}, u32[]{:S(2)}) collective-permute-start(bf16[8,10,1,128]{3,2,1,0:T(2,128)(2,1)S(1)} %get-tuple-element.213), channel_id=1, source_target_pairs={{0,4},{4,8},{8,12},{1,5},{5,9},{9,13},{2,6},{6,10},{10,14},{3,7},{... | collective-permute-start | bytes 61448 | tf_op jit(solution)/shard_map/ppermute | solution.py:15
  96.0 1.9 %collective-permute-start.7 = (bf16[8,10,1,128]{3,2,1,0:T(2,128)(2,1)S(1)}, bf16[8,10,1,128]{3,2,1,0:T(2,128)(2,1)S(1)}, u32[]{:S(2)}, u32[]{:S(2)}) collective-permute-start(bf16[8,10,1,128]{3,2,1,0:T(2,128)(2,1)S(1)} %get-tuple-element.212), channel_id=1, source_target_pairs={{4,0},{8,4},{12,8},{5,1},{9,5},{13,9},{6,2},{10,6},{14,10},{7,3},{... | collective-permute-start | bytes 61448 | tf_op jit(solution)/shard_map/ppermute | solution.py:17
  98.4 0.4 fusion.24
  98.8 2.6 %collective-permute-done.7 = bf16[8,10,1,128]{3,2,1,0:T(2,128)(2,1)S(1)} collective-permute-done((bf16[8,10,1,128]{3,2,1,0:T(2,128)(2,1)S(1)}, bf16[8,10,1,128]{3,2,1,0:T(2,128)(2,1)S(1)}, u32[]{:S(2)}, u32[]{:S(2)}) %collective-permute-start.7) | collective-permute-done | bytes 20512 | tf_op jit(solution)/shard_map/ppermute | solution.py:17
  101.4 0.8 pad_maximum_fusion
  102.2 0.4 fusion.44
  102.6 0.4 fusion.48
  103.1 0.4 fusion.46
  103.5 0.4 fusion.50
  103.9 0.4 fusion.52
  104.3 2.7 %fusion.11 = bf16[8,8,64,128]{3,2,1,0:T(8,128)(2,1)} fusion(f32[8,8,64,128]{3,2,1,0:T(8,128)S(1)} %fusion.24, f32[8,8,64,128]{3,2,1,0:T(8,128)S(1)} %fusion.44, f32[8,8,64,128]{3,2,1,0:T(8,128)S(1)} %fusion.46, f32[8,8,64,128]{3,2,1,0:T(8,128)S(1)} %fusion.62, f32[8,8,64,128]{3,2,1,0:T(8,128)S(1)} %fusion.48, f32[8,8,64,128]{3,2,1,0:T(8,128)S(1)} %fusion.50, ...), kind=kOutput, calls=%fused_computation.19 | convolution fusion | flops 144179200 | bytes 19955712 | tf_op jit(solution)/shard_map/fhwc,cp->fhwp/dot_general | solution.py:42
  (47 shorter events, 1.3 us)
Async XLA Ops:
  6.5 8.8 %copy-start = (bf16[8,8,64,128]{3,2,1,0:T(8,128)(2,1)S(1)}, bf16[8,8,64,128]{3,2,1,0:T(8,128)(2,1)}, u32[]{:S(2)}) copy-start(bf16[8,8,64,128]{3,2,1,0:T(8,128)(2,1)} %param.8) | copy-start | bytes 3145732
  6.5 8.7 %copy-start.3 = (f32[8,128]{1,0:T(8,128)S(1)}, f32[8,128]{1,0:T(8,128)}, u32[]{:S(2)}) copy-start(f32[8,128]{1,0:T(8,128)} %param.11) | copy-start | bytes 12292
  6.5 69.8 %all-gather.3.cloned.1.call-start = ((), (), s32[]{:S(2)}) async-start(), calls=%async_computation | async-start | bytes 1310720 | tf_op jit(solution)/shard_map/all_gather | solution.py:26
  8.3 7.0 %collective-permute-start = (bf16[8,1,64,128]{3,2,1,0:T(8,128)(2,1)}, bf16[8,1,64,128]{3,2,1,0:T(8,128)(2,1)S(1)}, u32[]{:S(2)}, u32[]{:S(2)}) collective-permute-start(bf16[8,1,64,128]{3,2,1,0:T(8,128)(2,1)} %get-tuple-element.218), channel_id=1, source_target_pairs={{0,16},{1,17},{2,18},{3,19},{4,20},{5,21},{6,22},{7,23},{8,24},{9,... | collective-permute-start | bytes 393224 | tf_op jit(solution)/shard_map/ppermute | solution.py:15
  12.3 6.0 %collective-permute-start.1 = (bf16[8,1,64,128]{3,2,1,0:T(8,128)(2,1)}, bf16[8,1,64,128]{3,2,1,0:T(8,128)(2,1)}, u32[]{:S(2)}, u32[]{:S(2)}) collective-permute-start(bf16[8,1,64,128]{3,2,1,0:T(8,128)(2,1)} %get-tuple-element.219), channel_id=1, source_target_pairs={{16,0},{17,1},{18,2},{19,3},{20,4},{21,5},{22,6},{23,7},{24,8},{25... | collective-permute-start | bytes 393224 | tf_op jit(solution)/shard_map/ppermute | solution.py:17
  15.3 11.1 %copy-start.1 = (bf16[3,3,128,128]{3,2,1,0:T(8,128)(2,1)S(1)}, bf16[3,3,128,128]{3,2,1,0:T(8,128)(2,1)}, u32[]{:S(2)}) copy-start(bf16[3,3,128,128]{3,2,1,0:T(8,128)(2,1)} %param.9) | copy-start | bytes 884740
  19.3 8.8 %collective-permute-start.3 = (bf16[8,10,1,128]{3,2,1,0:T(2,128)(2,1)S(1)}, bf16[8,10,1,128]{3,2,1,0:T(2,128)(2,1)S(1)}, u32[]{:S(2)}, u32[]{:S(2)}) collective-permute-start(bf16[8,10,1,128]{3,2,1,0:T(2,128)(2,1)S(1)} %get-tuple-element.214), channel_id=1, source_target_pairs={{4,0},{8,4},{12,8},{5,1},{9,5},{13,9},{6,2},{10,6},{14,10},{7,3},{... | collective-permute-start | bytes 61448 | tf_op jit(solution)/shard_map/ppermute | solution.py:17
  23.3 5.7 %collective-permute-start.2 = (bf16[8,10,1,128]{3,2,1,0:T(2,128)(2,1)S(1)}, bf16[8,10,1,128]{3,2,1,0:T(2,128)(2,1)S(1)}, u32[]{:S(2)}, u32[]{:S(2)}) collective-permute-start(bf16[8,10,1,128]{3,2,1,0:T(2,128)(2,1)S(1)} %get-tuple-element.215), channel_id=1, source_target_pairs={{0,4},{4,8},{8,12},{1,5},{5,9},{9,13},{2,6},{6,10},{10,14},{3,7},{... | collective-permute-start | bytes 61448 | tf_op jit(solution)/shard_map/ppermute | solution.py:15
  79.9 6.4 %copy-start.2 = (bf16[3,3,128,128]{3,2,1,0:T(8,128)(2,1)S(1)}, bf16[3,3,128,128]{3,2,1,0:T(8,128)(2,1)}, u32[]{:S(2)}) copy-start(bf16[3,3,128,128]{3,2,1,0:T(8,128)(2,1)} %param.10) | copy-start | bytes 884740
  81.9 5.0 %collective-permute-start.4 = (bf16[8,1,64,128]{3,2,1,0:T(8,128)(2,1)S(1)}, bf16[8,1,64,128]{3,2,1,0:T(8,128)(2,1)S(1)}, u32[]{:S(2)}, u32[]{:S(2)}) collective-permute-start(bf16[8,1,64,128]{3,2,1,0:T(8,128)(2,1)S(1)} %get-tuple-element.216), channel_id=1, source_target_pairs={{0,16},{1,17},{2,18},{3,19},{4,20},{5,21},{6,22},{7,23},{8,24},{9,... | collective-permute-start | bytes 393224 | tf_op jit(solution)/shard_map/ppermute | solution.py:15
  85.0 5.7 %collective-permute-start.5 = (bf16[8,1,64,128]{3,2,1,0:T(8,128)(2,1)S(1)}, bf16[8,1,64,128]{3,2,1,0:T(8,128)(2,1)S(1)}, u32[]{:S(2)}, u32[]{:S(2)}) collective-permute-start(bf16[8,1,64,128]{3,2,1,0:T(8,128)(2,1)S(1)} %get-tuple-element.217), channel_id=1, source_target_pairs={{16,0},{17,1},{18,2},{19,3},{20,4},{21,5},{22,6},{23,7},{24,8},{25... | collective-permute-start | bytes 393224 | tf_op jit(solution)/shard_map/ppermute | solution.py:17
  90.8 8.0 %collective-permute-start.6 = (bf16[8,10,1,128]{3,2,1,0:T(2,128)(2,1)S(1)}, bf16[8,10,1,128]{3,2,1,0:T(2,128)(2,1)S(1)}, u32[]{:S(2)}, u32[]{:S(2)}) collective-permute-start(bf16[8,10,1,128]{3,2,1,0:T(2,128)(2,1)S(1)} %get-tuple-element.213), channel_id=1, source_target_pairs={{0,4},{4,8},{8,12},{1,5},{5,9},{9,13},{2,6},{6,10},{10,14},{3,7},{... | collective-permute-start | bytes 61448 | tf_op jit(solution)/shard_map/ppermute | solution.py:15
  96.0 5.3 %collective-permute-start.7 = (bf16[8,10,1,128]{3,2,1,0:T(2,128)(2,1)S(1)}, bf16[8,10,1,128]{3,2,1,0:T(2,128)(2,1)S(1)}, u32[]{:S(2)}, u32[]{:S(2)}) collective-permute-start(bf16[8,10,1,128]{3,2,1,0:T(2,128)(2,1)S(1)} %get-tuple-element.212), channel_id=1, source_target_pairs={{4,0},{8,4},{12,8},{5,1},{9,5},{13,9},{6,2},{10,6},{14,10},{7,3},{... | collective-permute-start | bytes 61448 | tf_op jit(solution)/shard_map/ppermute | solution.py:17
Sparse Core Ops, SparseCore 0:
  49.3 27.0 all-gather.2
where the time goes:
time: 115 us; the launch traced here: 114 us
  waiting for transfers between devices  27.5 us (24%)
  starting transfers between devices  23.8 us (21%)
  other arithmetic  20.6 us (18%)
  matrix products  14.2 us (12%)
  between operations  13.7 us (12%)
  blocking collectives  9.09 us (8%)
  local copies, waits for them, and re-layouts  4.86 us (4%)
    all_gather x1, waiting for transfers between devices, entering(): pieces = jax.tree.map(lambda part: lax.all_gather(part, axis), value)  18.1 us
    ppermute x4, starting transfers between devices, padded_2(): lax.ppermute(tail, axis, [(i, (i + 1) % count) for i in range(ends)])  15.3 us
    dot_general x18, matrix products, convolve(): jnp.einsum('fhwc,cp->fhwp', padded[:, row_off:row_off + height, col_off:c...  14.2 us
    dynamic_update_slice x8, other arithmetic, on_device(): lax.scan(advance, start_carry, (decays, scaled))[1]  14.2 us
    ppermute x4, waiting for transfers between devices, padded_2(): lax.ppermute(head, axis, [((i + 1) % count, i) for i in range(ends)])  9.18 us
    all_gather x1, blocking collectives, entering(): pieces = jax.tree.map(lambda part: lax.all_gather(part, axis), value)  9.09 us
    ppermute x4, starting transfers between devices, padded_2(): lax.ppermute(head, axis, [((i + 1) % count, i) for i in range(ends)])  8.52 us
    select_n x3, other arithmetic, step(): jnp.where(position < mine, new, old)  3.45 us
  transfers between devices with their start and end apart: 9, of which 5 were waited for; matrix products, arithmetic and copies ran while one was open for 5% of the time, Pallas kernels for 0%

commit v1 on v0

v1 whole, which is shorter than its diff:
```python
import functools

import jax
import jax.numpy as jnp
from jax import lax
from jax.experimental import pallas as pl
from jax.experimental.pallas import tpu as pltpu
from jax.sharding import PartitionSpec as P

F32, BF16 = jnp.float32, jnp.bfloat16
VMEM = pl.BlockSpec(memory_space=pltpu.VMEM)
SMEM = pl.BlockSpec(memory_space=pltpu.SMEM)


def pair_weights(w_ref, wt, flip):
    chan_in, chan_out = w_ref.shape[2:]
    for k in range(4):
        for b in range(3):
            for rr in range(2):
                at = (k * 3 + b) * chan_in
                a = k - rr
                if 0 <= a <= 2:
                    block = w_ref[jnp.where(flip == 1, 2 - a, a), b]
                else:
                    block = jnp.zeros((chan_in, chan_out), BF16)
                wt[at : at + chan_in, rr * chan_out : (rr + 1) * chan_out] = block


def clear_margins(rowbuf):
    across = rowbuf.shape[1] - 16
    zeros = jnp.zeros((rowbuf.shape[0], 8, rowbuf.shape[2]), F32)
    rowbuf[:, 0:8, :] = zeros
    rowbuf[:, 8 + across : 16 + across, :] = zeros


def three_taps(rowbuf, slot, x3, row, f, middle):
    across = rowbuf.shape[1] - 16
    chan = rowbuf.shape[2]
    at = pl.ds(f * across, across)
    x3[row, at, 0:chan] = rowbuf[slot, 7 : 7 + across, :].astype(BF16)
    x3[row, at, chan : 2 * chan] = middle
    x3[row, at, 2 * chan : 3 * chan] = rowbuf[slot, 9 : 9 + across, :].astype(BF16)


def pair_dot(x3, slots, wt):
    width = x3.shape[2]
    first = next(k for k in range(4) if slots[k] is not None)
    rows = jnp.concatenate([x3[s] for s in slots[first:]], axis=1)
    return jnp.dot(rows, wt[first * width : 4 * width, :], preferred_element_type=F32)


def scan_rows(y, decays, scales, across, keep):
    frames = decays.shape[0]
    chan = decays.shape[1]
    finals = []
    for rr in range(2):
        s = None
        for f in range(frames):
            u = scales[f : f + 1] * y[f * across : (f + 1) * across, rr * chan : (rr + 1) * chan]
            s = u if s is None else decays[f : f + 1] * s + u
            keep(rr, f, s)
        finals.append(s)
    return finals


def load_decays(dec_ref):
    decays = dec_ref[...]
    return decays, jnp.sqrt(1.0 - decays * decays)


def inner_kernel(two, where_ref, frames_ref, w_ref, dec_ref, p_ref, f_ref, wt, rowbuf, x3):
    frames, height, across, chan = frames_ref.shape
    flip = where_ref[0]
    pair_weights(w_ref, wt, flip)
    clear_margins(rowbuf)
    decays, scales = load_decays(dec_ref)
    for r in range(height):
        natural = jnp.where(flip == 1, height - 1 - r, r)
        for f in range(frames):
            slot = (r * frames + f) % rowbuf.shape[0]
            x = frames_ref[f, natural]
            rowbuf[slot, 8 : 8 + across, :] = x.astype(F32)
            three_taps(rowbuf, slot, x3, r, f, x)
    first, first_row = (0, 1) if two else (1, 0)
    for p in range(first, height // 2):
        slots = [r if r >= 0 else None for r in range(2 * p - 2, 2 * p + 2)]
        y = pair_dot(x3, slots, wt)
        base = 2 * (p - first)

        def keep(rr, f, s, base=base):
            if base + rr >= first_row:
                p_ref[base + rr - first_row, f] = s

        for rr, s in enumerate(scan_rows(y, decays, scales, across, keep)):
            at = base + rr - first_row
            if at >= 0:
                f_ref[at * across : (at + 1) * across, :] = s.astype(BF16)
    total = decays[0:1]
    for f in range(1, frames):
        total = total * decays[f : f + 1]
    high = total.astype(BF16)
    rest = total - high.astype(F32)
    middle = rest.astype(BF16)
    low = rest - middle.astype(F32)
    row = lax.broadcasted_iota(jnp.int32, (16, chan), 0)
    parts = jnp.where(row == 0, high.astype(F32), jnp.where(row == 1, middle.astype(F32), jnp.where(row == 2, low, 0.0)))
    end = f_ref.shape[0]
    f_ref[end - 16 : end, :] = parts.astype(BF16)


def edge_kernel(
    two, where_ref, frames_ref, halo_ref, e_ref, l_ref, r_ref, w_ref, dec_ref,
    p_ref, pc_ref, f_ref, wt, rowbuf, x3, xc, yc,
):
    frames, height, across, chan = frames_ref.shape
    flip = where_ref[0]
    pair_weights(w_ref, wt, flip)
    clear_margins(rowbuf)
    decays, scales = load_decays(dec_ref)
    pairs = [height // 2] if two else [0, height // 2]
    for i, p in enumerate(pairs):
        for k in range(4):
            r = 2 * p - 2 + k
            for f in range(frames):
                slot = (k * frames + f) % rowbuf.shape[0]
                if 0 <= r < height:
                    x = frames_ref[f, jnp.where(flip == 1, height - 1 - r, r)]
                elif two:
                    x = halo_ref[f, jnp.where(flip == 1, 1 - (r - height), r - height)]
                else:
                    x = halo_ref[f, r + 2 if r < 0 else r - height + 2]
                rowbuf[slot, 8 : 8 + across, :] = x.astype(F32)
                three_taps(rowbuf, slot, x3, i * 4 + k, f, x)
        y = pair_dot(x3, [i * 4 + k for k in range(4)], wt)
        inside = 1.0
        if not two:
            inside = where_ref[3 if p == 0 else 4].astype(F32)

        def keep(rr, f, s, i=i, p=p, inside=inside):
            border = (rr == 0) if p == 0 else (rr == 1)
            p_ref[2 * i + rr, f] = s * inside if border and not two else s

        for rr, s in enumerate(scan_rows(y, decays, scales, across, keep)):
            border = (rr == 0) if p == 0 else (rr == 1)
            s = s * inside if border and not two else s
            f_ref[(2 * i + rr) * across : (2 * i + rr + 1) * across, :] = s.astype(BF16)

    n_pairs = height // 2 + 1
    for p in range(n_pairs):
        for k in range(4):
            r = 2 * p - 2 + k
            if two:
                at = None if r < 0 else jnp.where(flip == 1, height + 1 - r, r)
            else:
                at = r + 2
            to = slice(p * 4 * frames, (p + 1) * 4 * frames)
            lanes = k * 3 * chan
            if at is None:
                xc[to, lanes : lanes + 3 * chan] = jnp.zeros((4 * frames, 3 * chan), BF16)
                continue
            own = e_ref[at].astype(F32)
            left = l_ref[at].astype(F32)
            right = r_ref[at].astype(F32)
            cols = [left[:frames], left[frames:]] + [own[c * frames : (c + 1) * frames] for c in range(4)]
            cols += [right[:frames], right[frames:]]
            for b in range(3):
                piece = jnp.concatenate([cols[c + b] for c in (0, 1, 4, 5)], axis=0)
                xc[to, lanes + b * chan : lanes + (b + 1) * chan] = piece.astype(BF16)
    edge = jnp.dot(xc[...], wt[...], preferred_element_type=F32)
    for h in range(2):
        yc[h] = edge[:, h * chan : (h + 1) * chan]
    count = n_pairs * 4
    place = lax.broadcasted_iota(jnp.int32, (count, 2 * chan), 0)
    lane = lax.broadcasted_iota(jnp.int32, (count, 2 * chan), 1)
    mask = jnp.where(place % 4 == 0, where_ref[1].astype(F32), jnp.where(place % 4 == 3, where_ref[2].astype(F32), 1.0))
    above = (place < 4) & (lane < chan)
    if two:
        mask = jnp.where(above, 0.0, mask)
    else:
        below = (place >= count - 4) & (lane >= chan)
        mask = jnp.where(above, mask * where_ref[3].astype(F32), mask)
        mask = jnp.where(below, mask * where_ref[4].astype(F32), mask)
    s = None
    for f in range(frames):
        both = [jnp.concatenate([v[f : f + 1]] * 2, axis=1) for v in (decays, scales)]
        halves = [yc[h, pl.ds(f, count, stride=frames), :] for h in range(2)]
        u = both[1] * jnp.concatenate(halves, axis=1) * mask
        s = u if s is None else both[0] * s + u
        for h in range(2):
            pc_ref[h, pl.ds(f, count, stride=frames), :] = s[:, h * chan : (h + 1) * chan]
    base = len(pairs) * 2 * across
    pad = jnp.zeros((32 - count, chan), F32)
    for h in range(2):
        half = jnp.concatenate([s[:, h * chan : (h + 1) * chan], pad], axis=0)
        f_ref[base + 32 * h : base + 32 * (h + 1), :] = half.astype(BF16)


def outer_kernel(
    two, where_ref, frames_ref, pa_ref, pb_ref, pc_ref, ra_ref, za_ref, rb_ref, zb_ref, mix_ref, w_ref, dec_ref,
    out_ref, wt, rowbuf, x3, sc, ia, ib,
):
    frames, height, across, chan = frames_ref.shape
    flip = where_ref[0]
    pair_weights(w_ref, wt, flip)
    decays = dec_ref[...]
    alpha, beta = mix_ref[0:1], mix_ref[1:2]
    rows_a = pa_ref.shape[0]
    ia[...] = alpha * ra_ref[0 : rows_a * across].astype(F32) + beta * za_ref[0 : rows_a * across].astype(F32)
    ib[...] = alpha * rb_ref[...].astype(F32) + beta * zb_ref[...].astype(F32)
    running = [decays[0:1]]
    for f in range(1, frames):
        running.append(running[-1] * decays[f : f + 1])
    count = (height // 2 + 1) * 4
    base = pb_ref.shape[0] * across
    for f in range(frames):
        for h in range(2):
            part = pc_ref[h, pl.ds(f, count, stride=frames), :]
            sc[f, h, 0:count, :] = part + running[f] * ib[base + 32 * h : base + 32 * h + count, :]
    for n in range(height + 2):
        if two and n == 0:
            continue
        if two:
            src, at = ((pa_ref, ia), n - 1) if n < height else ((pb_ref, ib), n - height)
        elif 2 <= n < height:
            src, at = (pa_ref, ia), n - 2
        else:
            src, at = (pb_ref, ib), n if n < 2 else n - height + 2
        incoming = src[1][at * across : (at + 1) * across, :]
        for f in range(frames):
            slot = (n * frames + f) % rowbuf.shape[0]
            rowbuf[slot, 8 : 8 + across, :] = src[0][at, f] + running[f] * incoming
            corner = (n // 2) * 4
            h = n % 2
            rowbuf[slot, 7:8, :] = sc[f, h, corner : corner + 1, :]
            rowbuf[slot, 8:9, :] = sc[f, h, corner + 1 : corner + 2, :]
            rowbuf[slot, 7 + across : 8 + across, :] = sc[f, h, corner + 2 : corner + 3, :]
            rowbuf[slot, 8 + across : 9 + across, :] = sc[f, h, corner + 3 : corner + 4, :]
            three_taps(rowbuf, slot, x3, n, f, rowbuf[slot, 8 : 8 + across, :].astype(BF16))
    for p in range(height // 2):
        slots = [n if n > 0 or not two else None for n in range(2 * p, 2 * p + 4)]
        y = pair_dot(x3, slots, wt)
        for rr in range(2):
            r = 2 * p + rr
            natural = jnp.where(flip == 1, height - 1 - r, r)
            for f in range(frames):
                mixed = y[f * across : (f + 1) * across, rr * chan : (rr + 1) * chan]
                out_ref[f, natural] = (frames_ref[f, natural].astype(F32) + jax.nn.gelu(mixed)).astype(BF16)


def call(body, outs, scratch, flops, n_in):
    return pl.pallas_call(
        body,
        out_shape=outs,
        in_specs=[SMEM] + [VMEM] * (n_in - 1),
        out_specs=jax.tree.map(lambda _: VMEM, outs),
        scratch_shapes=scratch,
        compiler_params=pltpu.CompilerParams(vmem_limit_bytes=56 * 2**20),
        cost_estimate=pl.CostEstimate(flops=flops, bytes_accessed=4 * 2**20, transcendentals=0),
    )


def forward(ends):
    return [(i, i + 1) for i in range(ends - 1)]


def backward(ends):
    return [(i + 1, i) for i in range(ends - 1)]


def carry_general(locals_, total, ta):
    step = 1
    while step < ta:
        pairs = [(i, i + step) for i in range(ta - step)]
        moved = [lax.ppermute(v, "ta", pairs) for v in locals_]
        moved_total = lax.ppermute(total, "ta", pairs)
        has = lax.axis_index("ta") >= step
        locals_ = [(v.astype(F32) + total * m.astype(F32)).astype(BF16) for v, m in zip(locals_, moved)]
        total = jnp.where(has, total * moved_total, total)
        step *= 2
    return [lax.ppermute(v, "ta", forward(ta)) for v in locals_]


def on_device(gx, gy, ta, frames, in_weight, out_weight, decays):
    n_frames, height, across, chan = frames.shape
    two = gx == 2
    x, y, t = (lax.axis_index(a) for a in ("gx", "gy", "ta"))
    flip = x if two else jnp.zeros_like(x)
    where = jnp.stack([flip, (y > 0), (y < gy - 1), (x > 0), (x < gx - 1)]).astype(jnp.int32)

    cols = jnp.concatenate([frames[:, :, :2], frames[:, :, across - 2 :]], axis=2)
    cols = cols.transpose(1, 2, 0, 3).reshape(height, 4 * n_frames, chan)
    if two:
        swap = [(0, 1), (1, 0)]
        start = jnp.where(x == 1, 0, height - 2)
        halo = lax.ppermute(lax.dynamic_slice_in_dim(frames, start, 2, axis=1), "gx", swap)
        corner = lax.ppermute(lax.dynamic_slice_in_dim(cols, start, 2, axis=0), "gx", swap)
        cols = jnp.where(x == 1, jnp.concatenate([corner, cols]), jnp.concatenate([cols, corner]))
    else:
        above = lax.ppermute(frames[:, height - 2 :], "gx", forward(gx))
        below = lax.ppermute(frames[:, :2], "gx", backward(gx))
        halo = jnp.concatenate([above, below], axis=1)
        over = lax.ppermute(cols[height - 2 :], "gx", forward(gx))
        under = lax.ppermute(cols[:2], "gx", backward(gx))
        cols = jnp.concatenate([over, cols, under])

    rows_a = height - 1 if two else height - 2
    rows_b = 2 if two else 4
    wt = pltpu.VMEM((12 * chan, 2 * chan), BF16)
    rowbuf = pltpu.VMEM((16, across + 16, chan), F32)
    cells = n_frames * across
    flops = 2 * 9 * chan * chan * cells
    sds = jax.ShapeDtypeStruct
    pa, fa = call(
        functools.partial(inner_kernel, two),
        (sds((rows_a, n_frames, across, chan), F32), sds((rows_a * across + 16, chan), BF16)),
        [wt, rowbuf, pltpu.VMEM((height, cells, 3 * chan), BF16)],
        flops * height, 4,
    )(where, frames, in_weight, decays)

    left = lax.ppermute(cols[:, 2 * n_frames :], "gy", forward(gy))
    right = lax.ppermute(cols[:, : 2 * n_frames], "gy", backward(gy))
    n_cols = (height // 2 + 1) * 4
    pb, pc, fb = call(
        functools.partial(edge_kernel, two),
        (
            sds((rows_b, n_frames, across, chan), F32),
            sds((2, n_cols * n_frames, chan), F32),
            sds((rows_b * across + 64, chan), BF16),
        ),
        [
            wt, rowbuf, pltpu.VMEM((2 * rows_b, cells, 3 * chan), BF16),
            pltpu.VMEM((n_cols * n_frames, 12 * chan), BF16), pltpu.VMEM((2, n_cols * n_frames, chan), F32),
        ],
        flops * rows_b, 8,
    )(where, frames, halo, cols, left, right, in_weight, decays)

    total = jnp.prod(decays, axis=0)[None]
    if ta == 4:
        near, far = [(0, 1), (1, 0), (2, 3)], [(1, 2), (0, 3)]
        ra = lax.ppermute(fa, "ta", near)
        other = jnp.sum(ra[rows_a * across :].astype(F32), axis=0, keepdims=True)

        def joined(mine, theirs):
            mine, theirs = mine.astype(F32), theirs.astype(F32)
            return jnp.where(t == 0, theirs + other * mine, mine + total * theirs).astype(BF16)

        za = lax.ppermute(joined(fa, ra), "ta", far)
        rb = lax.ppermute(fb, "ta", near)
        zb = lax.ppermute(joined(fb, rb), "ta", far)
        alpha = jnp.where((t == 1) | (t == 3), 1.0, 0.0) * jnp.ones_like(total)
        beta = jnp.where(t == 2, 1.0, jnp.where(t == 3, other, 0.0))
    else:
        ra, rb = carry_general([fa, fb], total, ta)
        za, zb = ra, rb
        alpha, beta = jnp.ones_like(total), jnp.zeros_like(total)
    mix = jnp.concatenate([alpha, beta])

    return call(
        functools.partial(outer_kernel, two),
        sds(frames.shape, BF16),
        [
            wt, rowbuf, pltpu.VMEM((height + 2, cells, 3 * chan), BF16),
            pltpu.VMEM((n_frames, 2, (n_cols + 7) // 8 * 8, chan), F32),
            pltpu.VMEM((rows_a * across, chan), F32), pltpu.VMEM((rows_b * across + 64, chan), F32),
        ],
        flops * height, 12,
    )(where, frames, pa, pb, pc, ra, za, rb, zb, mix, out_weight, decays)


def solution(mesh):
    sizes = [mesh.shape[a] for a in ("gx", "gy", "ta")]
    placed = (P("ta", "gx", "gy", None), P(), P(), P("ta", None))
    return jax.shard_map(
        functools.partial(on_device, *sizes), mesh=mesh, in_specs=placed,
        out_specs=P("ta", "gx", "gy", None), check_vma=False,
    )
```

time: 115 us -> 45.5 us (0.40)
  the two profiles are of different devices: /device:TPU:1 before, /device:TPU:28 now
where the time goes in v1:
time: 45.5 us; the launch traced here: 45.1 us
  Pallas kernels  13.9 us (31%)
  waiting for transfers between devices  13 us (29%)
  starting transfers between devices  11.8 us (26%)
  local copies, waits for them, and re-layouts  5.13 us (11%)
  other arithmetic  1.04 us (2%)
    pallas_call x1, Pallas kernels, on_device(): call(functools.partial(outer_kernel, two), sds(frames.shape, BF16), [wt,...  5.86 us
    ppermute x1, waiting for transfers between devices, on_device(): zb = lax.ppermute(joined(fb, rb), 'ta', far)  5.53 us
    pallas_call x1, Pallas kernels, on_device(): call(functools.partial(inner_kernel, two), (sds((rows_a, n_frames, across...  4.66 us
    ppermute x1, waiting for transfers between devices, on_device(): rb = lax.ppermute(fb, 'ta', near)  4.24 us
    pallas_call x1, Pallas kernels, on_device(): call(functools.partial(edge_kernel, two), (sds((rows_b, n_frames, across,...  3.38 us
    ppermute x1, starting transfers between devices, on_device(): left = lax.ppermute(cols[:, 2 * n_frames:], 'gy', forward(gy))  2.4 us
    unnamed x20, local copies, waits for them, and re-layouts  1.93 us
    ppermute x1, starting transfers between devices, on_device(): right = lax.ppermute(cols[:, :2 * n_frames], 'gy', backward(gy))  1.92 us
  transfers between devices with their start and end apart: 8, of which 5 were waited for; matrix products, arithmetic and copies ran while one was open for 7% of the time, Pallas kernels for 10%

profile of v1, /device:TPU:28, one launch (start us, length us, event | category | flops | bytes accessed | tf_op | source)
XLA Modules:
  0.0 45.1 jit_solution(11240642080551680747)
XLA Ops:
  0.0 1.0 %fusion.5 = (bf16[8,8,2,128]{3,2,1,0:T(2,128)(2,1)S(1)}, bf16[8,8,2,128]{3,2,1,0:T(2,128)(2,1)S(1)}) fusion(bf16[8,8,64,128]{3,2,1,0:T(8,128)(2,1)} %frames_ref.5), kind=kLoop, calls=%fused_computation.21 | loop fusion | bytes 131072 | tf_op jit(solution)/shard_map/slice | solution.py:290
  1.0 0.1 maximum_bitcast_fusion
  1.2 1.6 %collective-permute-start.1 = (bf16[2,32,128]{2,1,0:T(8,128)(2,1)S(1)}, bf16[2,32,128]{2,1,0:T(8,128)(2,1)S(1)}, u32[]{:S(2)}, u32[]{:S(2)}) collective-permute-start(bf16[2,32,128]{2,1,0:T(8,128)(2,1)S(1)} %constant_dynamic-slice_fusion), channel_id=1, source_target_pairs={{0,16},{16,0},{1,17},{17,1},{2,18},{18,2},{3,19},{19,3},{4,20},{20... | collective-permute-start | bytes 49160 | tf_op jit(solution)/shard_map/ppermute | solution.py:296
  2.7 1.0 %constant_dynamic-slice_fusion.1 = bf16[8,2,64,128]{3,2,1,0:T(8,128)(2,1)S(1)} fusion(bf16[8,8,64,128]{3,2,1,0:T(8,128)(2,1)} %frames_ref.5, s32[]{:T(128)S(6)} %select_n.70), kind=kLoop, calls=%fused_computation.20 | loop fusion | bytes 524292 | tf_op jit(solution)/shard_map/dynamic_slice | solution.py:295
  3.7 0.6 %collective-permute-start = (bf16[8,2,64,128]{3,2,1,0:T(8,128)(2,1)S(1)}, bf16[8,2,64,128]{3,2,1,0:T(8,128)(2,1)S(1)}, u32[]{:S(2)}, u32[]{:S(2)}) collective-permute-start(bf16[8,2,64,128]{3,2,1,0:T(8,128)(2,1)S(1)} %constant_dynamic-slice_fusion.1), channel_id=1, source_target_pairs={{0,16},{16,0},{1,17},{17,1},{2,18},{18,2},{3,19},{19,3},{4,20},{20... | collective-permute-start | bytes 786440 | tf_op jit(solution)/shard_map/ppermute | solution.py:295
  4.3 0.6 %stack.39.where_ref = s32[5]{0:T(128)} concatenate(s32[1]{0:T(128)} %bitcast, s32[1]{0:T(128)} %bitcast.1, s32[1]{0:T(128)} %bitcast.2, s32[1]{0:T(128)} %bitcast.3, s32[1]{0:T(128)} %bitcast.4), dimensions={0} | concatenate | bytes 40 | tf_op jit(solution)/shard_map/stack | solution.py:288
  4.9 0.0 copy-start.9
  4.9 4.7 %shard_map.46 = (f32[7,8,64,128]{3,2,1,0:T(8,128)}, bf16[464,128]{1,0:T(8,128)(2,1)}) custom-call(s32[5]{0:T(128)} %stack.39.where_ref, bf16[8,8,64,128]{3,2,1,0:T(8,128)(2,1)} %frames_ref.5, bf16[3,3,128,128]{3,2,1,0:T(8,128)(2,1)} %w_ref.4, f32[8,128]{1,0:T(8,128)} %dec_ref.5), custom_call_target="tpu_custom_call" | custom-call | flops 1207959552 | bytes 4194304 | tf_op jit(solution)/shard_map/pallas_call | solution.py:313
  9.6 0.0 copy-start.4
  9.6 1.4 %collective-permute-start.4 = (bf16[464,128]{1,0:T(8,128)(2,1)}, bf16[464,128]{1,0:T(8,128)(2,1)S(1)}, u32[]{:S(2)}, u32[]{:S(2)}) collective-permute-start(bf16[464,128]{1,0:T(8,128)(2,1)} %get-tuple-element.13), channel_id=1, source_target_pairs={{0,1},{1,0},{2,3},{4,5},{5,4},{6,7},{8,9},{9,8},{10,11},{12,13},{1... | collective-permute-start | bytes 356360 | tf_op jit(solution)/shard_map/ppermute | solution.py:340
  11.0 0.0 copy-done.9
  11.0 0.0 collective-permute-done.1
  11.1 0.0 copy-start
  11.1 1.9 %collective-permute-start.3 = (bf16[10,16,128]{2,1,0:T(8,128)(2,1)S(1)}, bf16[10,16,128]{2,1,0:T(8,128)(2,1)S(1)}, u32[]{:S(2)}, u32[]{:S(2)}) collective-permute-start(bf16[10,16,128]{2,1,0:T(8,128)(2,1)S(1)} %get-tuple-element.17), channel_id=1, source_target_pairs={{4,0},{8,4},{12,8},{5,1},{9,5},{13,9},{6,2},{10,6},{14,10},{7,3},{... | collective-permute-start | bytes 122888 | tf_op jit(solution)/shard_map/ppermute | solution.py:321
  13.0 2.4 %collective-permute-start.2 = (bf16[10,16,128]{2,1,0:T(8,128)(2,1)S(1)}, bf16[10,16,128]{2,1,0:T(8,128)(2,1)S(1)}, u32[]{:S(2)}, u32[]{:S(2)}) collective-permute-start(bf16[10,16,128]{2,1,0:T(8,128)(2,1)S(1)} %get-tuple-element.18), channel_id=1, source_target_pairs={{0,4},{4,8},{8,12},{1,5},{5,9},{9,13},{2,6},{6,10},{10,14},{3,7},{... | collective-permute-start | bytes 122888 | tf_op jit(solution)/shard_map/ppermute | solution.py:320
  15.4 1.2 %collective-permute-done.4.ra_ref = bf16[464,128]{1,0:T(8,128)(2,1)S(1)} collective-permute-done((bf16[464,128]{1,0:T(8,128)(2,1)}, bf16[464,128]{1,0:T(8,128)(2,1)S(1)}, u32[]{:S(2)}, u32[]{:S(2)}) %collective-permute-start.4) | collective-permute-done | bytes 118816 | tf_op jit(solution)/shard_map/ppermute | solution.py:340
  16.6 0.0 copy-start.1
  16.7 0.0 collective-permute-done.3.r_ref
  16.7 0.0 copy-start.7
  16.7 1.7 %collective-permute-done.2.l_ref = bf16[10,16,128]{2,1,0:T(8,128)(2,1)S(1)} collective-permute-done((bf16[10,16,128]{2,1,0:T(8,128)(2,1)S(1)}, bf16[10,16,128]{2,1,0:T(8,128)(2,1)S(1)}, u32[]{:S(2)}, u32[]{:S(2)}) %collective-permute-start.2) | collective-permute-done | bytes 40992 | tf_op jit(solution)/shard_map/ppermute | solution.py:320
  18.4 0.0 copy-start.8
  18.4 0.0 collective-permute-done.halo_ref
  18.4 0.0 copy-done
  18.4 0.0 copy-done.7
  18.4 0.6 %copy-done.8 = bf16[10,16,128]{2,1,0:T(8,128)(2,1)} copy-done((bf16[10,16,128]{2,1,0:T(8,128)(2,1)}, bf16[10,16,128]{2,1,0:T(8,128)(2,1)S(1)}, u32[]{:S(2)}) %copy-start.8) | copy-done | bytes 40984
  19.0 0.0 copy-start.2
  19.0 0.7 %copy-done.2 = bf16[8,2,64,128]{3,2,1,0:T(8,128)(2,1)} copy-done((bf16[8,2,64,128]{3,2,1,0:T(8,128)(2,1)}, bf16[8,2,64,128]{3,2,1,0:T(8,128)(2,1)S(1)}, u32[]{:S(2)}) %copy-start.2) | copy-done | bytes 262168
  19.7 3.4 %shard_map.47 = (f32[2,8,64,128]{3,2,1,0:T(8,128)}, f32[2,160,128]{2,1,0:T(8,128)}, bf16[192,128]{1,0:T(8,128)(2,1)}) custom-call(s32[5]{0:T(128)} %stack.39.where_ref, bf16[8,8,64,128]{3,2,1,0:T(8,128)(2,1)} %frames_ref.5, bf16[8,2,64,128]{3,2,1,0:T(8,128)(2,1)} %copy-done.2, bf16[10,32,128]{2,1,0:T(8,128)(2,1)} %copy-done, bf16[10,16,128]{2,1,0:T(8,128)(2,1)} %copy-done.8, ...), custom_call_target="tpu_custom_call" | custom-call | flops 301989888 | bytes 4194304 | tf_op jit(solution)/shard_map/pallas_call | solution.py:323
  23.0 1.3 %collective-permute-start.6 = (bf16[192,128]{1,0:T(8,128)(2,1)}, bf16[192,128]{1,0:T(8,128)(2,1)S(1)}, u32[]{:S(2)}, u32[]{:S(2)}) collective-permute-start(bf16[192,128]{1,0:T(8,128)(2,1)} %get-tuple-element.14), channel_id=1, source_target_pairs={{0,1},{1,0},{2,3},{4,5},{5,4},{6,7},{8,9},{9,8},{10,11},{12,13},{1... | collective-permute-start | bytes 147464 | tf_op jit(solution)/shard_map/ppermute | solution.py:348
  24.3 0.0 copy-done.4
  24.3 0.1 fusion.1
  24.4 1.3 %collective-permute-start.5 = (bf16[464,128]{1,0:T(8,128)(2,1)S(1)}, bf16[464,128]{1,0:T(8,128)(2,1)S(1)}, u32[]{:S(2)}, u32[]{:S(2)}) collective-permute-start(bf16[464,128]{1,0:T(8,128)(2,1)S(1)} %fusion.1), channel_id=1, source_target_pairs={{1,2},{0,3},{5,6},{4,7},{9,10},{8,11},{13,14},{12,15},{17,18},{16,... | collective-permute-start | bytes 356360 | tf_op jit(solution)/shard_map/ppermute | solution.py:347
  25.7 4.2 %collective-permute-done.6.rb_ref = bf16[192,128]{1,0:T(8,128)(2,1)S(1)} collective-permute-done((bf16[192,128]{1,0:T(8,128)(2,1)}, bf16[192,128]{1,0:T(8,128)(2,1)S(1)}, u32[]{:S(2)}, u32[]{:S(2)}) %collective-permute-start.6) | collective-permute-done | bytes 49184 | tf_op jit(solution)/shard_map/ppermute | solution.py:348
  30.0 0.0 copy-start.3
  30.0 0.8 %fusion.3 = bf16[192,128]{1,0:T(8,128)(2,1)S(1)} fusion(bf16[192,128]{1,0:T(8,128)(2,1)S(1)} %collective-permute-done.6.rb_ref, bf16[192,128]{1,0:T(8,128)(2,1)} %get-tuple-element.14, f32[128]{0:T(128)S(1)} %reduce_prod.9, f32[128]{0:T(128)S(1)} %convert_reduce_fusion, pred[]{:T(512)S(6)} %eq.19), kind=kLoop, calls=%fused_computation.11 | loop fusion | flops 196608 | bytes 148481 | tf_op jit(solution)/shard_map/convert_element_type | solution.py:345
  30.8 1.3 %collective-permute-start.7 = (bf16[192,128]{1,0:T(8,128)(2,1)S(1)}, bf16[192,128]{1,0:T(8,128)(2,1)S(1)}, u32[]{:S(2)}, u32[]{:S(2)}) collective-permute-start(bf16[192,128]{1,0:T(8,128)(2,1)S(1)} %fusion.3), channel_id=1, source_target_pairs={{1,2},{0,3},{5,6},{4,7},{9,10},{8,11},{13,14},{12,15},{17,18},{16,... | collective-permute-start | bytes 147464 | tf_op jit(solution)/shard_map/ppermute | solution.py:349
  32.1 0.5 %concatenate.15.mix_ref = f32[2,128]{1,0:T(2,128)} pad(f32[1,128]{1,0:T(1,128)S(1)} %fusion.4, f32[]{:T(128)S(6)} %select_n.82), padding=1_0x0_0 | pad | bytes 1540 | tf_op jit(solution)/shard_map/concatenate | solution.py:356
  32.7 0.4 collective-permute-done.5.za_ref
  33.1 0.0 copy-start.5
  33.1 5.5 %collective-permute-done.7.zb_ref = bf16[192,128]{1,0:T(8,128)(2,1)S(1)} collective-permute-done((bf16[192,128]{1,0:T(8,128)(2,1)S(1)}, bf16[192,128]{1,0:T(8,128)(2,1)S(1)}, u32[]{:S(2)}, u32[]{:S(2)}) %collective-permute-start.7) | collective-permute-done | bytes 49184 | tf_op jit(solution)/shard_map/ppermute | solution.py:349
  38.6 0.0 copy-start.6
  38.6 0.0 copy-done.1
  38.6 0.0 copy-done.3
  38.6 0.0 copy-done.5
  38.6 0.6 %copy-done.6 = bf16[192,128]{1,0:T(8,128)(2,1)} copy-done((bf16[192,128]{1,0:T(8,128)(2,1)}, bf16[192,128]{1,0:T(8,128)(2,1)S(1)}, u32[]{:S(2)}) %copy-start.6) | copy-done | bytes 49176
  39.2 5.9 %shard_map.48 = bf16[8,8,64,128]{3,2,1,0:T(8,128)(2,1)} custom-call(s32[5]{0:T(128)} %stack.39.where_ref, bf16[8,8,64,128]{3,2,1,0:T(8,128)(2,1)} %frames_ref.5, f32[7,8,64,128]{3,2,1,0:T(8,128)} %get-tuple-element.10.pa_ref, f32[2,8,64,128]{3,2,1,0:T(8,128)} %get-tuple-element.11.pb_ref, f32[2,160,128]{2,1,0:T(8,128)} %get-tuple-element.12.pc_ref, ...), custom_call_target="tpu_custom_call" | custom-call | flops 1207959552 | bytes 4194304 | tf_op jit(solution)/shard_map/pallas_call | solution.py:358
  (7 shorter events, 0.1 us)
Async XLA Ops:
  1.2 9.9 %collective-permute-start.1 = (bf16[2,32,128]{2,1,0:T(8,128)(2,1)S(1)}, bf16[2,32,128]{2,1,0:T(8,128)(2,1)S(1)}, u32[]{:S(2)}, u32[]{:S(2)}) collective-permute-start(bf16[2,32,128]{2,1,0:T(8,128)(2,1)S(1)} %constant_dynamic-slice_fusion), channel_id=1, source_target_pairs={{0,16},{16,0},{1,17},{17,1},{2,18},{18,2},{3,19},{19,3},{4,20},{20... | collective-permute-start | bytes 49160 | tf_op jit(solution)/shard_map/ppermute | solution.py:296
  3.7 14.7 %collective-permute-start = (bf16[8,2,64,128]{3,2,1,0:T(8,128)(2,1)S(1)}, bf16[8,2,64,128]{3,2,1,0:T(8,128)(2,1)S(1)}, u32[]{:S(2)}, u32[]{:S(2)}) collective-permute-start(bf16[8,2,64,128]{3,2,1,0:T(8,128)(2,1)S(1)} %constant_dynamic-slice_fusion.1), channel_id=1, source_target_pairs={{0,16},{16,0},{1,17},{17,1},{2,18},{18,2},{3,19},{19,3},{4,20},{20... | collective-permute-start | bytes 786440 | tf_op jit(solution)/shard_map/ppermute | solution.py:295
  4.9 6.1 %copy-start.9 = (f32[8,128]{1,0:T(8,128)S(1)}, f32[8,128]{1,0:T(8,128)}, u32[]{:S(2)}) copy-start(f32[8,128]{1,0:T(8,128)} %dec_ref.5) | copy-start | bytes 12292
  9.6 14.8 %copy-start.4 = (bf16[464,128]{1,0:T(8,128)(2,1)S(1)}, bf16[464,128]{1,0:T(8,128)(2,1)}, u32[]{:S(2)}) copy-start(bf16[464,128]{1,0:T(8,128)(2,1)} %get-tuple-element.13) | copy-start | bytes 356356
  9.6 7.1 %collective-permute-start.4 = (bf16[464,128]{1,0:T(8,128)(2,1)}, bf16[464,128]{1,0:T(8,128)(2,1)S(1)}, u32[]{:S(2)}, u32[]{:S(2)}) collective-permute-start(bf16[464,128]{1,0:T(8,128)(2,1)} %get-tuple-element.13), channel_id=1, source_target_pairs={{0,1},{1,0},{2,3},{4,5},{5,4},{6,7},{8,9},{9,8},{10,11},{12,13},{1... | collective-permute-start | bytes 356360 | tf_op jit(solution)/shard_map/ppermute | solution.py:340
  11.1 7.3 %copy-start = (bf16[10,32,128]{2,1,0:T(8,128)(2,1)}, bf16[10,32,128]{2,1,0:T(8,128)(2,1)S(1)}, u32[]{:S(2)}) copy-start(bf16[10,32,128]{2,1,0:T(8,128)(2,1)S(1)} %maximum_select_fusion.e_ref) | copy-start | bytes 245764
  11.1 5.6 %collective-permute-start.3 = (bf16[10,16,128]{2,1,0:T(8,128)(2,1)S(1)}, bf16[10,16,128]{2,1,0:T(8,128)(2,1)S(1)}, u32[]{:S(2)}, u32[]{:S(2)}) collective-permute-start(bf16[10,16,128]{2,1,0:T(8,128)(2,1)S(1)} %get-tuple-element.17), channel_id=1, source_target_pairs={{4,0},{8,4},{12,8},{5,1},{9,5},{13,9},{6,2},{10,6},{14,10},{7,3},{... | collective-permute-start | bytes 122888 | tf_op jit(solution)/shard_map/ppermute | solution.py:321
  13.0 5.3 %collective-permute-start.2 = (bf16[10,16,128]{2,1,0:T(8,128)(2,1)S(1)}, bf16[10,16,128]{2,1,0:T(8,128)(2,1)S(1)}, u32[]{:S(2)}, u32[]{:S(2)}) collective-permute-start(bf16[10,16,128]{2,1,0:T(8,128)(2,1)S(1)} %get-tuple-element.18), channel_id=1, source_target_pairs={{0,4},{4,8},{8,12},{1,5},{5,9},{9,13},{2,6},{6,10},{10,14},{3,7},{... | collective-permute-start | bytes 122888 | tf_op jit(solution)/shard_map/ppermute | solution.py:320
  16.6 22.0 %copy-start.1 = (bf16[464,128]{1,0:T(8,128)(2,1)}, bf16[464,128]{1,0:T(8,128)(2,1)S(1)}, u32[]{:S(2)}) copy-start(bf16[464,128]{1,0:T(8,128)(2,1)S(1)} %collective-permute-done.4.ra_ref) | copy-start | bytes 356356
  16.7 1.7 %copy-start.7 = (bf16[10,16,128]{2,1,0:T(8,128)(2,1)}, bf16[10,16,128]{2,1,0:T(8,128)(2,1)S(1)}, u32[]{:S(2)}) copy-start(bf16[10,16,128]{2,1,0:T(8,128)(2,1)S(1)} %collective-permute-done.3.r_ref) | copy-start | bytes 122884
  18.4 0.6 %copy-start.8 = (bf16[10,16,128]{2,1,0:T(8,128)(2,1)}, bf16[10,16,128]{2,1,0:T(8,128)(2,1)S(1)}, u32[]{:S(2)}) copy-start(bf16[10,16,128]{2,1,0:T(8,128)(2,1)S(1)} %collective-permute-done.2.l_ref) | copy-start | bytes 122884
  19.0 0.7 %copy-start.2 = (bf16[8,2,64,128]{3,2,1,0:T(8,128)(2,1)}, bf16[8,2,64,128]{3,2,1,0:T(8,128)(2,1)S(1)}, u32[]{:S(2)}) copy-start(bf16[8,2,64,128]{3,2,1,0:T(8,128)(2,1)S(1)} %collective-permute-done.halo_ref) | copy-start | bytes 786436
  23.0 6.9 %collective-permute-start.6 = (bf16[192,128]{1,0:T(8,128)(2,1)}, bf16[192,128]{1,0:T(8,128)(2,1)S(1)}, u32[]{:S(2)}, u32[]{:S(2)}) collective-permute-start(bf16[192,128]{1,0:T(8,128)(2,1)} %get-tuple-element.14), channel_id=1, source_target_pairs={{0,1},{1,0},{2,3},{4,5},{5,4},{6,7},{8,9},{9,8},{10,11},{12,13},{1... | collective-permute-start | bytes 147464 | tf_op jit(solution)/shard_map/ppermute | solution.py:348
  24.4 8.6 %collective-permute-start.5 = (bf16[464,128]{1,0:T(8,128)(2,1)S(1)}, bf16[464,128]{1,0:T(8,128)(2,1)S(1)}, u32[]{:S(2)}, u32[]{:S(2)}) collective-permute-start(bf16[464,128]{1,0:T(8,128)(2,1)S(1)} %fusion.1), channel_id=1, source_target_pairs={{1,2},{0,3},{5,6},{4,7},{9,10},{8,11},{13,14},{12,15},{17,18},{16,... | collective-permute-start | bytes 356360 | tf_op jit(solution)/shard_map/ppermute | solution.py:347
  30.0 8.6 %copy-start.3 = (bf16[192,128]{1,0:T(8,128)(2,1)}, bf16[192,128]{1,0:T(8,128)(2,1)S(1)}, u32[]{:S(2)}) copy-start(bf16[192,128]{1,0:T(8,128)(2,1)S(1)} %collective-permute-done.6.rb_ref) | copy-start | bytes 147460
  30.8 7.8 %collective-permute-start.7 = (bf16[192,128]{1,0:T(8,128)(2,1)S(1)}, bf16[192,128]{1,0:T(8,128)(2,1)S(1)}, u32[]{:S(2)}, u32[]{:S(2)}) collective-permute-start(bf16[192,128]{1,0:T(8,128)(2,1)S(1)} %fusion.3), channel_id=1, source_target_pairs={{1,2},{0,3},{5,6},{4,7},{9,10},{8,11},{13,14},{12,15},{17,18},{16,... | collective-permute-start | bytes 147464 | tf_op jit(solution)/shard_map/ppermute | solution.py:349
  33.1 5.5 %copy-start.5 = (bf16[464,128]{1,0:T(8,128)(2,1)}, bf16[464,128]{1,0:T(8,128)(2,1)S(1)}, u32[]{:S(2)}) copy-start(bf16[464,128]{1,0:T(8,128)(2,1)S(1)} %collective-permute-done.5.za_ref) | copy-start | bytes 356356
  38.6 0.6 %copy-start.6 = (bf16[192,128]{1,0:T(8,128)(2,1)}, bf16[192,128]{1,0:T(8,128)(2,1)S(1)}, u32[]{:S(2)}) copy-start(bf16[192,128]{1,0:T(8,128)(2,1)S(1)} %collective-permute-done.7.zb_ref) | copy-start | bytes 147460

commit v2 on v1

--- a/solution.py
+++ b/solution.py
@@ -9,7 +9,6 @@
 
 F32, BF16 = jnp.float32, jnp.bfloat16
 VMEM = pl.BlockSpec(memory_space=pltpu.VMEM)
-SMEM = pl.BlockSpec(memory_space=pltpu.SMEM)
 
 
 def pair_weights(w_ref, wt, flip):
@@ -68,9 +67,9 @@
     return decays, jnp.sqrt(1.0 - decays * decays)
 
 
-def inner_kernel(two, where_ref, frames_ref, w_ref, dec_ref, p_ref, f_ref, wt, rowbuf, x3):
+def inner_kernel(two, frames_ref, w_ref, dec_ref, p_ref, f_ref, wt, rowbuf, x3):
     frames, height, across, chan = frames_ref.shape
-    flip = where_ref[0]
+    flip = mirrored(two)
     pair_weights(w_ref, wt, flip)
     clear_margins(rowbuf)
     decays, scales = load_decays(dec_ref)
@@ -109,11 +108,14 @@
 
 
 def edge_kernel(
-    two, where_ref, frames_ref, halo_ref, e_ref, l_ref, r_ref, w_ref, dec_ref,
+    two, gx, gy, frames_ref, halo_ref, e_ref, l_ref, r_ref, w_ref, dec_ref,
     p_ref, pc_ref, f_ref, wt, rowbuf, x3, xc, yc,
 ):
     frames, height, across, chan = frames_ref.shape
-    flip = where_ref[0]
+    flip = mirrored(two)
+    x, y_at = lax.axis_index("gx"), lax.axis_index("gy")
+    has_left, has_right = (y_at > 0).astype(F32), (y_at < gy - 1).astype(F32)
+    has_above, has_below = (x > 0).astype(F32), (x < gx - 1).astype(F32)
     pair_weights(w_ref, wt, flip)
     clear_margins(rowbuf)
     decays, scales = load_decays(dec_ref)
@@ -134,7 +136,7 @@
         y = pair_dot(x3, [i * 4 + k for k in range(4)], wt)
         inside = 1.0
         if not two:
-            inside = where_ref[3 if p == 0 else 4].astype(F32)
+            inside = has_above if p == 0 else has_below
 
         def keep(rr, f, s, i=i, p=p, inside=inside):
             border = (rr == 0) if p == 0 else (rr == 1)
@@ -172,14 +174,14 @@
     count = n_pairs * 4
     place = lax.broadcasted_iota(jnp.int32, (count, 2 * chan), 0)
     lane = lax.broadcasted_iota(jnp.int32, (count, 2 * chan), 1)
-    mask = jnp.where(place % 4 == 0, where_ref[1].astype(F32), jnp.where(place % 4 == 3, where_ref[2].astype(F32), 1.0))
+    mask = jnp.where(place % 4 == 0, has_left, jnp.where(place % 4 == 3, has_right, 1.0))
     above = (place < 4) & (lane < chan)
     if two:
         mask = jnp.where(above, 0.0, mask)
     else:
         below = (place >= count - 4) & (lane >= chan)
-        mask = jnp.where(above, mask * where_ref[3].astype(F32), mask)
-        mask = jnp.where(below, mask * where_ref[4].astype(F32), mask)
+        mask = jnp.where(above, mask * has_above, mask)
+        mask = jnp.where(below, mask * has_below, mask)
     s = None
     for f in range(frames):
         both = [jnp.concatenate([v[f : f + 1]] * 2, axis=1) for v in (decays, scales)]
@@ -196,15 +198,22 @@
 
 
 def outer_kernel(
-    two, where_ref, frames_ref, pa_ref, pb_ref, pc_ref, ra_ref, za_ref, rb_ref, zb_ref, mix_ref, w_ref, dec_ref,
+    two, ta, frames_ref, pa_ref, pb_ref, pc_ref, ra_ref, za_ref, rb_ref, zb_ref, w_ref, dec_ref,
     out_ref, wt, rowbuf, x3, sc, ia, ib,
 ):
     frames, height, across, chan = frames_ref.shape
-    flip = where_ref[0]
+    flip = mirrored(two)
     pair_weights(w_ref, wt, flip)
     decays = dec_ref[...]
-    alpha, beta = mix_ref[0:1], mix_ref[1:2]
     rows_a = pa_ref.shape[0]
+    if ta == 4:
+        t = lax.axis_index("ta")
+        end = ra_ref.shape[0]
+        other = jnp.sum(ra_ref[end - 16 : end, :].astype(F32), axis=0, keepdims=True)
+        alpha = ((t == 1) | (t == 3)).astype(F32)
+        beta = jnp.where(t == 3, other, (t == 2).astype(F32))
+    else:
+        alpha, beta = 1.0, 0.0
     ia[...] = alpha * ra_ref[0 : rows_a * across].astype(F32) + beta * za_ref[0 : rows_a * across].astype(F32)
     ib[...] = alpha * rb_ref[...].astype(F32) + beta * zb_ref[...].astype(F32)
     running = [decays[0:1]]
@@ -247,16 +256,20 @@
                 out_ref[f, natural] = (frames_ref[f, natural].astype(F32) + jax.nn.gelu(mixed)).astype(BF16)
 
 
-def call(body, outs, scratch, flops, n_in):
+def call(body, outs, scratch, flops, args):
     return pl.pallas_call(
         body,
         out_shape=outs,
-        in_specs=[SMEM] + [VMEM] * (n_in - 1),
+        in_specs=[VMEM] * len(args),
         out_specs=jax.tree.map(lambda _: VMEM, outs),
         scratch_shapes=scratch,
-        compiler_params=pltpu.CompilerParams(vmem_limit_bytes=56 * 2**20),
+        compiler_params=pltpu.CompilerParams(vmem_limit_bytes=32 * 2**20),
         cost_estimate=pl.CostEstimate(flops=flops, bytes_accessed=4 * 2**20, transcendentals=0),
-    )
+    )(*[pltpu.with_memory_space_constraint(a, pltpu.VMEM) for a in args])
+
+
+def mirrored(two):
+    return lax.axis_index("gx") if two else 0
 
 
 def forward(ends):
@@ -283,9 +296,7 @@
 def on_device(gx, gy, ta, frames, in_weight, out_weight, decays):
     n_frames, height, across, chan = frames.shape
     two = gx == 2
-    x, y, t = (lax.axis_index(a) for a in ("gx", "gy", "ta"))
-    flip = x if two else jnp.zeros_like(x)
-    where = jnp.stack([flip, (y > 0), (y < gy - 1), (x > 0), (x < gx - 1)]).astype(jnp.int32)
+    x, t = lax.axis_index("gx"), lax.axis_index("ta")
 
     cols = jnp.concatenate([frames[:, :, :2], frames[:, :, across - 2 :]], axis=2)
     cols = cols.transpose(1, 2, 0, 3).reshape(height, 4 * n_frames, chan)
@@ -309,30 +320,30 @@
     rowbuf = pltpu.VMEM((16, across + 16, chan), F32)
     cells = n_frames * across
     flops = 2 * 9 * chan * chan * cells
-    sds = jax.ShapeDtypeStruct
+    near_mem = pltpu.VMEM
     pa, fa = call(
         functools.partial(inner_kernel, two),
-        (sds((rows_a, n_frames, across, chan), F32), sds((rows_a * across + 16, chan), BF16)),
+        (near_mem((rows_a, n_frames, across, chan), F32), near_mem((rows_a * across + 16, chan), BF16)),
         [wt, rowbuf, pltpu.VMEM((height, cells, 3 * chan), BF16)],
-        flops * height, 4,
-    )(where, frames, in_weight, decays)
+        flops * height, [frames, in_weight, decays],
+    )
 
     left = lax.ppermute(cols[:, 2 * n_frames :], "gy", forward(gy))
     right = lax.ppermute(cols[:, : 2 * n_frames], "gy", backward(gy))
     n_cols = (height // 2 + 1) * 4
     pb, pc, fb = call(
-        functools.partial(edge_kernel, two),
+        functools.partial(edge_kernel, two, gx, gy),
         (
-            sds((rows_b, n_frames, across, chan), F32),
-            sds((2, n_cols * n_frames, chan), F32),
-            sds((rows_b * across + 64, chan), BF16),
+            near_mem((rows_b, n_frames, across, chan), F32),
+            near_mem((2, n_cols * n_frames, chan), F32),
+            near_mem((rows_b * across + 64, chan), BF16),
         ),
         [
             wt, rowbuf, pltpu.VMEM((2 * rows_b, cells, 3 * chan), BF16),
             pltpu.VMEM((n_cols * n_frames, 12 * chan), BF16), pltpu.VMEM((2, n_cols * n_frames, chan), F32),
         ],
-        flops * rows_b, 8,
-    )(where, frames, halo, cols, left, right, in_weight, decays)
+        flops * rows_b, [frames, halo, cols, left, right, in_weight, decays],
+    )
 
     total = jnp.prod(decays, axis=0)[None]
     if ta == 4:
@@ -347,24 +358,20 @@
         za = lax.ppermute(joined(fa, ra), "ta", far)
         rb = lax.ppermute(fb, "ta", near)
         zb = lax.ppermute(joined(fb, rb), "ta", far)
-        alpha = jnp.where((t == 1) | (t == 3), 1.0, 0.0) * jnp.ones_like(total)
-        beta = jnp.where(t == 2, 1.0, jnp.where(t == 3, other, 0.0))
     else:
         ra, rb = carry_general([fa, fb], total, ta)
         za, zb = ra, rb
-        alpha, beta = jnp.ones_like(total), jnp.zeros_like(total)
-    mix = jnp.concatenate([alpha, beta])
 
     return call(
-        functools.partial(outer_kernel, two),
-        sds(frames.shape, BF16),
+        functools.partial(outer_kernel, two, ta),
+        jax.ShapeDtypeStruct(frames.shape, BF16),
         [
             wt, rowbuf, pltpu.VMEM((height + 2, cells, 3 * chan), BF16),
             pltpu.VMEM((n_frames, 2, (n_cols + 7) // 8 * 8, chan), F32),
             pltpu.VMEM((rows_a * across, chan), F32), pltpu.VMEM((rows_b * across + 64, chan), F32),
         ],
-        flops * height, 12,
-    )(where, frames, pa, pb, pc, ra, za, rb, zb, mix, out_weight, decays)
+        flops * height, [frames, pa, pb, pc, ra, za, rb, zb, out_weight, decays],
+    )
 
 
 def solution(mesh):

time: 45.5 us -> 40.1 us (0.88)
  the two profiles are of different devices: /device:TPU:28 before, /device:TPU:19 now
where the time goes in v2:
time: 40.1 us; the launch traced here: 39.6 us
  starting transfers between devices  15.2 us (38%)
  waiting for transfers between devices  9.7 us (24%)
  Pallas kernels  7.7 us (19%)
  local copies, waits for them, and re-layouts  6.59 us (16%)
    pallas_call x3, Pallas kernels, call(): pl.pallas_call(body, out_shape=outs, in_specs=[VMEM] * len(args), out_spe...  7.7 us
    ppermute x1, waiting for transfers between devices, on_device(): za = lax.ppermute(joined(fa, ra), 'ta', far)  7.62 us
    unnamed x14, local copies, waits for them, and re-layouts  3.85 us
    ppermute x1, starting transfers between devices, on_device(): right = lax.ppermute(cols[:, :2 * n_frames], 'gy', backward(gy))  3.42 us
    ppermute x1, starting transfers between devices, on_device(): ra = lax.ppermute(fa, 'ta', near)  3.34 us
    ppermute x1, starting transfers between devices, on_device(): left = lax.ppermute(cols[:, 2 * n_frames:], 'gy', forward(gy))  3.04 us
    dynamic_slice x1, local copies, waits for them, and re-layouts, on_device(): lax.dynamic_slice_in_dim(frames, start, 2, axis=1)  1.67 us
    ppermute x1, starting transfers between devices, on_device(): rb = lax.ppermute(fb, 'ta', near)  1.29 us
  transfers between devices with their start and end apart: 8, of which 3 were waited for; matrix products, arithmetic and copies ran while one was open for 5% of the time, Pallas kernels for 5%

profile of v2, /device:TPU:19, one launch (start us, length us, event | category | flops | bytes accessed | tf_op | source)
XLA Modules:
  0.0 39.6 jit_solution(15203573338826183529)
XLA Ops:
  0.0 1.0 %fusion.4 = (bf16[8,8,2,128]{3,2,1,0:T(2,128)(2,1)S(1)}, bf16[8,8,2,128]{3,2,1,0:T(2,128)(2,1)S(1)}) fusion(bf16[8,8,64,128]{3,2,1,0:T(8,128)(2,1)} %frames_ref.5), kind=kLoop, calls=%fused_computation.18 | loop fusion | bytes 131072 | tf_op jit(solution)/shard_map/slice | solution.py:301
  1.0 0.1 maximum_bitcast_fusion
  1.2 0.3 collective-permute-start.1
  1.5 1.7 %constant_dynamic-slice_fusion.1 = bf16[8,2,64,128]{3,2,1,0:T(8,128)(2,1)} fusion(bf16[8,8,64,128]{3,2,1,0:T(8,128)(2,1)} %frames_ref.5, s32[]{:T(128)S(6)} %select_n.30), kind=kLoop, calls=%fused_computation.17 | loop fusion | bytes 524292 | tf_op jit(solution)/shard_map/dynamic_slice | solution.py:306
  3.2 1.2 %collective-permute-start = (bf16[8,2,64,128]{3,2,1,0:T(8,128)(2,1)}, bf16[8,2,64,128]{3,2,1,0:T(8,128)(2,1)}, u32[]{:S(2)}, u32[]{:S(2)}) collective-permute-start(bf16[8,2,64,128]{3,2,1,0:T(8,128)(2,1)} %constant_dynamic-slice_fusion.1), channel_id=1, source_target_pairs={{0,16},{16,0},{1,17},{17,1},{2,18},{18,2},{3,19},{19,3},{4,20},{20... | collective-permute-start | bytes 786440 | tf_op jit(solution)/shard_map/ppermute | solution.py:306
  4.4 0.0 copy-start
  4.4 1.2 %copy-done = bf16[8,8,64,128]{3,2,1,0:T(8,128)(2,1)S(1)} copy-done((bf16[8,8,64,128]{3,2,1,0:T(8,128)(2,1)S(1)}, bf16[8,8,64,128]{3,2,1,0:T(8,128)(2,1)}, u32[]{:S(2)}) %copy-start) | copy-done | bytes 1048600
  5.6 0.0 copy-start.3
  5.6 1.0 %copy-done.3 = bf16[3,3,128,128]{3,2,1,0:T(8,128)(2,1)S(1)} copy-done((bf16[3,3,128,128]{3,2,1,0:T(8,128)(2,1)S(1)}, bf16[3,3,128,128]{3,2,1,0:T(8,128)(2,1)}, u32[]{:S(2)}) %copy-start.3) | copy-done | bytes 294936
  6.6 0.0 copy-start.5
  6.6 0.7 %copy-done.5 = f32[8,128]{1,0:T(8,128)S(1)} copy-done((f32[8,128]{1,0:T(8,128)S(1)}, f32[8,128]{1,0:T(8,128)}, u32[]{:S(2)}) %copy-start.5) | copy-done | bytes 4120
  7.2 0.0 copy-start.6
  7.2 0.0 copy-start.1
  7.3 2.0 %shard_map.46 = (f32[7,8,64,128]{3,2,1,0:T(8,128)S(1)}, bf16[464,128]{1,0:T(8,128)(2,1)S(1)}) custom-call(bf16[8,8,64,128]{3,2,1,0:T(8,128)(2,1)S(1)} %copy-done, bf16[3,3,128,128]{3,2,1,0:T(8,128)(2,1)S(1)} %copy-done.3, f32[8,128]{1,0:T(8,128)S(1)} %copy-done.5), custom_call_target="tpu_custom_call" | custom-call | flops 1207959552 | bytes 4194304 | tf_op jit(solution)/shard_map/pallas_call | solution.py:260
  9.2 0.0 copy-start.2
  9.2 3.3 %collective-permute-start.4 = (bf16[464,128]{1,0:T(8,128)(2,1)S(1)}, bf16[464,128]{1,0:T(8,128)(2,1)S(1)}, u32[]{:S(2)}, u32[]{:S(2)}) collective-permute-start(bf16[464,128]{1,0:T(8,128)(2,1)S(1)} %get-tuple-element.13), channel_id=1, source_target_pairs={{0,1},{1,0},{2,3},{4,5},{5,4},{6,7},{8,9},{9,8},{10,11},{12,13},{1... | collective-permute-start | bytes 356360 | tf_op jit(solution)/shard_map/ppermute | solution.py:351
  12.6 0.0 copy-done.6
  12.6 0.0 collective-permute-done.1
  12.7 3.4 %collective-permute-start.3 = (bf16[10,16,128]{2,1,0:T(8,128)(2,1)S(1)}, bf16[10,16,128]{2,1,0:T(8,128)(2,1)S(1)}, u32[]{:S(2)}, u32[]{:S(2)}) collective-permute-start(bf16[10,16,128]{2,1,0:T(8,128)(2,1)S(1)} %get-tuple-element.17), channel_id=1, source_target_pairs={{4,0},{8,4},{12,8},{5,1},{9,5},{13,9},{6,2},{10,6},{14,10},{7,3},{... | collective-permute-start | bytes 122888 | tf_op jit(solution)/shard_map/ppermute | solution.py:332
  16.1 3.0 %collective-permute-start.2 = (bf16[10,16,128]{2,1,0:T(8,128)(2,1)S(1)}, bf16[10,16,128]{2,1,0:T(8,128)(2,1)S(1)}, u32[]{:S(2)}, u32[]{:S(2)}) collective-permute-start(bf16[10,16,128]{2,1,0:T(8,128)(2,1)S(1)} %get-tuple-element.18), channel_id=1, source_target_pairs={{0,4},{4,8},{8,12},{1,5},{5,9},{9,13},{2,6},{6,10},{10,14},{3,7},{... | collective-permute-start | bytes 122888 | tf_op jit(solution)/shard_map/ppermute | solution.py:331
  19.2 0.0 collective-permute-done.4.ra_ref
  19.2 0.0 collective-permute-done.3.r_ref
  19.2 1.0 %collective-permute-done.2.l_ref = bf16[10,16,128]{2,1,0:T(8,128)(2,1)S(1)} collective-permute-done((bf16[10,16,128]{2,1,0:T(8,128)(2,1)S(1)}, bf16[10,16,128]{2,1,0:T(8,128)(2,1)S(1)}, u32[]{:S(2)}, u32[]{:S(2)}) %collective-permute-start.2) | collective-permute-done | bytes 40992 | tf_op jit(solution)/shard_map/ppermute | solution.py:331
  20.2 0.0 collective-permute-done.halo_ref
  20.2 0.0 copy-done.1
  20.2 0.0 copy-start.4
  20.2 1.0 %copy-done.4 = bf16[3,3,128,128]{3,2,1,0:T(8,128)(2,1)S(1)} copy-done((bf16[3,3,128,128]{3,2,1,0:T(8,128)(2,1)S(1)}, bf16[3,3,128,128]{3,2,1,0:T(8,128)(2,1)}, u32[]{:S(2)}) %copy-start.4) | copy-done | bytes 294936
  21.2 2.0 %shard_map.47 = (f32[2,8,64,128]{3,2,1,0:T(8,128)S(1)}, f32[2,160,128]{2,1,0:T(8,128)S(1)}, bf16[192,128]{1,0:T(8,128)(2,1)S(1)}) custom-call(bf16[8,8,64,128]{3,2,1,0:T(8,128)(2,1)S(1)} %copy-done.1, bf16[8,2,64,128]{3,2,1,0:T(8,128)(2,1)} %collective-permute-done.halo_ref, bf16[10,32,128]{2,1,0:T(8,128)(2,1)S(1)} %maximum_select_fusion.e_ref, ...), custom_call_target="tpu_custom_call" | custom-call | flops 301989888 | bytes 4194304 | tf_op jit(solution)/shard_map/pallas_call | solution.py:260
  23.2 1.3 %collective-permute-start.6 = (bf16[192,128]{1,0:T(8,128)(2,1)S(1)}, bf16[192,128]{1,0:T(8,128)(2,1)S(1)}, u32[]{:S(2)}, u32[]{:S(2)}) collective-permute-start(bf16[192,128]{1,0:T(8,128)(2,1)S(1)} %get-tuple-element.14), channel_id=1, source_target_pairs={{0,1},{1,0},{2,3},{4,5},{5,4},{6,7},{8,9},{9,8},{10,11},{12,13},{1... | collective-permute-start | bytes 147464 | tf_op jit(solution)/shard_map/ppermute | solution.py:359
  24.5 0.1 fusion.1
  24.6 1.3 %collective-permute-start.5 = (bf16[464,128]{1,0:T(8,128)(2,1)S(1)}, bf16[464,128]{1,0:T(8,128)(2,1)S(1)}, u32[]{:S(2)}, u32[]{:S(2)}) collective-permute-start(bf16[464,128]{1,0:T(8,128)(2,1)S(1)} %fusion.1), channel_id=1, source_target_pairs={{1,2},{0,3},{5,6},{4,7},{9,10},{8,11},{13,14},{12,15},{17,18},{16,... | collective-permute-start | bytes 356360 | tf_op jit(solution)/shard_map/ppermute | solution.py:358
  25.9 0.0 collective-permute-done.6.rb_ref
  25.9 1.3 %collective-permute-start.7 = (bf16[192,128]{1,0:T(8,128)(2,1)S(1)}, bf16[192,128]{1,0:T(8,128)(2,1)S(1)}, u32[]{:S(2)}, u32[]{:S(2)}) collective-permute-start(bf16[192,128]{1,0:T(8,128)(2,1)S(1)} %fusion.3), channel_id=1, source_target_pairs={{1,2},{0,3},{5,6},{4,7},{9,10},{8,11},{13,14},{12,15},{17,18},{16,... | collective-permute-start | bytes 147464 | tf_op jit(solution)/shard_map/ppermute | solution.py:360
  27.2 7.6 %collective-permute-done.5.za_ref = bf16[464,128]{1,0:T(8,128)(2,1)S(1)} collective-permute-done((bf16[464,128]{1,0:T(8,128)(2,1)S(1)}, bf16[464,128]{1,0:T(8,128)(2,1)S(1)}, u32[]{:S(2)}, u32[]{:S(2)}) %collective-permute-start.5) | collective-permute-done | bytes 118816 | tf_op jit(solution)/shard_map/ppermute | solution.py:358
  34.8 1.0 %collective-permute-done.7.zb_ref = bf16[192,128]{1,0:T(8,128)(2,1)S(1)} collective-permute-done((bf16[192,128]{1,0:T(8,128)(2,1)S(1)}, bf16[192,128]{1,0:T(8,128)(2,1)S(1)}, u32[]{:S(2)}, u32[]{:S(2)}) %collective-permute-start.7) | collective-permute-done | bytes 49184 | tf_op jit(solution)/shard_map/ppermute | solution.py:360
  35.9 0.0 copy-done.2
  35.9 3.7 %shard_map.48 = bf16[8,8,64,128]{3,2,1,0:T(8,128)(2,1)} custom-call(bf16[8,8,64,128]{3,2,1,0:T(8,128)(2,1)S(1)} %copy-done.1, f32[7,8,64,128]{3,2,1,0:T(8,128)S(1)} %get-tuple-element.10.pa_ref, f32[2,8,64,128]{3,2,1,0:T(8,128)S(1)} %get-tuple-element.11.pb_ref, f32[2,160,128]{2,1,0:T(8,128)S(1)} %get-tuple-element.12.pc_ref, ...), custom_call_target="tpu_custom_call" | custom-call | flops 1207959552 | bytes 4194304 | tf_op jit(solution)/shard_map/pallas_call | solution.py:260
  (7 shorter events, 0.1 us)
Async XLA Ops:
  1.2 11.5 %collective-permute-start.1 = (bf16[2,32,128]{2,1,0:T(8,128)(2,1)S(1)}, bf16[2,32,128]{2,1,0:T(8,128)(2,1)S(1)}, u32[]{:S(2)}, u32[]{:S(2)}) collective-permute-start(bf16[2,32,128]{2,1,0:T(8,128)(2,1)S(1)} %constant_dynamic-slice_fusion), channel_id=1, source_target_pairs={{0,16},{16,0},{1,17},{17,1},{2,18},{18,2},{3,19},{19,3},{4,20},{20... | collective-permute-start | bytes 49160 | tf_op jit(solution)/shard_map/ppermute | solution.py:307
  3.2 17.1 %collective-permute-start = (bf16[8,2,64,128]{3,2,1,0:T(8,128)(2,1)}, bf16[8,2,64,128]{3,2,1,0:T(8,128)(2,1)}, u32[]{:S(2)}, u32[]{:S(2)}) collective-permute-start(bf16[8,2,64,128]{3,2,1,0:T(8,128)(2,1)} %constant_dynamic-slice_fusion.1), channel_id=1, source_target_pairs={{0,16},{16,0},{1,17},{17,1},{2,18},{18,2},{3,19},{19,3},{4,20},{20... | collective-permute-start | bytes 786440 | tf_op jit(solution)/shard_map/ppermute | solution.py:306
  4.4 1.2 %copy-start = (bf16[8,8,64,128]{3,2,1,0:T(8,128)(2,1)S(1)}, bf16[8,8,64,128]{3,2,1,0:T(8,128)(2,1)}, u32[]{:S(2)}) copy-start(bf16[8,8,64,128]{3,2,1,0:T(8,128)(2,1)} %frames_ref.5) | copy-start | bytes 3145732
  5.6 1.0 %copy-start.3 = (bf16[3,3,128,128]{3,2,1,0:T(8,128)(2,1)S(1)}, bf16[3,3,128,128]{3,2,1,0:T(8,128)(2,1)}, u32[]{:S(2)}) copy-start(bf16[3,3,128,128]{3,2,1,0:T(8,128)(2,1)} %w_ref.4) | copy-start | bytes 884740
  6.6 0.7 %copy-start.5 = (f32[8,128]{1,0:T(8,128)S(1)}, f32[8,128]{1,0:T(8,128)}, u32[]{:S(2)}) copy-start(f32[8,128]{1,0:T(8,128)} %dec_ref.5) | copy-start | bytes 12292
  7.2 5.4 %copy-start.6 = (f32[8,128]{1,0:T(8,128)S(1)}, f32[8,128]{1,0:T(8,128)}, u32[]{:S(2)}) copy-start(f32[8,128]{1,0:T(8,128)} %dec_ref.5) | copy-start | bytes 12292
  7.2 13.0 %copy-start.1 = (bf16[8,8,64,128]{3,2,1,0:T(8,128)(2,1)S(1)}, bf16[8,8,64,128]{3,2,1,0:T(8,128)(2,1)}, u32[]{:S(2)}) copy-start(bf16[8,8,64,128]{3,2,1,0:T(8,128)(2,1)} %frames_ref.5) | copy-start | bytes 3145732
  9.2 26.6 %copy-start.2 = (bf16[3,3,128,128]{3,2,1,0:T(8,128)(2,1)S(1)}, bf16[3,3,128,128]{3,2,1,0:T(8,128)(2,1)}, u32[]{:S(2)}) copy-start(bf16[3,3,128,128]{3,2,1,0:T(8,128)(2,1)} %w_ref.5) | copy-start | bytes 884740
  9.2 9.9 %collective-permute-start.4 = (bf16[464,128]{1,0:T(8,128)(2,1)S(1)}, bf16[464,128]{1,0:T(8,128)(2,1)S(1)}, u32[]{:S(2)}, u32[]{:S(2)}) collective-permute-start(bf16[464,128]{1,0:T(8,128)(2,1)S(1)} %get-tuple-element.13), channel_id=1, source_target_pairs={{0,1},{1,0},{2,3},{4,5},{5,4},{6,7},{8,9},{9,8},{10,11},{12,13},{1... | collective-permute-start | bytes 356360 | tf_op jit(solution)/shard_map/ppermute | solution.py:351
  12.7 6.5 %collective-permute-start.3 = (bf16[10,16,128]{2,1,0:T(8,128)(2,1)S(1)}, bf16[10,16,128]{2,1,0:T(8,128)(2,1)S(1)}, u32[]{:S(2)}, u32[]{:S(2)}) collective-permute-start(bf16[10,16,128]{2,1,0:T(8,128)(2,1)S(1)} %get-tuple-element.17), channel_id=1, source_target_pairs={{4,0},{8,4},{12,8},{5,1},{9,5},{13,9},{6,2},{10,6},{14,10},{7,3},{... | collective-permute-start | bytes 122888 | tf_op jit(solution)/shard_map/ppermute | solution.py:332
  16.1 4.1 %collective-permute-start.2 = (bf16[10,16,128]{2,1,0:T(8,128)(2,1)S(1)}, bf16[10,16,128]{2,1,0:T(8,128)(2,1)S(1)}, u32[]{:S(2)}, u32[]{:S(2)}) collective-permute-start(bf16[10,16,128]{2,1,0:T(8,128)(2,1)S(1)} %get-tuple-element.18), channel_id=1, source_target_pairs={{0,4},{4,8},{8,12},{1,5},{5,9},{9,13},{2,6},{6,10},{10,14},{3,7},{... | collective-permute-start | bytes 122888 | tf_op jit(solution)/shard_map/ppermute | solution.py:331
  20.2 1.0 %copy-start.4 = (bf16[3,3,128,128]{3,2,1,0:T(8,128)(2,1)S(1)}, bf16[3,3,128,128]{3,2,1,0:T(8,128)(2,1)}, u32[]{:S(2)}) copy-start(bf16[3,3,128,128]{3,2,1,0:T(8,128)(2,1)} %w_ref.4) | copy-start | bytes 884740
  23.2 2.7 %collective-permute-start.6 = (bf16[192,128]{1,0:T(8,128)(2,1)S(1)}, bf16[192,128]{1,0:T(8,128)(2,1)S(1)}, u32[]{:S(2)}, u32[]{:S(2)}) collective-permute-start(bf16[192,128]{1,0:T(8,128)(2,1)S(1)} %get-tuple-element.14), channel_id=1, source_target_pairs={{0,1},{1,0},{2,3},{4,5},{5,4},{6,7},{8,9},{9,8},{10,11},{12,13},{1... | collective-permute-start | bytes 147464 | tf_op jit(solution)/shard_map/ppermute | solution.py:359
  24.6 10.3 %collective-permute-start.5 = (bf16[464,128]{1,0:T(8,128)(2,1)S(1)}, bf16[464,128]{1,0:T(8,128)(2,1)S(1)}, u32[]{:S(2)}, u32[]{:S(2)}) collective-permute-start(bf16[464,128]{1,0:T(8,128)(2,1)S(1)} %fusion.1), channel_id=1, source_target_pairs={{1,2},{0,3},{5,6},{4,7},{9,10},{8,11},{13,14},{12,15},{17,18},{16,... | collective-permute-start | bytes 356360 | tf_op jit(solution)/shard_map/ppermute | solution.py:358
  25.9 9.9 %collective-permute-start.7 = (bf16[192,128]{1,0:T(8,128)(2,1)S(1)}, bf16[192,128]{1,0:T(8,128)(2,1)S(1)}, u32[]{:S(2)}, u32[]{:S(2)}) collective-permute-start(bf16[192,128]{1,0:T(8,128)(2,1)S(1)} %fusion.3), channel_id=1, source_target_pairs={{1,2},{0,3},{5,6},{4,7},{9,10},{8,11},{13,14},{12,15},{17,18},{16,... | collective-permute-start | bytes 147464 | tf_op jit(solution)/shard_map/ppermute | solution.py:360

commit v3 on v2

--- a/solution.py
+++ b/solution.py
@@ -9,6 +9,7 @@
 
 F32, BF16 = jnp.float32, jnp.bfloat16
 VMEM = pl.BlockSpec(memory_space=pltpu.VMEM)
+HBM = pl.BlockSpec(memory_space=pltpu.HBM)
 
 
 def pair_weights(w_ref, wt, flip):
@@ -65,6 +66,25 @@
 def load_decays(dec_ref):
     decays = dec_ref[...]
     return decays, jnp.sqrt(1.0 - decays * decays)
+
+
+def fetch_kernel(frames_hbm, w_in_hbm, w_out_hbm, dec_hbm, frames_ref, w_in_ref, w_out_ref, dec_ref, cols_ref, edge, sems):
+    pairs = [(frames_hbm, frames_ref), (dec_hbm, dec_ref), (w_in_hbm, w_in_ref), (w_out_hbm, w_out_ref)]
+    copies = [pltpu.make_async_copy(src, dst, sems.at[i]) for i, (src, dst) in enumerate(pairs)]
+    for copy in copies:
+        copy.start()
+    copies[0].wait()
+    frames, height, across, chan = frames_ref.shape
+    for r in range(height):
+        for f in range(frames):
+            at = r * 4 * frames + f
+            edge[pl.ds(at, 2, stride=frames), :] = frames_ref[f, r, 0:16, :].astype(F32)[0:2]
+            last = frames_ref[f, r, across - 16 : across, :].astype(F32)[14:16]
+            edge[pl.ds(at + 2 * frames, 2, stride=frames), :] = last
+    for r in range(height):
+        cols_ref[r] = edge[r * 4 * frames : (r + 1) * 4 * frames, :].astype(BF16)
+    for copy in copies[1:]:
+        copy.wait()
 
 
 def inner_kernel(two, frames_ref, w_ref, dec_ref, p_ref, f_ref, wt, rowbuf, x3):
@@ -108,15 +128,15 @@
 
 
 def edge_kernel(
-    two, gx, gy, frames_ref, halo_ref, e_ref, l_ref, r_ref, w_ref, dec_ref,
-    p_ref, pc_ref, f_ref, wt, rowbuf, x3, xc, yc,
+    two, gx, gy, frames_ref, halo_ref, e_ref, l_ref, r_ref, wt, dec_ref, w_next,
+    p_ref, pc_ref, f_ref, wt_next, rowbuf, x3, xc, yc,
 ):
     frames, height, across, chan = frames_ref.shape
     flip = mirrored(two)
     x, y_at = lax.axis_index("gx"), lax.axis_index("gy")
     has_left, has_right = (y_at > 0).astype(F32), (y_at < gy - 1).astype(F32)
     has_above, has_below = (x > 0).astype(F32), (x < gx - 1).astype(F32)
-    pair_weights(w_ref, wt, flip)
+    pair_weights(w_next, wt_next, flip)
     clear_margins(rowbuf)
     decays, scales = load_decays(dec_ref)
     pairs = [height // 2] if two else [0, height // 2]
@@ -198,12 +218,11 @@
 
 
 def outer_kernel(
-    two, ta, frames_ref, pa_ref, pb_ref, pc_ref, ra_ref, za_ref, rb_ref, zb_ref, w_ref, dec_ref,
-    out_ref, wt, rowbuf, x3, sc, ia, ib,
+    two, ta, frames_ref, pa_ref, pb_ref, pc_ref, ra_ref, za_ref, rb_ref, zb_ref, wt, dec_ref,
+    out_ref, rowbuf, x3, sc, ia, ib, done, sems,
 ):
     frames, height, across, chan = frames_ref.shape
     flip = mirrored(two)
-    pair_weights(w_ref, wt, flip)
     decays = dec_ref[...]
     rows_a = pa_ref.shape[0]
     if ta == 4:
@@ -245,119 +264,152 @@
             rowbuf[slot, 7 + across : 8 + across, :] = sc[f, h, corner + 2 : corner + 3, :]
             rowbuf[slot, 8 + across : 9 + across, :] = sc[f, h, corner + 3 : corner + 4, :]
             three_taps(rowbuf, slot, x3, n, f, rowbuf[slot, 8 : 8 + across, :].astype(BF16))
+    copies = []
     for p in range(height // 2):
         slots = [n if n > 0 or not two else None for n in range(2 * p, 2 * p + 4)]
         y = pair_dot(x3, slots, wt)
+        first = jnp.where(flip == 1, height - 2 - 2 * p, 2 * p)
         for rr in range(2):
-            r = 2 * p + rr
-            natural = jnp.where(flip == 1, height - 1 - r, r)
+            row = jnp.where(flip == 1, 1 - rr, rr)
             for f in range(frames):
                 mixed = y[f * across : (f + 1) * across, rr * chan : (rr + 1) * chan]
-                out_ref[f, natural] = (frames_ref[f, natural].astype(F32) + jax.nn.gelu(mixed)).astype(BF16)
-
-
-def call(body, outs, scratch, flops, args):
+                frame = frames_ref[f, first + row].astype(F32)
+                done[p, f, row] = (frame + jax.nn.gelu(mixed)).astype(BF16)
+        copies.append(pltpu.make_async_copy(done.at[p], out_ref.at[:, pl.ds(first, 2)], sems.at[p]))
+        copies[-1].start()
+    for copy in copies:
+        copy.wait()
+
+
+def call(body, outs, scratch, flops, args, place=(VMEM, VMEM)):
+    args = [pltpu.with_memory_space_constraint(a, place[0].memory_space) for a in args]
     return pl.pallas_call(
         body,
         out_shape=outs,
-        in_specs=[VMEM] * len(args),
-        out_specs=jax.tree.map(lambda _: VMEM, outs),
+        in_specs=[place[0]] * len(args),
+        out_specs=jax.tree.map(lambda _: place[1], outs),
         scratch_shapes=scratch,
         compiler_params=pltpu.CompilerParams(vmem_limit_bytes=32 * 2**20),
         cost_estimate=pl.CostEstimate(flops=flops, bytes_accessed=4 * 2**20, transcendentals=0),
-    )(*[pltpu.with_memory_space_constraint(a, pltpu.VMEM) for a in args])
+    )(*args)
 
 
 def mirrored(two):
     return lax.axis_index("gx") if two else 0
 
 
-def forward(ends):
-    return [(i, i + 1) for i in range(ends - 1)]
-
-
-def backward(ends):
-    return [(i + 1, i) for i in range(ends - 1)]
+def swapped(value, axis, count, odd_first):
+    off = 1 if odd_first else 0
+    pairs = [((i + off) % count, (i + 1 + off) % count) for i in range(0, count, 2)]
+    return lax.ppermute(value, axis, pairs + [(b, a) for a, b in pairs])
+
+
+def exchange(low, high, axis, count):
+    if count % 2:
+        up = lax.ppermute(high, axis, [(i, i + 1) for i in range(count - 1)])
+        return up, lax.ppermute(low, axis, [(i + 1, i) for i in range(count - 1)])
+    at = lax.axis_index(axis)
+    odd = at % 2 == 1
+    near = swapped(jnp.where(odd, low, high), axis, count, False)
+    if count == 2:
+        far = jnp.zeros_like(near)
+    else:
+        far = swapped(jnp.where(odd, high, low), axis, count, True)
+        far = jnp.where((at == 0) | (at == count - 1), jnp.zeros_like(far), far)
+    return jnp.where(odd, near, far), jnp.where(odd, far, near)
 
 
 def carry_general(locals_, total, ta):
+    t = lax.axis_index("ta")
+
+    def moved(value, step):
+        got = lax.ppermute(value, "ta", [(i, (i + step) % ta) for i in range(ta)])
+        return jnp.where(t >= step, got, jnp.zeros_like(got))
+
     step = 1
     while step < ta:
-        pairs = [(i, i + step) for i in range(ta - step)]
-        moved = [lax.ppermute(v, "ta", pairs) for v in locals_]
-        moved_total = lax.ppermute(total, "ta", pairs)
-        has = lax.axis_index("ta") >= step
-        locals_ = [(v.astype(F32) + total * m.astype(F32)).astype(BF16) for v, m in zip(locals_, moved)]
-        total = jnp.where(has, total * moved_total, total)
+        came = [moved(v, step) for v in locals_]
+        locals_ = [(v.astype(F32) + total * m.astype(F32)).astype(BF16) for v, m in zip(locals_, came)]
+        total = jnp.where(t >= step, total * moved(total, step), total)
         step *= 2
-    return [lax.ppermute(v, "ta", forward(ta)) for v in locals_]
+    return [moved(v, 1) for v in locals_]
 
 
 def on_device(gx, gy, ta, frames, in_weight, out_weight, decays):
     n_frames, height, across, chan = frames.shape
     two = gx == 2
     x, t = lax.axis_index("gx"), lax.axis_index("ta")
-
-    cols = jnp.concatenate([frames[:, :, :2], frames[:, :, across - 2 :]], axis=2)
-    cols = cols.transpose(1, 2, 0, 3).reshape(height, 4 * n_frames, chan)
+    near_mem = pltpu.VMEM
+    frames, in_weight, out_weight, decays, cols = call(
+        fetch_kernel,
+        (
+            near_mem(frames.shape, BF16), near_mem(in_weight.shape, BF16), near_mem(out_weight.shape, BF16),
+            near_mem(decays.shape, F32), near_mem((height, 4 * n_frames, chan), BF16),
+        ),
+        [pltpu.VMEM((height * 4 * n_frames, chan), F32), pltpu.SemaphoreType.DMA((4,))],
+        0, [frames, in_weight, out_weight, decays], (HBM, VMEM),
+    )
     if two:
-        swap = [(0, 1), (1, 0)]
         start = jnp.where(x == 1, 0, height - 2)
-        halo = lax.ppermute(lax.dynamic_slice_in_dim(frames, start, 2, axis=1), "gx", swap)
-        corner = lax.ppermute(lax.dynamic_slice_in_dim(cols, start, 2, axis=0), "gx", swap)
+        corner = swapped(lax.dynamic_slice_in_dim(cols, start, 2, axis=0), "gx", 2, False)
+        halo = swapped(lax.dynamic_slice_in_dim(frames, start, 2, axis=1), "gx", 2, False)
         cols = jnp.where(x == 1, jnp.concatenate([corner, cols]), jnp.concatenate([cols, corner]))
     else:
-        above = lax.ppermute(frames[:, height - 2 :], "gx", forward(gx))
-        below = lax.ppermute(frames[:, :2], "gx", backward(gx))
+        over, under = exchange(cols[:2], cols[height - 2 :], "gx", gx)
+        cols = jnp.concatenate([over, cols, under])
+        above, below = exchange(frames[:, :2], frames[:, height - 2 :], "gx", gx)
         halo = jnp.concatenate([above, below], axis=1)
-        over = lax.ppermute(cols[height - 2 :], "gx", forward(gx))
-        under = lax.ppermute(cols[:2], "gx", backward(gx))
-        cols = jnp.concatenate([over, cols, under])
 
     rows_a = height - 1 if two else height - 2
     rows_b = 2 if two else 4
-    wt = pltpu.VMEM((12 * chan, 2 * chan), BF16)
+    wide = (12 * chan, 2 * chan)
     rowbuf = pltpu.VMEM((16, across + 16, chan), F32)
     cells = n_frames * across
     flops = 2 * 9 * chan * chan * cells
-    near_mem = pltpu.VMEM
-    pa, fa = call(
+    pa, fa, wt_in = call(
         functools.partial(inner_kernel, two),
-        (near_mem((rows_a, n_frames, across, chan), F32), near_mem((rows_a * across + 16, chan), BF16)),
-        [wt, rowbuf, pltpu.VMEM((height, cells, 3 * chan), BF16)],
+        (
+            near_mem((rows_a, n_frames, across, chan), F32), near_mem((rows_a * across + 16, chan), BF16),
+            near_mem(wide, BF16),
+        ),
+        [rowbuf, pltpu.VMEM((height, cells, 3 * chan), BF16)],
         flops * height, [frames, in_weight, decays],
     )
 
-    left = lax.ppermute(cols[:, 2 * n_frames :], "gy", forward(gy))
-    right = lax.ppermute(cols[:, : 2 * n_frames], "gy", backward(gy))
+    cols, fa = lax.optimization_barrier((cols, fa))
+    left, right = exchange(cols[:, : 2 * n_frames], cols[:, 2 * n_frames :], "gy", gy)
+    total = jnp.prod(decays, axis=0)[None]
+    if ta == 4:
+        ra = swapped(fa, "ta", ta, False)
+        other = jnp.sum(ra[rows_a * across :].astype(F32), axis=0, keepdims=True)
+
+        def joined(mine, theirs):
+            mine, theirs = mine.astype(F32), theirs.astype(F32)
+            return jnp.where(t == 0, theirs + other * mine, mine + total * theirs).astype(BF16)
+
+        across_two = [(0, 2), (2, 0), (1, 3), (3, 1)]
+        left, right, ga = lax.optimization_barrier((left, right, joined(fa, ra)))
+        za = lax.ppermute(ga, "ta", across_two)
+
     n_cols = (height // 2 + 1) * 4
-    pb, pc, fb = call(
+    pb, pc, fb, wt_out = call(
         functools.partial(edge_kernel, two, gx, gy),
         (
             near_mem((rows_b, n_frames, across, chan), F32),
             near_mem((2, n_cols * n_frames, chan), F32),
             near_mem((rows_b * across + 64, chan), BF16),
+            near_mem(wide, BF16),
         ),
         [
-            wt, rowbuf, pltpu.VMEM((2 * rows_b, cells, 3 * chan), BF16),
+            rowbuf, pltpu.VMEM((2 * rows_b, cells, 3 * chan), BF16),
             pltpu.VMEM((n_cols * n_frames, 12 * chan), BF16), pltpu.VMEM((2, n_cols * n_frames, chan), F32),
         ],
-        flops * rows_b, [frames, halo, cols, left, right, in_weight, decays],
+        flops * rows_b, [frames, halo, cols, left, right, wt_in, decays, out_weight],
     )
 
-    total = jnp.prod(decays, axis=0)[None]
     if ta == 4:
-        near, far = [(0, 1), (1, 0), (2, 3)], [(1, 2), (0, 3)]
-        ra = lax.ppermute(fa, "ta", near)
-        other = jnp.sum(ra[rows_a * across :].astype(F32), axis=0, keepdims=True)
-
-        def joined(mine, theirs):
-            mine, theirs = mine.astype(F32), theirs.astype(F32)
-            return jnp.where(t == 0, theirs + other * mine, mine + total * theirs).astype(BF16)
-
-        za = lax.ppermute(joined(fa, ra), "ta", far)
-        rb = lax.ppermute(fb, "ta", near)
-        zb = lax.ppermute(joined(fb, rb), "ta", far)
+        rb = swapped(fb, "ta", ta, False)
+        zb = lax.ppermute(joined(fb, rb), "ta", across_two)
     else:
         ra, rb = carry_general([fa, fb], total, ta)
         za, zb = ra, rb
@@ -366,11 +418,12 @@
         functools.partial(outer_kernel, two, ta),
         jax.ShapeDtypeStruct(frames.shape, BF16),
         [
-            wt, rowbuf, pltpu.VMEM((height + 2, cells, 3 * chan), BF16),
+            rowbuf, pltpu.VMEM((height + 2, cells, 3 * chan), BF16),
             pltpu.VMEM((n_frames, 2, (n_cols + 7) // 8 * 8, chan), F32),
             pltpu.VMEM((rows_a * across, chan), F32), pltpu.VMEM((rows_b * across + 64, chan), F32),
+            pltpu.VMEM((height // 2, n_frames, 2, across, chan), BF16), pltpu.SemaphoreType.DMA((height // 2,)),
         ],
-        flops * height, [frames, pa, pb, pc, ra, za, rb, zb, out_weight, decays],
+        flops * height, [frames, pa, pb, pc, ra, za, rb, zb, wt_out, decays], (VMEM, HBM),
     )
 
 

time: 40.1 us -> 36.5 us (0.910)
  the two profiles are of different devices: /device:TPU:19 before, /device:TPU:0 now
where the time goes in v3:
time: 36.5 us; the launch traced here: 36.3 us
  starting transfers between devices  13.2 us (36%)
  waiting for transfers between devices  9.23 us (25%)
  Pallas kernels  7.92 us (22%)
  local copies, waits for them, and re-layouts  3.39 us (9%)
  other arithmetic  2.47 us (7%)
    ppermute x6, starting transfers between devices, swapped(): return lax.ppermute(value, axis, pairs + [(b, a) for a, b in pairs])  8.39 us
    pallas_call x4, Pallas kernels, call(): pl.pallas_call(body, out_shape=outs, in_specs=[place[0]] * len(args), out...  7.92 us
    ppermute x6, waiting for transfers between devices, swapped(): return lax.ppermute(value, axis, pairs + [(b, a) for a, b in pairs])  4.9 us
    ppermute x1, waiting for transfers between devices, on_device(): za = lax.ppermute(ga, 'ta', across_two)  3.81 us
    unnamed x6, local copies, waits for them, and re-layouts  2.65 us
    ppermute x1, starting transfers between devices, on_device(): za = lax.ppermute(ga, 'ta', across_two)  2.58 us
    ppermute x1, starting transfers between devices, on_device(): zb = lax.ppermute(joined(fb, rb), 'ta', across_two)  2.22 us
    convert_element_type x2, other arithmetic, joined(): jnp.where(t == 0, theirs + other * mine, mine + total * theirs).astype(BF16)  1 us
  transfers between devices with their start and end apart: 8, of which 5 were waited for; matrix products, arithmetic and copies ran while one was open for 7% of the time, Pallas kernels for 5%

profile of v3, /device:TPU:0, one launch (start us, length us, event | category | flops | bytes accessed | tf_op | source)
XLA Modules:
  0.0 36.3 jit_solution(1190679250685650439)
XLA Ops:
  0.0 1.4 %shard_map.46 = (bf16[8,8,64,128]{3,2,1,0:T(8,128)(2,1)S(1)}, bf16[3,3,128,128]{3,2,1,0:T(8,128)(2,1)S(1)}, bf16[3,3,128,128]{3,2,1,0:T(8,128)(2,1)S(1)}, f32[8,128]{1,0:T(8,128)S(1)}, bf16[8,32,128]{2,1,0:T(8,128)(2,1)S(1)}) custom-call(bf16[8,8,64,128]{3,2,1,0:T(8,128)(2,1)} %frames_hbm.1, bf16[3,3,128,128]{3,2,1,0:T(8,128)(2,1)} %w_in_hbm.1, ...), custom_call_target="tpu_custom_call" | custom-call | bytes 4194304 | tf_op jit(solution)/shard_map/pallas_call | solution.py:286
  1.4 3.0 %collective-permute-start.1 = (bf16[2,32,128]{2,1,0:T(8,128)(2,1)S(1)}, bf16[2,32,128]{2,1,0:T(8,128)(2,1)S(1)}, u32[]{:S(2)}, u32[]{:S(2)}) collective-permute-start(bf16[2,32,128]{2,1,0:T(8,128)(2,1)S(1)} %constant_dynamic-slice_fusion), channel_id=1, source_target_pairs={{0,16},{16,0},{1,17},{17,1},{2,18},{18,2},{3,19},{19,3},{4,20},{20... | collective-permute-start | bytes 49160 | tf_op jit(solution)/shard_map/ppermute | solution.py:304
  4.4 2.0 %shard_map.47 = (f32[7,8,64,128]{3,2,1,0:T(8,128)S(1)}, bf16[464,128]{1,0:T(8,128)(2,1)S(1)}, bf16[1536,256]{1,0:T(8,128)(2,1)S(1)}) custom-call(bf16[8,8,64,128]{3,2,1,0:T(8,128)(2,1)S(1)} %get-tuple-element.22.frames_ref, bf16[3,3,128,128]{3,2,1,0:T(8,128)(2,1)S(1)} %get-tuple-element.23.w_ref, f32[8,128]{1,0:T(8,128)S(1)} %get-tuple-element.24.dec_ref), custom_call_target="tpu_custom_call" | custom-call | flops 1207959552 | bytes 4194304 | tf_op jit(solution)/shard_map/pallas_call | solution.py:286
  6.4 0.0 copy-start
  6.4 0.9 %copy-done = bf16[1536,256]{1,0:T(8,128)(2,1)} copy-done((bf16[1536,256]{1,0:T(8,128)(2,1)}, bf16[1536,256]{1,0:T(8,128)(2,1)S(1)}, u32[]{:S(2)}) %copy-start) | copy-done | bytes 786456
  7.3 0.0 copy-start.2
  7.3 0.6 %copy-done.2 = bf16[464,128]{1,0:T(8,128)(2,1)} copy-done((bf16[464,128]{1,0:T(8,128)(2,1)}, bf16[464,128]{1,0:T(8,128)(2,1)S(1)}, u32[]{:S(2)}) %copy-start.2) | copy-done | bytes 118808
  8.0 0.0 collective-permute-done.1
  8.0 0.6 %broadcast_select_fusion.3 = (bf16[10,16,128]{2,1,0:T(8,128)(2,1)}, bf16[10,16,128]{2,1,0:T(8,128)(2,1)}) fusion(pred[]{:T(512)S(6)} %eq.20, bf16[10,32,128]{2,1,0:T(8,128)(2,1)S(1)} %maximum_select_fusion.e_ref), kind=kLoop, calls=%fused_computation.16 | loop fusion | flops 40960 | bytes 163841 | tf_op jit(solution)/shard_map/jit(_where)/select_n | solution.py:317
  8.6 0.7 %collective-permute-start.3 = (bf16[10,16,128]{2,1,0:T(8,128)(2,1)}, bf16[10,16,128]{2,1,0:T(8,128)(2,1)}, u32[]{:S(2)}, u32[]{:S(2)}) collective-permute-start(bf16[10,16,128]{2,1,0:T(8,128)(2,1)} %get-tuple-element.41), channel_id=1, source_target_pairs={{4,8},{12,0},{8,4},{0,12},{5,9},{13,1},{9,5},{1,13},{6,10},{14,2},... | collective-permute-start | bytes 122888 | tf_op jit(solution)/shard_map/ppermute | solution.py:304
  9.3 1.0 %collective-permute-start.2 = (bf16[10,16,128]{2,1,0:T(8,128)(2,1)}, bf16[10,16,128]{2,1,0:T(8,128)(2,1)}, u32[]{:S(2)}, u32[]{:S(2)}) collective-permute-start(bf16[10,16,128]{2,1,0:T(8,128)(2,1)} %get-tuple-element.42), channel_id=1, source_target_pairs={{0,4},{8,12},{4,0},{12,8},{1,5},{9,13},{5,1},{13,9},{2,6},{10,14},... | collective-permute-start | bytes 122888 | tf_op jit(solution)/shard_map/ppermute | solution.py:304
  10.2 0.7 %constant_dynamic-slice_fusion.1 = bf16[8,2,64,128]{3,2,1,0:T(8,128)(2,1)} fusion(bf16[8,8,64,128]{3,2,1,0:T(8,128)(2,1)S(1)} %get-tuple-element.22.frames_ref, s32[]{:T(128)S(6)} %select_n.63), kind=kLoop, calls=%fused_computation.20 | loop fusion | bytes 524292 | tf_op jit(solution)/shard_map/dynamic_slice | solution.py:355
  11.0 0.5 %collective-permute-start = (bf16[8,2,64,128]{3,2,1,0:T(8,128)(2,1)}, bf16[8,2,64,128]{3,2,1,0:T(8,128)(2,1)S(1)}, u32[]{:S(2)}, u32[]{:S(2)}) collective-permute-start(bf16[8,2,64,128]{3,2,1,0:T(8,128)(2,1)} %constant_dynamic-slice_fusion.1), channel_id=1, source_target_pairs={{0,16},{16,0},{1,17},{17,1},{2,18},{18,2},{3,19},{19,3},{4,20},{20... | collective-permute-start | bytes 786440 | tf_op jit(solution)/shard_map/ppermute | solution.py:304
  11.5 1.6 %collective-permute-start.4 = (bf16[464,128]{1,0:T(8,128)(2,1)}, bf16[464,128]{1,0:T(8,128)(2,1)S(1)}, u32[]{:S(2)}, u32[]{:S(2)}) collective-permute-start(bf16[464,128]{1,0:T(8,128)(2,1)} %copy-done.2), channel_id=1, source_target_pairs={{0,1},{2,3},{1,0},{3,2},{4,5},{6,7},{5,4},{7,6},{8,9},{10,11},{9,8... | collective-permute-start | bytes 356360 | tf_op jit(solution)/shard_map/ppermute | solution.py:304
  13.1 0.0 collective-permute-done.3
  13.1 0.0 collective-permute-done.2
  13.1 0.8 %broadcast_select_fusion.1 = (bf16[10,16,128]{2,1,0:T(8,128)(2,1)S(1)}, bf16[10,16,128]{2,1,0:T(8,128)(2,1)S(1)}) fusion(bf16[10,16,128]{2,1,0:T(8,128)(2,1)} %collective-permute-done.2, pred[]{:T(512)S(6)} %eq.20, bf16[10,16,128]{2,1,0:T(8,128)(2,1)} %collective-permute-done.3, pred[]{:T(512)S(6)} %or.3), kind=kLoop, calls=%fused_computation.14 | loop fusion | flops 61440 | bytes 163842 | tf_op jit(solution)/shard_map/jit(_where)/select_n | solution.py:319
  13.9 2.7 %collective-permute-done.4.ra_ref = bf16[464,128]{1,0:T(8,128)(2,1)S(1)} collective-permute-done((bf16[464,128]{1,0:T(8,128)(2,1)}, bf16[464,128]{1,0:T(8,128)(2,1)S(1)}, u32[]{:S(2)}, u32[]{:S(2)}) %collective-permute-start.4) | collective-permute-done | bytes 118816 | tf_op jit(solution)/shard_map/ppermute | solution.py:304
  16.6 1.0 %fusion.1 = bf16[464,128]{1,0:T(8,128)(2,1)S(1)} fusion(bf16[464,128]{1,0:T(8,128)(2,1)S(1)} %collective-permute-done.4.ra_ref, bf16[464,128]{1,0:T(8,128)(2,1)} %copy-done.2, f32[128]{0:T(128)S(1)} %reduce_prod.9, f32[128]{0:T(128)S(1)} %convert_reduce_fusion, pred[]{:T(512)S(6)} %eq.23), kind=kLoop, calls=%fused_computation.5 | loop fusion | flops 475136 | bytes 357377 | tf_op jit(solution)/shard_map/convert_element_type | solution.py:388
  17.6 1.8 %collective-permute-done.halo_ref = bf16[8,2,64,128]{3,2,1,0:T(8,128)(2,1)S(1)} collective-permute-done((bf16[8,2,64,128]{3,2,1,0:T(8,128)(2,1)}, bf16[8,2,64,128]{3,2,1,0:T(8,128)(2,1)S(1)}, u32[]{:S(2)}, u32[]{:S(2)}) %collective-permute-start) | collective-permute-done | bytes 262176 | tf_op jit(solution)/shard_map/ppermute | solution.py:304
  19.4 0.0 copy-start.1
  19.4 1.1 %copy-done.1 = bf16[1536,256]{1,0:T(8,128)(2,1)S(1)} copy-done((bf16[1536,256]{1,0:T(8,128)(2,1)S(1)}, bf16[1536,256]{1,0:T(8,128)(2,1)}, u32[]{:S(2)}) %copy-start.1) | copy-done | bytes 786456
  20.5 1.0 %shard_map.48 = (f32[2,8,64,128]{3,2,1,0:T(8,128)S(1)}, f32[2,160,128]{2,1,0:T(8,128)S(1)}, bf16[192,128]{1,0:T(8,128)(2,1)S(1)}, bf16[1536,256]{1,0:T(8,128)(2,1)S(1)}) custom-call(bf16[8,8,64,128]{3,2,1,0:T(8,128)(2,1)S(1)} %get-tuple-element.22.frames_ref, bf16[8,2,64,128]{3,2,1,0:T(8,128)(2,1)S(1)} %collective-permute-done.halo_ref, ...), custom_call_target="tpu_custom_call" | custom-call | flops 301989888 | bytes 4194304 | tf_op jit(solution)/shard_map/pallas_call | solution.py:286
  21.5 1.6 %collective-permute-start.6 = (bf16[192,128]{1,0:T(8,128)(2,1)S(1)}, bf16[192,128]{1,0:T(8,128)(2,1)S(1)}, u32[]{:S(2)}, u32[]{:S(2)}) collective-permute-start(bf16[192,128]{1,0:T(8,128)(2,1)S(1)} %get-tuple-element.37), channel_id=1, source_target_pairs={{0,1},{2,3},{1,0},{3,2},{4,5},{6,7},{5,4},{7,6},{8,9},{10,11},{9,8... | collective-permute-start | bytes 147464 | tf_op jit(solution)/shard_map/ppermute | solution.py:304
  23.2 2.6 %collective-permute-start.5 = (bf16[464,128]{1,0:T(8,128)(2,1)S(1)}, bf16[464,128]{1,0:T(8,128)(2,1)S(1)}, u32[]{:S(2)}, u32[]{:S(2)}) collective-permute-start(bf16[464,128]{1,0:T(8,128)(2,1)S(1)} %fusion.1), channel_id=1, source_target_pairs={{0,2},{2,0},{1,3},{3,1},{4,6},{6,4},{5,7},{7,5},{8,10},{10,8},{9,1... | collective-permute-start | bytes 356360 | tf_op jit(solution)/shard_map/ppermute | solution.py:392
  25.7 0.4 %collective-permute-done.6.rb_ref = bf16[192,128]{1,0:T(8,128)(2,1)S(1)} collective-permute-done((bf16[192,128]{1,0:T(8,128)(2,1)S(1)}, bf16[192,128]{1,0:T(8,128)(2,1)S(1)}, u32[]{:S(2)}, u32[]{:S(2)}) %collective-permute-start.6) | collective-permute-done | bytes 49184 | tf_op jit(solution)/shard_map/ppermute | solution.py:304
  26.2 2.2 %collective-permute-start.7 = (bf16[192,128]{1,0:T(8,128)(2,1)S(1)}, bf16[192,128]{1,0:T(8,128)(2,1)S(1)}, u32[]{:S(2)}, u32[]{:S(2)}) collective-permute-start(bf16[192,128]{1,0:T(8,128)(2,1)S(1)} %fusion.3), channel_id=1, source_target_pairs={{0,2},{2,0},{1,3},{3,1},{4,6},{6,4},{5,7},{7,5},{8,10},{10,8},{9,1... | collective-permute-start | bytes 147464 | tf_op jit(solution)/shard_map/ppermute | solution.py:412
  28.4 3.8 %collective-permute-done.5.za_ref = bf16[464,128]{1,0:T(8,128)(2,1)S(1)} collective-permute-done((bf16[464,128]{1,0:T(8,128)(2,1)S(1)}, bf16[464,128]{1,0:T(8,128)(2,1)S(1)}, u32[]{:S(2)}, u32[]{:S(2)}) %collective-permute-start.5) | collective-permute-done | bytes 118816 | tf_op jit(solution)/shard_map/ppermute | solution.py:392
  32.2 0.5 %collective-permute-done.7.zb_ref = bf16[192,128]{1,0:T(8,128)(2,1)S(1)} collective-permute-done((bf16[192,128]{1,0:T(8,128)(2,1)S(1)}, bf16[192,128]{1,0:T(8,128)(2,1)S(1)}, u32[]{:S(2)}, u32[]{:S(2)}) %collective-permute-start.7) | collective-permute-done | bytes 49184 | tf_op jit(solution)/shard_map/ppermute | solution.py:412
  32.7 3.5 %shard_map.49 = bf16[8,8,64,128]{3,2,1,0:T(8,128)(2,1)} custom-call(bf16[8,8,64,128]{3,2,1,0:T(8,128)(2,1)S(1)} %get-tuple-element.22.frames_ref, f32[7,8,64,128]{3,2,1,0:T(8,128)S(1)} %get-tuple-element.25.pa_ref, f32[2,8,64,128]{3,2,1,0:T(8,128)S(1)} %get-tuple-element.34.pb_ref, f32[2,160,128]{2,1,0:T(8,128)S(1)} %get-tuple-element.35.pc_ref, ...), custom_call_target="tpu_custom_call" | custom-call | flops 1207959552 | bytes 4194304 | tf_op jit(solution)/shard_map/pallas_call | solution.py:286
  (5 shorter events, 0.1 us)
Async XLA Ops:
  1.4 6.5 %collective-permute-start.1 = (bf16[2,32,128]{2,1,0:T(8,128)(2,1)S(1)}, bf16[2,32,128]{2,1,0:T(8,128)(2,1)S(1)}, u32[]{:S(2)}, u32[]{:S(2)}) collective-permute-start(bf16[2,32,128]{2,1,0:T(8,128)(2,1)S(1)} %constant_dynamic-slice_fusion), channel_id=1, source_target_pairs={{0,16},{16,0},{1,17},{17,1},{2,18},{18,2},{3,19},{19,3},{4,20},{20... | collective-permute-start | bytes 49160 | tf_op jit(solution)/shard_map/ppermute | solution.py:304
  6.4 0.9 %copy-start = (bf16[1536,256]{1,0:T(8,128)(2,1)}, bf16[1536,256]{1,0:T(8,128)(2,1)S(1)}, u32[]{:S(2)}) copy-start(bf16[1536,256]{1,0:T(8,128)(2,1)S(1)} %get-tuple-element.32.wt) | copy-start | bytes 2359300
  7.3 0.6 %copy-start.2 = (bf16[464,128]{1,0:T(8,128)(2,1)}, bf16[464,128]{1,0:T(8,128)(2,1)S(1)}, u32[]{:S(2)}) copy-start(bf16[464,128]{1,0:T(8,128)(2,1)S(1)} %get-tuple-element.29) | copy-start | bytes 356356
  8.6 4.5 %collective-permute-start.3 = (bf16[10,16,128]{2,1,0:T(8,128)(2,1)}, bf16[10,16,128]{2,1,0:T(8,128)(2,1)}, u32[]{:S(2)}, u32[]{:S(2)}) collective-permute-start(bf16[10,16,128]{2,1,0:T(8,128)(2,1)} %get-tuple-element.41), channel_id=1, source_target_pairs={{4,8},{12,0},{8,4},{0,12},{5,9},{13,1},{9,5},{1,13},{6,10},{14,2},... | collective-permute-start | bytes 122888 | tf_op jit(solution)/shard_map/ppermute | solution.py:304
  9.3 3.8 %collective-permute-start.2 = (bf16[10,16,128]{2,1,0:T(8,128)(2,1)}, bf16[10,16,128]{2,1,0:T(8,128)(2,1)}, u32[]{:S(2)}, u32[]{:S(2)}) collective-permute-start(bf16[10,16,128]{2,1,0:T(8,128)(2,1)} %get-tuple-element.42), channel_id=1, source_target_pairs={{0,4},{8,12},{4,0},{12,8},{1,5},{9,13},{5,1},{13,9},{2,6},{10,14},... | collective-permute-start | bytes 122888 | tf_op jit(solution)/shard_map/ppermute | solution.py:304
  11.0 8.4 %collective-permute-start = (bf16[8,2,64,128]{3,2,1,0:T(8,128)(2,1)}, bf16[8,2,64,128]{3,2,1,0:T(8,128)(2,1)S(1)}, u32[]{:S(2)}, u32[]{:S(2)}) collective-permute-start(bf16[8,2,64,128]{3,2,1,0:T(8,128)(2,1)} %constant_dynamic-slice_fusion.1), channel_id=1, source_target_pairs={{0,16},{16,0},{1,17},{17,1},{2,18},{18,2},{3,19},{19,3},{4,20},{20... | collective-permute-start | bytes 786440 | tf_op jit(solution)/shard_map/ppermute | solution.py:304
  11.5 5.1 %collective-permute-start.4 = (bf16[464,128]{1,0:T(8,128)(2,1)}, bf16[464,128]{1,0:T(8,128)(2,1)S(1)}, u32[]{:S(2)}, u32[]{:S(2)}) collective-permute-start(bf16[464,128]{1,0:T(8,128)(2,1)} %copy-done.2), channel_id=1, source_target_pairs={{0,1},{2,3},{1,0},{3,2},{4,5},{6,7},{5,4},{7,6},{8,9},{10,11},{9,8... | collective-permute-start | bytes 356360 | tf_op jit(solution)/shard_map/ppermute | solution.py:304
  19.4 1.1 %copy-start.1 = (bf16[1536,256]{1,0:T(8,128)(2,1)S(1)}, bf16[1536,256]{1,0:T(8,128)(2,1)}, u32[]{:S(2)}) copy-start(bf16[1536,256]{1,0:T(8,128)(2,1)} %copy-done) | copy-start | bytes 2359300
  21.5 4.6 %collective-permute-start.6 = (bf16[192,128]{1,0:T(8,128)(2,1)S(1)}, bf16[192,128]{1,0:T(8,128)(2,1)S(1)}, u32[]{:S(2)}, u32[]{:S(2)}) collective-permute-start(bf16[192,128]{1,0:T(8,128)(2,1)S(1)} %get-tuple-element.37), channel_id=1, source_target_pairs={{0,1},{2,3},{1,0},{3,2},{4,5},{6,7},{5,4},{7,6},{8,9},{10,11},{9,8... | collective-permute-start | bytes 147464 | tf_op jit(solution)/shard_map/ppermute | solution.py:304
  23.2 9.0 %collective-permute-start.5 = (bf16[464,128]{1,0:T(8,128)(2,1)S(1)}, bf16[464,128]{1,0:T(8,128)(2,1)S(1)}, u32[]{:S(2)}, u32[]{:S(2)}) collective-permute-start(bf16[464,128]{1,0:T(8,128)(2,1)S(1)} %fusion.1), channel_id=1, source_target_pairs={{0,2},{2,0},{1,3},{3,1},{4,6},{6,4},{5,7},{7,5},{8,10},{10,8},{9,1... | collective-permute-start | bytes 356360 | tf_op jit(solution)/shard_map/ppermute | solution.py:392
  26.2 6.6 %collective-permute-start.7 = (bf16[192,128]{1,0:T(8,128)(2,1)S(1)}, bf16[192,128]{1,0:T(8,128)(2,1)S(1)}, u32[]{:S(2)}, u32[]{:S(2)}) collective-permute-start(bf16[192,128]{1,0:T(8,128)(2,1)S(1)} %fusion.3), channel_id=1, source_target_pairs={{0,2},{2,0},{1,3},{3,1},{4,6},{6,4},{5,7},{7,5},{8,10},{10,8},{9,1... | collective-permute-start | bytes 147464 | tf_op jit(solution)/shard_map/ppermute | solution.py:412

commit v4 on v3

--- a/solution.py
+++ b/solution.py
@@ -68,6 +68,14 @@
     return decays, jnp.sqrt(1.0 - decays * decays)
 
 
+def gather_edges(src, row, edge, at):
+    frames, across = src.shape[0], src.shape[2]
+    for f in range(frames):
+        edge[pl.ds(at + f, 2, stride=frames), :] = src[f, row, 0:16, :].astype(F32)[0:2]
+        last = src[f, row, across - 16 : across, :].astype(F32)[14:16]
+        edge[pl.ds(at + f + 2 * frames, 2, stride=frames), :] = last
+
+
 def fetch_kernel(frames_hbm, w_in_hbm, w_out_hbm, dec_hbm, frames_ref, w_in_ref, w_out_ref, dec_ref, cols_ref, edge, sems):
     pairs = [(frames_hbm, frames_ref), (dec_hbm, dec_ref), (w_in_hbm, w_in_ref), (w_out_hbm, w_out_ref)]
     copies = [pltpu.make_async_copy(src, dst, sems.at[i]) for i, (src, dst) in enumerate(pairs)]
@@ -76,11 +84,7 @@
     copies[0].wait()
     frames, height, across, chan = frames_ref.shape
     for r in range(height):
-        for f in range(frames):
-            at = r * 4 * frames + f
-            edge[pl.ds(at, 2, stride=frames), :] = frames_ref[f, r, 0:16, :].astype(F32)[0:2]
-            last = frames_ref[f, r, across - 16 : across, :].astype(F32)[14:16]
-            edge[pl.ds(at + 2 * frames, 2, stride=frames), :] = last
+        gather_edges(frames_ref, r, edge, r * 4 * frames)
     for r in range(height):
         cols_ref[r] = edge[r * 4 * frames : (r + 1) * 4 * frames, :].astype(BF16)
     for copy in copies[1:]:
@@ -127,10 +131,8 @@
     f_ref[end - 16 : end, :] = parts.astype(BF16)
 
 
-def edge_kernel(
-    two, gx, gy, frames_ref, halo_ref, e_ref, l_ref, r_ref, wt, dec_ref, w_next,
-    p_ref, pc_ref, f_ref, wt_next, rowbuf, x3, xc, yc,
-):
+def edge_kernel(two, gx, gy, frames_ref, halo_ref, wt, dec_ref, w_next, e_ref, l_ref, r_ref, *refs):
+    *corner_refs, p_ref, pc_ref, f_ref, wt_next, rowbuf, x3, xc, yc, edge = refs
     frames, height, across, chan = frames_ref.shape
     flip = mirrored(two)
     x, y_at = lax.axis_index("gx"), lax.axis_index("gy")
@@ -168,21 +170,24 @@
             f_ref[(2 * i + rr) * across : (2 * i + rr + 1) * across, :] = s.astype(BF16)
 
     n_pairs = height // 2 + 1
+    if two:
+        for i in range(2):
+            gather_edges(halo_ref, jnp.where(flip == 1, 1 - i, i), edge, i * 4 * frames)
     for p in range(n_pairs):
         for k in range(4):
             r = 2 * p - 2 + k
-            if two:
-                at = None if r < 0 else jnp.where(flip == 1, height + 1 - r, r)
-            else:
-                at = r + 2
             to = slice(p * 4 * frames, (p + 1) * 4 * frames)
             lanes = k * 3 * chan
-            if at is None:
+            if two and r < 0:
                 xc[to, lanes : lanes + 3 * chan] = jnp.zeros((4 * frames, 3 * chan), BF16)
                 continue
-            own = e_ref[at].astype(F32)
-            left = l_ref[at].astype(F32)
-            right = r_ref[at].astype(F32)
+            if two and r >= height:
+                at = jnp.where(flip == 1, 1 - (r - height), r - height)
+                own = edge[(r - height) * 4 * frames : (r - height + 1) * 4 * frames, :]
+                left, right = (ref[at].astype(F32) for ref in corner_refs)
+            else:
+                at = jnp.where(flip == 1, height - 1 - r, r) if two else r + 2
+                own, left, right = (ref[at].astype(F32) for ref in (e_ref, l_ref, r_ref))
             cols = [left[:frames], left[frames:]] + [own[c * frames : (c + 1) * frames] for c in range(4)]
             cols += [right[:frames], right[frames:]]
             for b in range(3):
@@ -298,23 +303,29 @@
     return lax.axis_index("gx") if two else 0
 
 
-def swapped(value, axis, count, odd_first):
+def swapped(value, axis, count, odd_first=False, mirror=None):
     off = 1 if odd_first else 0
     pairs = [((i + off) % count, (i + 1 + off) % count) for i in range(0, count, 2)]
-    return lax.ppermute(value, axis, pairs + [(b, a) for a, b in pairs])
-
-
-def exchange(low, high, axis, count):
-    if count % 2:
-        up = lax.ppermute(high, axis, [(i, i + 1) for i in range(count - 1)])
-        return up, lax.ppermute(low, axis, [(i + 1, i) for i in range(count - 1)])
+    pairs += [(b, a) for a, b in pairs]
+    if mirror is None:
+        return lax.ppermute(value, axis, pairs)
+    both = [(m * count + a, (1 - m) * count + b) for m in range(2) for a, b in pairs]
+    return lax.ppermute(value, (mirror, axis), both)
+
+
+def exchange(low, high, axis, count, mirror=None):
     at = lax.axis_index(axis)
     odd = at % 2 == 1
-    near = swapped(jnp.where(odd, low, high), axis, count, False)
+    if count % 2:
+        ups, downs = [(i, i + 1) for i in range(count - 1)], [(i + 1, i) for i in range(count - 1)]
+        if mirror is not None:
+            high, low = (lax.ppermute(v, mirror, [(0, 1), (1, 0)]) for v in (high, low))
+        return lax.ppermute(high, axis, ups), lax.ppermute(low, axis, downs)
+    near = swapped(jnp.where(odd, low, high), axis, count, False, mirror)
     if count == 2:
         far = jnp.zeros_like(near)
     else:
-        far = swapped(jnp.where(odd, high, low), axis, count, True)
+        far = swapped(jnp.where(odd, high, low), axis, count, True, mirror)
         far = jnp.where((at == 0) | (at == count - 1), jnp.zeros_like(far), far)
     return jnp.where(odd, near, far), jnp.where(odd, far, near)
 
@@ -349,16 +360,19 @@
         [pltpu.VMEM((height * 4 * n_frames, chan), F32), pltpu.SemaphoreType.DMA((4,))],
         0, [frames, in_weight, out_weight, decays], (HBM, VMEM),
     )
+    low, high = cols[:, : 2 * n_frames], cols[:, 2 * n_frames :]
     if two:
         start = jnp.where(x == 1, 0, height - 2)
-        corner = swapped(lax.dynamic_slice_in_dim(cols, start, 2, axis=0), "gx", 2, False)
-        halo = swapped(lax.dynamic_slice_in_dim(frames, start, 2, axis=1), "gx", 2, False)
-        cols = jnp.where(x == 1, jnp.concatenate([corner, cols]), jnp.concatenate([cols, corner]))
+        halo = lax.ppermute(lax.dynamic_slice_in_dim(frames, start, 2, axis=1), "gx", [(0, 1), (1, 0)])
+        left, right = exchange(low, high, "gy", gy)
+        facing = [lax.dynamic_slice_in_dim(v, start, 2, axis=0) for v in (low, high)]
+        sides = [cols, left, right, *exchange(*facing, "gy", gy, "gx")]
     else:
+        above, below = exchange(frames[:, :2], frames[:, height - 2 :], "gx", gx)
+        halo = jnp.concatenate([above, below], axis=1)
         over, under = exchange(cols[:2], cols[height - 2 :], "gx", gx)
         cols = jnp.concatenate([over, cols, under])
-        above, below = exchange(frames[:, :2], frames[:, height - 2 :], "gx", gx)
-        halo = jnp.concatenate([above, below], axis=1)
+        sides = [cols, *exchange(cols[:, : 2 * n_frames], cols[:, 2 * n_frames :], "gy", gy)]
 
     rows_a = height - 1 if two else height - 2
     rows_b = 2 if two else 4
@@ -376,8 +390,6 @@
         flops * height, [frames, in_weight, decays],
     )
 
-    cols, fa = lax.optimization_barrier((cols, fa))
-    left, right = exchange(cols[:, : 2 * n_frames], cols[:, 2 * n_frames :], "gy", gy)
     total = jnp.prod(decays, axis=0)[None]
     if ta == 4:
         ra = swapped(fa, "ta", ta, False)
@@ -388,8 +400,7 @@
             return jnp.where(t == 0, theirs + other * mine, mine + total * theirs).astype(BF16)
 
         across_two = [(0, 2), (2, 0), (1, 3), (3, 1)]
-        left, right, ga = lax.optimization_barrier((left, right, joined(fa, ra)))
-        za = lax.ppermute(ga, "ta", across_two)
+        za = lax.ppermute(joined(fa, ra), "ta", across_two)
 
     n_cols = (height // 2 + 1) * 4
     pb, pc, fb, wt_out = call(
@@ -403,8 +414,9 @@
         [
             rowbuf, pltpu.VMEM((2 * rows_b, cells, 3 * chan), BF16),
             pltpu.VMEM((n_cols * n_frames, 12 * chan), BF16), pltpu.VMEM((2, n_cols * n_frames, chan), F32),
+            pltpu.VMEM((8 * n_frames, chan), F32),
         ],
-        flops * rows_b, [frames, halo, cols, left, right, wt_in, decays, out_weight],
+        flops * rows_b, [frames, halo, wt_in, decays, out_weight, *sides],
     )
 
     if ta == 4:

time: 36.5 us -> 35.5 us (0.973)
  waiting for transfers between devices: 9.23 us -> 5.99 us
  starting transfers between devices: 13.2 us -> 14.7 us
  local copies, waits for them, and re-layouts: 3.39 us -> 4.34 us
    ppermute x7 -> x8, waiting for transfers between devices: 8.71 us -> 5.47 us  [the longest x1 2.76 us: on_device(): za = lax.ppermute(joined(fa, ra), 'ta', across_two)]
    ppermute x7 -> x8, starting transfers between devices: 11 us -> 12.2 us  [the longest x2 4.15 us: swapped(): return lax.ppermute(value, (mirror, axis), both)]
    unnamed x6 -> x12, local copies, waits for them, and re-layouts: 2.65 us -> 3.62 us
    convert_element_type x2, other arithmetic: 1 us -> 0.1 us  [joined(): jnp.where(t == 0, theirs + other * mine, mine + total * theirs).astype(BF16)]
    slice x0 -> x1, other arithmetic: none -> 0.68 us  [on_device(): low, high = (cols[:, :2 * n_frames], cols[:, 2 * n_frames:])]
    select_n x1 -> x2, other arithmetic: 0.79 us -> 0.78 us  [exchange(): return (jnp.where(odd, near, far), jnp.where(odd, far, near))]
  transfers between devices with their start and end apart: 8 -> 9, of which waited for: 5 -> 3; matrix products, arithmetic and copies ran while one was open for 7% -> 5% of each run, Pallas kernels for 5% -> 6%
where the time goes in v4:
time: 35.5 us; the launch traced here: 35.3 us
  starting transfers between devices  14.7 us (41%)
  Pallas kernels  7.94 us (22%)
  waiting for transfers between devices  5.99 us (17%)
  local copies, waits for them, and re-layouts  4.34 us (12%)
  other arithmetic  2.2 us (6%)
    pallas_call x4, Pallas kernels, call(): pl.pallas_call(body, out_shape=outs, in_specs=[place[0]] * len(args), out...  7.94 us
    ppermute x2, starting transfers between devices, swapped(): return lax.ppermute(value, (mirror, axis), both)  4.15 us
    unnamed x12, local copies, waits for them, and re-layouts  3.62 us
    ppermute x4, starting transfers between devices, swapped(): return lax.ppermute(value, axis, pairs)  3.32 us
    ppermute x1, waiting for transfers between devices, on_device(): za = lax.ppermute(joined(fa, ra), 'ta', across_two)  2.76 us
    ppermute x4, waiting for transfers between devices, swapped(): return lax.ppermute(value, axis, pairs)  2.7 us
    ppermute x1, starting transfers between devices, on_device(): za = lax.ppermute(joined(fa, ra), 'ta', across_two)  2.65 us
    ppermute x1, starting transfers between devices, on_device(): zb = lax.ppermute(joined(fb, rb), 'ta', across_two)  2.51 us
  transfers between devices with their start and end apart: 9, of which 3 were waited for; matrix products, arithmetic and copies ran while one was open for 5% of the time, Pallas kernels for 6%

profile of v4, /device:TPU:0, one launch (start us, length us, event | category | flops | bytes accessed | tf_op | source)
XLA Modules:
  0.0 35.3 jit_solution(12552230369994715308)
XLA Ops:
  0.0 1.4 %shard_map.46 = (bf16[8,8,64,128]{3,2,1,0:T(8,128)(2,1)S(1)}, bf16[3,3,128,128]{3,2,1,0:T(8,128)(2,1)S(1)}, bf16[3,3,128,128]{3,2,1,0:T(8,128)(2,1)S(1)}, f32[8,128]{1,0:T(8,128)S(1)}, bf16[8,32,128]{2,1,0:T(8,128)(2,1)S(1)}) custom-call(bf16[8,8,64,128]{3,2,1,0:T(8,128)(2,1)} %frames_hbm.1, bf16[3,3,128,128]{3,2,1,0:T(8,128)(2,1)} %w_in_hbm.1, ...), custom_call_target="tpu_custom_call" | custom-call | bytes 4194304 | tf_op jit(solution)/shard_map/pallas_call | solution.py:291
  1.4 0.0 copy-start.4
  1.4 0.7 %fusion.4 = (bf16[8,16,128]{2,1,0:T(8,128)(2,1)S(1)}, bf16[8,16,128]{2,1,0:T(8,128)(2,1)}, bf16[8,16,128]{2,1,0:T(8,128)(2,1)S(1)}, bf16[8,16,128]{2,1,0:T(8,128)(2,1)S(1)}) fusion(bf16[8,32,128]{2,1,0:T(8,128)(2,1)S(1)} %get-tuple-element.23.e_ref, pred[]{:T(512)S(6)} %eq.23), kind=kLoop, calls=%fused_computation.24 | loop fusion | flops 32768 | bytes 196609 | tf_op jit(solution)/shard_map/slice | solution.py:363
  2.1 0.6 %broadcast_select_fusion.8 = (bf16[2,16,128]{2,1,0:T(8,128)(2,1)}, bf16[2,16,128]{2,1,0:T(8,128)(2,1)}) fusion(pred[]{:T(512)S(6)} %eq.23, bf16[8,16,128]{2,1,0:T(8,128)(2,1)S(1)} %get-tuple-element.34, s32[]{:T(128)S(6)} %select_n.84, bf16[8,16,128]{2,1,0:T(8,128)(2,1)S(1)} %get-tuple-element.31), kind=kLoop, calls=%fused_computation.21 | loop fusion | flops 8192 | bytes 32773 | tf_op jit(solution)/shard_map/jit(_where)/select_n | solution.py:328
  2.7 2.4 %collective-permute-start.3 = (bf16[2,16,128]{2,1,0:T(8,128)(2,1)}, bf16[2,16,128]{2,1,0:T(8,128)(2,1)S(1)}, u32[]{:S(2)}, u32[]{:S(2)}) collective-permute-start(bf16[2,16,128]{2,1,0:T(8,128)(2,1)} %get-tuple-element.30), channel_id=1, source_target_pairs={{0,20},{8,28},{4,16},{12,24},{16,4},{24,12},{20,0},{28,8},{1,21},{... | collective-permute-start | bytes 24584 | tf_op jit(solution)/shard_map/ppermute | solution.py:313
  5.1 1.8 %collective-permute-start.4 = (bf16[2,16,128]{2,1,0:T(8,128)(2,1)}, bf16[2,16,128]{2,1,0:T(8,128)(2,1)}, u32[]{:S(2)}, u32[]{:S(2)}) collective-permute-start(bf16[2,16,128]{2,1,0:T(8,128)(2,1)} %get-tuple-element.29), channel_id=1, source_target_pairs={{4,24},{12,16},{8,20},{0,28},{20,8},{28,0},{24,4},{16,12},{5,25},{... | collective-permute-start | bytes 24584 | tf_op jit(solution)/shard_map/ppermute | solution.py:313
  6.9 0.0 collective-permute-start.1
  6.9 0.0 collective-permute-start.2
  6.9 0.7 %constant_dynamic-slice_fusion = bf16[8,2,64,128]{3,2,1,0:T(8,128)(2,1)} fusion(bf16[8,8,64,128]{3,2,1,0:T(8,128)(2,1)S(1)} %get-tuple-element.17.frames_ref, s32[]{:T(128)S(6)} %select_n.84), kind=kLoop, calls=%fused_computation.23 | loop fusion | bytes 524292 | tf_op jit(solution)/shard_map/dynamic_slice | solution.py:366
  7.6 2.1 %collective-permute-start = (bf16[8,2,64,128]{3,2,1,0:T(8,128)(2,1)}, bf16[8,2,64,128]{3,2,1,0:T(8,128)(2,1)S(1)}, u32[]{:S(2)}, u32[]{:S(2)}) collective-permute-start(bf16[8,2,64,128]{3,2,1,0:T(8,128)(2,1)} %constant_dynamic-slice_fusion), channel_id=1, source_target_pairs={{0,16},{16,0},{1,17},{17,1},{2,18},{18,2},{3,19},{19,3},{4,20},{20... | collective-permute-start | bytes 786440 | tf_op jit(solution)/shard_map/ppermute | solution.py:366
  9.7 0.0 copy-done.4
  9.7 0.0 copy-start.5
  9.7 1.0 %copy-done.5 = bf16[3,3,128,128]{3,2,1,0:T(8,128)(2,1)S(1)} copy-done((bf16[3,3,128,128]{3,2,1,0:T(8,128)(2,1)S(1)}, bf16[3,3,128,128]{3,2,1,0:T(8,128)(2,1)}, u32[]{:S(2)}) %copy-start.5) | copy-done | bytes 294936
  10.7 2.0 %shard_map.47 = (f32[7,8,64,128]{3,2,1,0:T(8,128)S(1)}, bf16[464,128]{1,0:T(8,128)(2,1)S(1)}, bf16[1536,256]{1,0:T(8,128)(2,1)S(1)}) custom-call(bf16[8,8,64,128]{3,2,1,0:T(8,128)(2,1)S(1)} %get-tuple-element.17.frames_ref, bf16[3,3,128,128]{3,2,1,0:T(8,128)(2,1)S(1)} %copy-done.5, f32[8,128]{1,0:T(8,128)S(1)} %get-tuple-element.19.dec_ref), custom_call_target="tpu_custom_call" | custom-call | flops 1207959552 | bytes 4194304 | tf_op jit(solution)/shard_map/pallas_call | solution.py:291
  12.7 0.0 copy-start
  12.7 0.9 %copy-done = bf16[1536,256]{1,0:T(8,128)(2,1)} copy-done((bf16[1536,256]{1,0:T(8,128)(2,1)}, bf16[1536,256]{1,0:T(8,128)(2,1)S(1)}, u32[]{:S(2)}) %copy-start) | copy-done | bytes 786456
  13.5 0.0 copy-start.2
  13.5 0.6 %copy-done.2 = bf16[464,128]{1,0:T(8,128)(2,1)} copy-done((bf16[464,128]{1,0:T(8,128)(2,1)}, bf16[464,128]{1,0:T(8,128)(2,1)S(1)}, u32[]{:S(2)}) %copy-start.2) | copy-done | bytes 118808
  14.2 0.0 copy-start.3
  14.2 0.0 collective-permute-done.3
  14.2 1.6 %collective-permute-start.5 = (bf16[464,128]{1,0:T(8,128)(2,1)}, bf16[464,128]{1,0:T(8,128)(2,1)S(1)}, u32[]{:S(2)}, u32[]{:S(2)}) collective-permute-start(bf16[464,128]{1,0:T(8,128)(2,1)} %copy-done.2), channel_id=1, source_target_pairs={{0,1},{2,3},{1,0},{3,2},{4,5},{6,7},{5,4},{7,6},{8,9},{10,11},{9,8... | collective-permute-start | bytes 356360 | tf_op jit(solution)/shard_map/ppermute | solution.py:311
  15.8 0.0 collective-permute-done.4
  15.9 0.0 collective-permute-done.1
  15.9 0.0 collective-permute-done.2
  15.9 0.8 %broadcast_select_fusion.1 = (bf16[8,16,128]{2,1,0:T(8,128)(2,1)S(1)}, bf16[8,16,128]{2,1,0:T(8,128)(2,1)S(1)}) fusion(bf16[8,16,128]{2,1,0:T(8,128)(2,1)} %collective-permute-done.1, pred[]{:T(512)S(6)} %eq.23, bf16[8,16,128]{2,1,0:T(8,128)(2,1)} %collective-permute-done.2, pred[]{:T(512)S(6)} %or.4), kind=kLoop, calls=%fused_computation.13 | loop fusion | flops 49152 | bytes 131074 | tf_op jit(solution)/shard_map/jit(_where)/select_n | solution.py:330
  16.7 2.7 %collective-permute-done.5.ra_ref = bf16[464,128]{1,0:T(8,128)(2,1)S(1)} collective-permute-done((bf16[464,128]{1,0:T(8,128)(2,1)}, bf16[464,128]{1,0:T(8,128)(2,1)S(1)}, u32[]{:S(2)}, u32[]{:S(2)}) %collective-permute-start.5) | collective-permute-done | bytes 118816 | tf_op jit(solution)/shard_map/ppermute | solution.py:311
  19.4 0.0 collective-permute-done.halo_ref
  19.4 0.0 copy-start.1
  19.4 1.1 %copy-done.1 = bf16[1536,256]{1,0:T(8,128)(2,1)S(1)} copy-done((bf16[1536,256]{1,0:T(8,128)(2,1)S(1)}, bf16[1536,256]{1,0:T(8,128)(2,1)}, u32[]{:S(2)}) %copy-start.1) | copy-done | bytes 786456
  20.5 1.0 %shard_map.48 = (f32[2,8,64,128]{3,2,1,0:T(8,128)S(1)}, f32[2,160,128]{2,1,0:T(8,128)S(1)}, bf16[192,128]{1,0:T(8,128)(2,1)S(1)}, bf16[1536,256]{1,0:T(8,128)(2,1)S(1)}) custom-call(bf16[8,8,64,128]{3,2,1,0:T(8,128)(2,1)S(1)} %get-tuple-element.17.frames_ref, bf16[8,2,64,128]{3,2,1,0:T(8,128)(2,1)S(1)} %collective-permute-done.halo_ref, ...), custom_call_target="tpu_custom_call" | custom-call | flops 301989888 | bytes 4194304 | tf_op jit(solution)/shard_map/pallas_call | solution.py:291
  21.5 1.6 %collective-permute-start.7 = (bf16[192,128]{1,0:T(8,128)(2,1)S(1)}, bf16[192,128]{1,0:T(8,128)(2,1)S(1)}, u32[]{:S(2)}, u32[]{:S(2)}) collective-permute-start(bf16[192,128]{1,0:T(8,128)(2,1)S(1)} %get-tuple-element.27), channel_id=1, source_target_pairs={{0,1},{2,3},{1,0},{3,2},{4,5},{6,7},{5,4},{7,6},{8,9},{10,11},{9,8... | collective-permute-start | bytes 147464 | tf_op jit(solution)/shard_map/ppermute | solution.py:311
  23.1 0.0 copy-done.3
  23.2 0.1 fusion.1
  23.2 2.7 %collective-permute-start.6 = (bf16[464,128]{1,0:T(8,128)(2,1)S(1)}, bf16[464,128]{1,0:T(8,128)(2,1)S(1)}, u32[]{:S(2)}, u32[]{:S(2)}) collective-permute-start(bf16[464,128]{1,0:T(8,128)(2,1)S(1)} %fusion.1), channel_id=1, source_target_pairs={{0,2},{2,0},{1,3},{3,1},{4,6},{6,4},{5,7},{7,5},{8,10},{10,8},{9,1... | collective-permute-start | bytes 356360 | tf_op jit(solution)/shard_map/ppermute | solution.py:403
  25.9 0.0 collective-permute-done.7.rb_ref
  25.9 2.5 %collective-permute-start.8 = (bf16[192,128]{1,0:T(8,128)(2,1)S(1)}, bf16[192,128]{1,0:T(8,128)(2,1)S(1)}, u32[]{:S(2)}, u32[]{:S(2)}) collective-permute-start(bf16[192,128]{1,0:T(8,128)(2,1)S(1)} %fusion.3), channel_id=1, source_target_pairs={{0,2},{2,0},{1,3},{3,1},{4,6},{6,4},{5,7},{7,5},{8,10},{10,8},{9,1... | collective-permute-start | bytes 147464 | tf_op jit(solution)/shard_map/ppermute | solution.py:424
  28.4 2.8 %collective-permute-done.6.za_ref = bf16[464,128]{1,0:T(8,128)(2,1)S(1)} collective-permute-done((bf16[464,128]{1,0:T(8,128)(2,1)S(1)}, bf16[464,128]{1,0:T(8,128)(2,1)S(1)}, u32[]{:S(2)}, u32[]{:S(2)}) %collective-permute-start.6) | collective-permute-done | bytes 118816 | tf_op jit(solution)/shard_map/ppermute | solution.py:403
  31.2 0.5 %collective-permute-done.8.zb_ref = bf16[192,128]{1,0:T(8,128)(2,1)S(1)} collective-permute-done((bf16[192,128]{1,0:T(8,128)(2,1)S(1)}, bf16[192,128]{1,0:T(8,128)(2,1)S(1)}, u32[]{:S(2)}, u32[]{:S(2)}) %collective-permute-start.8) | collective-permute-done | bytes 49184 | tf_op jit(solution)/shard_map/ppermute | solution.py:424
  31.7 3.6 %shard_map.49 = bf16[8,8,64,128]{3,2,1,0:T(8,128)(2,1)} custom-call(bf16[8,8,64,128]{3,2,1,0:T(8,128)(2,1)S(1)} %get-tuple-element.17.frames_ref, f32[7,8,64,128]{3,2,1,0:T(8,128)S(1)} %get-tuple-element.20.pa_ref, f32[2,8,64,128]{3,2,1,0:T(8,128)S(1)} %get-tuple-element.24.pb_ref, f32[2,160,128]{2,1,0:T(8,128)S(1)} %get-tuple-element.25.pc_ref, ...), custom_call_target="tpu_custom_call" | custom-call | flops 1207959552 | bytes 4194304 | tf_op jit(solution)/shard_map/pallas_call | solution.py:291
  (4 shorter events, 0.1 us)
Async XLA Ops:
  1.4 8.3 %copy-start.4 = (bf16[3,3,128,128]{3,2,1,0:T(8,128)(2,1)}, bf16[3,3,128,128]{3,2,1,0:T(8,128)(2,1)S(1)}, u32[]{:S(2)}) copy-start(bf16[3,3,128,128]{3,2,1,0:T(8,128)(2,1)S(1)} %get-tuple-element.18.w_ref) | copy-start | bytes 884740
  2.7 11.5 %collective-permute-start.3 = (bf16[2,16,128]{2,1,0:T(8,128)(2,1)}, bf16[2,16,128]{2,1,0:T(8,128)(2,1)S(1)}, u32[]{:S(2)}, u32[]{:S(2)}) collective-permute-start(bf16[2,16,128]{2,1,0:T(8,128)(2,1)} %get-tuple-element.30), channel_id=1, source_target_pairs={{0,20},{8,28},{4,16},{12,24},{16,4},{24,12},{20,0},{28,8},{1,21},{... | collective-permute-start | bytes 24584 | tf_op jit(solution)/shard_map/ppermute | solution.py:313
  5.1 10.8 %collective-permute-start.4 = (bf16[2,16,128]{2,1,0:T(8,128)(2,1)}, bf16[2,16,128]{2,1,0:T(8,128)(2,1)}, u32[]{:S(2)}, u32[]{:S(2)}) collective-permute-start(bf16[2,16,128]{2,1,0:T(8,128)(2,1)} %get-tuple-element.29), channel_id=1, source_target_pairs={{4,24},{12,16},{8,20},{0,28},{20,8},{28,0},{24,4},{16,12},{5,25},{... | collective-permute-start | bytes 24584 | tf_op jit(solution)/shard_map/ppermute | solution.py:313
  6.9 9.0 %collective-permute-start.1 = (bf16[8,16,128]{2,1,0:T(8,128)(2,1)}, bf16[8,16,128]{2,1,0:T(8,128)(2,1)}, u32[]{:S(2)}, u32[]{:S(2)}) collective-permute-start(bf16[8,16,128]{2,1,0:T(8,128)(2,1)} %get-tuple-element.32), channel_id=1, source_target_pairs={{0,4},{8,12},{4,0},{12,8},{1,5},{9,13},{5,1},{13,9},{2,6},{10,14},... | collective-permute-start | bytes 98312 | tf_op jit(solution)/shard_map/ppermute | solution.py:311
  6.9 9.0 %collective-permute-start.2 = (bf16[8,16,128]{2,1,0:T(8,128)(2,1)S(1)}, bf16[8,16,128]{2,1,0:T(8,128)(2,1)}, u32[]{:S(2)}, u32[]{:S(2)}) collective-permute-start(bf16[8,16,128]{2,1,0:T(8,128)(2,1)S(1)} %get-tuple-element.33), channel_id=1, source_target_pairs={{4,8},{12,0},{8,4},{0,12},{5,9},{13,1},{9,5},{1,13},{6,10},{14,2},... | collective-permute-start | bytes 98312 | tf_op jit(solution)/shard_map/ppermute | solution.py:311
  7.6 11.7 %collective-permute-start = (bf16[8,2,64,128]{3,2,1,0:T(8,128)(2,1)}, bf16[8,2,64,128]{3,2,1,0:T(8,128)(2,1)S(1)}, u32[]{:S(2)}, u32[]{:S(2)}) collective-permute-start(bf16[8,2,64,128]{3,2,1,0:T(8,128)(2,1)} %constant_dynamic-slice_fusion), channel_id=1, source_target_pairs={{0,16},{16,0},{1,17},{17,1},{2,18},{18,2},{3,19},{19,3},{4,20},{20... | collective-permute-start | bytes 786440 | tf_op jit(solution)/shard_map/ppermute | solution.py:366
  9.7 1.0 %copy-start.5 = (bf16[3,3,128,128]{3,2,1,0:T(8,128)(2,1)S(1)}, bf16[3,3,128,128]{3,2,1,0:T(8,128)(2,1)}, u32[]{:S(2)}) copy-start(bf16[3,3,128,128]{3,2,1,0:T(8,128)(2,1)} %copy-done.4) | copy-start | bytes 884740
  12.7 0.9 %copy-start = (bf16[1536,256]{1,0:T(8,128)(2,1)}, bf16[1536,256]{1,0:T(8,128)(2,1)S(1)}, u32[]{:S(2)}) copy-start(bf16[1536,256]{1,0:T(8,128)(2,1)S(1)} %get-tuple-element.21.wt) | copy-start | bytes 2359300
  13.5 0.6 %copy-start.2 = (bf16[464,128]{1,0:T(8,128)(2,1)}, bf16[464,128]{1,0:T(8,128)(2,1)S(1)}, u32[]{:S(2)}) copy-start(bf16[464,128]{1,0:T(8,128)(2,1)S(1)} %get-tuple-element.26) | copy-start | bytes 356356
  14.2 8.9 %copy-start.3 = (bf16[464,128]{1,0:T(8,128)(2,1)S(1)}, bf16[464,128]{1,0:T(8,128)(2,1)}, u32[]{:S(2)}) copy-start(bf16[464,128]{1,0:T(8,128)(2,1)} %copy-done.2) | copy-start | bytes 356356
  14.2 5.1 %collective-permute-start.5 = (bf16[464,128]{1,0:T(8,128)(2,1)}, bf16[464,128]{1,0:T(8,128)(2,1)S(1)}, u32[]{:S(2)}, u32[]{:S(2)}) collective-permute-start(bf16[464,128]{1,0:T(8,128)(2,1)} %copy-done.2), channel_id=1, source_target_pairs={{0,1},{2,3},{1,0},{3,2},{4,5},{6,7},{5,4},{7,6},{8,9},{10,11},{9,8... | collective-permute-start | bytes 356360 | tf_op jit(solution)/shard_map/ppermute | solution.py:311
  19.4 1.1 %copy-start.1 = (bf16[1536,256]{1,0:T(8,128)(2,1)S(1)}, bf16[1536,256]{1,0:T(8,128)(2,1)}, u32[]{:S(2)}) copy-start(bf16[1536,256]{1,0:T(8,128)(2,1)} %copy-done) | copy-start | bytes 2359300
  21.5 4.4 %collective-permute-start.7 = (bf16[192,128]{1,0:T(8,128)(2,1)S(1)}, bf16[192,128]{1,0:T(8,128)(2,1)S(1)}, u32[]{:S(2)}, u32[]{:S(2)}) collective-permute-start(bf16[192,128]{1,0:T(8,128)(2,1)S(1)} %get-tuple-element.27), channel_id=1, source_target_pairs={{0,1},{2,3},{1,0},{3,2},{4,5},{6,7},{5,4},{7,6},{8,9},{10,11},{9,8... | collective-permute-start | bytes 147464 | tf_op jit(solution)/shard_map/ppermute | solution.py:311
  23.2 8.0 %collective-permute-start.6 = (bf16[464,128]{1,0:T(8,128)(2,1)S(1)}, bf16[464,128]{1,0:T(8,128)(2,1)S(1)}, u32[]{:S(2)}, u32[]{:S(2)}) collective-permute-start(bf16[464,128]{1,0:T(8,128)(2,1)S(1)} %fusion.1), channel_id=1, source_target_pairs={{0,2},{2,0},{1,3},{3,1},{4,6},{6,4},{5,7},{7,5},{8,10},{10,8},{9,1... | collective-permute-start | bytes 356360 | tf_op jit(solution)/shard_map/ppermute | solution.py:403
  25.9 5.8 %collective-permute-start.8 = (bf16[192,128]{1,0:T(8,128)(2,1)S(1)}, bf16[192,128]{1,0:T(8,128)(2,1)S(1)}, u32[]{:S(2)}, u32[]{:S(2)}) collective-permute-start(bf16[192,128]{1,0:T(8,128)(2,1)S(1)} %fusion.3), channel_id=1, source_target_pairs={{0,2},{2,0},{1,3},{3,1},{4,6},{6,4},{5,7},{7,5},{8,10},{10,8},{9,1... | collective-permute-start | bytes 147464 | tf_op jit(solution)/shard_map/ppermute | solution.py:424

commit v5 on v4

--- a/solution.py
+++ b/solution.py
@@ -76,8 +76,9 @@
         edge[pl.ds(at + f + 2 * frames, 2, stride=frames), :] = last
 
 
-def fetch_kernel(frames_hbm, w_in_hbm, w_out_hbm, dec_hbm, frames_ref, w_in_ref, w_out_ref, dec_ref, cols_ref, edge, sems):
-    pairs = [(frames_hbm, frames_ref), (dec_hbm, dec_ref), (w_in_hbm, w_in_ref), (w_out_hbm, w_out_ref)]
+def fetch_kernel(two, frames_hbm, dec_hbm, w_hbm, frames_ref, dec_ref, w_ref, cols_ref, *refs):
+    *sent, edge, sems = refs
+    pairs = [(frames_hbm, frames_ref), (dec_hbm, dec_ref), (w_hbm, w_ref)]
     copies = [pltpu.make_async_copy(src, dst, sems.at[i]) for i, (src, dst) in enumerate(pairs)]
     for copy in copies:
         copy.start()
@@ -87,11 +88,23 @@
         gather_edges(frames_ref, r, edge, r * 4 * frames)
     for r in range(height):
         cols_ref[r] = edge[r * 4 * frames : (r + 1) * 4 * frames, :].astype(BF16)
+    if two:
+        halo_ref, near_ref, far_ref, near_corner, far_corner = sent
+        odd = lax.axis_index("gy") % 2 == 1
+        start = jnp.where(lax.axis_index("gx") == 1, 0, height - 2)
+        halo_ref[...] = frames_ref[:, pl.ds(start, 2)]
+        half = 2 * frames
+        for refs, rows in (((near_ref, far_ref), range(height)), ((near_corner, far_corner), (start, start + 1))):
+            for i, r in enumerate(rows):
+                at = pl.multiple_of(r * 2 * half, 2 * half)
+                low, high = edge[pl.ds(at, half), :], edge[pl.ds(at + half, half), :]
+                refs[0][i] = jnp.where(odd, low, high).astype(BF16)
+                refs[1][i] = jnp.where(odd, high, low).astype(BF16)
     for copy in copies[1:]:
         copy.wait()
 
 
-def inner_kernel(two, frames_ref, w_ref, dec_ref, p_ref, f_ref, wt, rowbuf, x3):
+def inner_kernel(two, frames_ref, dec_ref, w_ref, p_ref, f_ref, wt, rowbuf, x3):
     frames, height, across, chan = frames_ref.shape
     flip = mirrored(two)
     pair_weights(w_ref, wt, flip)
@@ -131,14 +144,17 @@
     f_ref[end - 16 : end, :] = parts.astype(BF16)
 
 
-def edge_kernel(two, gx, gy, frames_ref, halo_ref, wt, dec_ref, w_next, e_ref, l_ref, r_ref, *refs):
-    *corner_refs, p_ref, pc_ref, f_ref, wt_next, rowbuf, x3, xc, yc, edge = refs
-    frames, height, across, chan = frames_ref.shape
+def edge_kernel(two, gx, gy, own_ref, dec_ref, w_ref, halo_ref, e_ref, *refs):
+    *sides, next_hbm, p_ref, pc_ref, f_ref, next_ref, wt, rowbuf, x3, xc, yc, edge, sem = refs
+    fetch = pltpu.make_async_copy(next_hbm, next_ref, sem)
+    fetch.start()
+    frames, across, chan = own_ref.shape[0], *own_ref.shape[2:]
+    height = e_ref.shape[0] if two else own_ref.shape[1]
     flip = mirrored(two)
     x, y_at = lax.axis_index("gx"), lax.axis_index("gy")
     has_left, has_right = (y_at > 0).astype(F32), (y_at < gy - 1).astype(F32)
     has_above, has_below = (x > 0).astype(F32), (x < gx - 1).astype(F32)
-    pair_weights(w_next, wt_next, flip)
+    pair_weights(w_ref, wt, flip)
     clear_margins(rowbuf)
     decays, scales = load_decays(dec_ref)
     pairs = [height // 2] if two else [0, height // 2]
@@ -147,27 +163,24 @@
             r = 2 * p - 2 + k
             for f in range(frames):
                 slot = (k * frames + f) % rowbuf.shape[0]
-                if 0 <= r < height:
-                    x = frames_ref[f, jnp.where(flip == 1, height - 1 - r, r)]
+                if two and r < height:
+                    x = own_ref[f, jnp.where(flip == 1, height - 1 - r, r - height + 2)]
+                elif 0 <= r < height:
+                    x = own_ref[f, r]
                 elif two:
                     x = halo_ref[f, jnp.where(flip == 1, 1 - (r - height), r - height)]
                 else:
                     x = halo_ref[f, r + 2 if r < 0 else r - height + 2]
                 rowbuf[slot, 8 : 8 + across, :] = x.astype(F32)
                 three_taps(rowbuf, slot, x3, i * 4 + k, f, x)
-        y = pair_dot(x3, [i * 4 + k for k in range(4)], wt)
-        inside = 1.0
+    odd = y_at % 2 == 1
+
+    def beside(at, first, second):
+        first, second = first[at].astype(F32), second[at].astype(F32)
         if not two:
-            inside = has_above if p == 0 else has_below
-
-        def keep(rr, f, s, i=i, p=p, inside=inside):
-            border = (rr == 0) if p == 0 else (rr == 1)
-            p_ref[2 * i + rr, f] = s * inside if border and not two else s
-
-        for rr, s in enumerate(scan_rows(y, decays, scales, across, keep)):
-            border = (rr == 0) if p == 0 else (rr == 1)
-            s = s * inside if border and not two else s
-            f_ref[(2 * i + rr) * across : (2 * i + rr + 1) * across, :] = s.astype(BF16)
+            return first, second
+        second = jnp.where((y_at == 0) | (y_at == gy - 1), 0.0, second)
+        return jnp.where(odd, first, second), jnp.where(odd, second, first)
 
     n_pairs = height // 2 + 1
     if two:
@@ -184,18 +197,34 @@
             if two and r >= height:
                 at = jnp.where(flip == 1, 1 - (r - height), r - height)
                 own = edge[(r - height) * 4 * frames : (r - height + 1) * 4 * frames, :]
-                left, right = (ref[at].astype(F32) for ref in corner_refs)
+                left, right = beside(at, *sides[2:])
             else:
                 at = jnp.where(flip == 1, height - 1 - r, r) if two else r + 2
-                own, left, right = (ref[at].astype(F32) for ref in (e_ref, l_ref, r_ref))
+                own = e_ref[at].astype(F32)
+                left, right = beside(at, *sides[:2])
             cols = [left[:frames], left[frames:]] + [own[c * frames : (c + 1) * frames] for c in range(4)]
             cols += [right[:frames], right[frames:]]
             for b in range(3):
                 piece = jnp.concatenate([cols[c + b] for c in (0, 1, 4, 5)], axis=0)
                 xc[to, lanes + b * chan : lanes + (b + 1) * chan] = piece.astype(BF16)
-    edge = jnp.dot(xc[...], wt[...], preferred_element_type=F32)
+    for i, p in enumerate(pairs):
+        y = pair_dot(x3, [i * 4 + k for k in range(4)], wt)
+        inside = 1.0
+        if not two:
+            inside = has_above if p == 0 else has_below
+
+        def keep(rr, f, s, i=i, p=p, inside=inside):
+            border = (rr == 0) if p == 0 else (rr == 1)
+            p_ref[2 * i + rr, f] = s * inside if border and not two else s
+
+        for rr, s in enumerate(scan_rows(y, decays, scales, across, keep)):
+            border = (rr == 0) if p == 0 else (rr == 1)
+            s = s * inside if border and not two else s
+            f_ref[(2 * i + rr) * across : (2 * i + rr + 1) * across, :] = s.astype(BF16)
+
+    wide = jnp.dot(xc[...], wt[...], preferred_element_type=F32)
     for h in range(2):
-        yc[h] = edge[:, h * chan : (h + 1) * chan]
+        yc[h] = wide[:, h * chan : (h + 1) * chan]
     count = n_pairs * 4
     place = lax.broadcasted_iota(jnp.int32, (count, 2 * chan), 0)
     lane = lax.broadcasted_iota(jnp.int32, (count, 2 * chan), 1)
@@ -220,14 +249,18 @@
     for h in range(2):
         half = jnp.concatenate([s[:, h * chan : (h + 1) * chan], pad], axis=0)
         f_ref[base + 32 * h : base + 32 * (h + 1), :] = half.astype(BF16)
+    fetch.wait()
 
 
 def outer_kernel(
-    two, ta, frames_ref, pa_ref, pb_ref, pc_ref, ra_ref, za_ref, rb_ref, zb_ref, wt, dec_ref,
-    out_ref, rowbuf, x3, sc, ia, ib, done, sems,
+    two, ta, pa_ref, pb_ref, pc_ref, ra_ref, za_ref, rb_ref, zb_ref, dec_ref, w_ref, frames_hbm,
+    out_ref, frames_ref, wt, rowbuf, x3, sc, ia, ib, done, sems,
 ):
     frames, height, across, chan = frames_ref.shape
+    fetch = pltpu.make_async_copy(frames_hbm, frames_ref, sems.at[0])
+    fetch.start()
     flip = mirrored(two)
+    pair_weights(w_ref, wt, flip)
     decays = dec_ref[...]
     rows_a = pa_ref.shape[0]
     if ta == 4:
@@ -249,9 +282,9 @@
         for h in range(2):
             part = pc_ref[h, pl.ds(f, count, stride=frames), :]
             sc[f, h, 0:count, :] = part + running[f] * ib[base + 32 * h : base + 32 * h + count, :]
-    for n in range(height + 2):
+    def build(n):
         if two and n == 0:
-            continue
+            return
         if two:
             src, at = ((pa_ref, ia), n - 1) if n < height else ((pb_ref, ib), n - height)
         elif 2 <= n < height:
@@ -269,10 +302,8 @@
             rowbuf[slot, 7 + across : 8 + across, :] = sc[f, h, corner + 2 : corner + 3, :]
             rowbuf[slot, 8 + across : 9 + across, :] = sc[f, h, corner + 3 : corner + 4, :]
             three_taps(rowbuf, slot, x3, n, f, rowbuf[slot, 8 : 8 + across, :].astype(BF16))
-    copies = []
-    for p in range(height // 2):
-        slots = [n if n > 0 or not two else None for n in range(2 * p, 2 * p + 4)]
-        y = pair_dot(x3, slots, wt)
+
+    def finish(p, y):
         first = jnp.where(flip == 1, height - 2 - 2 * p, 2 * p)
         for rr in range(2):
             row = jnp.where(flip == 1, 1 - rr, rr)
@@ -280,23 +311,39 @@
                 mixed = y[f * across : (f + 1) * across, rr * chan : (rr + 1) * chan]
                 frame = frames_ref[f, first + row].astype(F32)
                 done[p, f, row] = (frame + jax.nn.gelu(mixed)).astype(BF16)
-        copies.append(pltpu.make_async_copy(done.at[p], out_ref.at[:, pl.ds(first, 2)], sems.at[p]))
-        copies[-1].start()
+        copy = pltpu.make_async_copy(done.at[p], out_ref.at[:, pl.ds(first, 2)], sems.at[1 + p])
+        copy.start()
+        return copy
+
+    copies, waiting = [], []
+    for n in range(2):
+        build(n)
+    for p in range(height // 2):
+        build(2 * p + 2)
+        build(2 * p + 3)
+        slots = [n if n > 0 or not two else None for n in range(2 * p, 2 * p + 4)]
+        waiting.append((p, pair_dot(x3, slots, wt)))
+        if p == 1:
+            fetch.wait()
+        if p >= 1:
+            copies += [finish(*w) for w in waiting]
+            waiting = []
     for copy in copies:
         copy.wait()
 
 
-def call(body, outs, scratch, flops, args, place=(VMEM, VMEM)):
-    args = [pltpu.with_memory_space_constraint(a, place[0].memory_space) for a in args]
+def call(body, outs, scratch, flops, near, far=(), out_place=VMEM):
+    near = [pltpu.with_memory_space_constraint(a, pltpu.VMEM) for a in near]
+    far = [pltpu.with_memory_space_constraint(a, pltpu.HBM) for a in far]
     return pl.pallas_call(
         body,
         out_shape=outs,
-        in_specs=[place[0]] * len(args),
-        out_specs=jax.tree.map(lambda _: place[1], outs),
+        in_specs=[VMEM] * len(near) + [HBM] * len(far),
+        out_specs=jax.tree.map(lambda _: out_place, outs),
         scratch_shapes=scratch,
-        compiler_params=pltpu.CompilerParams(vmem_limit_bytes=32 * 2**20),
+        compiler_params=pltpu.CompilerParams(vmem_limit_bytes=24 * 2**20),
         cost_estimate=pl.CostEstimate(flops=flops, bytes_accessed=4 * 2**20, transcendentals=0),
-    )(*args)
+    )(*near, *far)
 
 
 def mirrored(two):
@@ -346,50 +393,49 @@
     return [moved(v, 1) for v in locals_]
 
 
-def on_device(gx, gy, ta, frames, in_weight, out_weight, decays):
-    n_frames, height, across, chan = frames.shape
-    two = gx == 2
-    x, t = lax.axis_index("gx"), lax.axis_index("ta")
+def on_device(gx, gy, ta, frames_far, in_weight, out_weight, decays_far):
+    n_frames, height, across, chan = frames_far.shape
+    two = gx == 2 and gy > 2 and gy % 2 == 0
+    t = lax.axis_index("ta")
     near_mem = pltpu.VMEM
-    frames, in_weight, out_weight, decays, cols = call(
-        fetch_kernel,
-        (
-            near_mem(frames.shape, BF16), near_mem(in_weight.shape, BF16), near_mem(out_weight.shape, BF16),
-            near_mem(decays.shape, F32), near_mem((height, 4 * n_frames, chan), BF16),
-        ),
-        [pltpu.VMEM((height * 4 * n_frames, chan), F32), pltpu.SemaphoreType.DMA((4,))],
-        0, [frames, in_weight, out_weight, decays], (HBM, VMEM),
+    sent = []
+    if two:
+        side, corner = (height, 2 * n_frames, chan), (2, 2 * n_frames, chan)
+        sent = [near_mem(s, BF16) for s in ((n_frames, 2, across, chan), side, side, corner, corner)]
+    frames, decays, w_in, cols, *sent = call(
+        functools.partial(fetch_kernel, two),
+        [
+            near_mem(frames_far.shape, BF16), near_mem(decays_far.shape, F32), near_mem(in_weight.shape, BF16),
+            near_mem((height, 4 * n_frames, chan), BF16), *sent,
+        ],
+        [pltpu.VMEM((height * 4 * n_frames, chan), F32), pltpu.SemaphoreType.DMA((3,))],
+        0, [], [frames_far, decays_far, in_weight],
     )
-    low, high = cols[:, : 2 * n_frames], cols[:, 2 * n_frames :]
-    if two:
-        start = jnp.where(x == 1, 0, height - 2)
-        halo = lax.ppermute(lax.dynamic_slice_in_dim(frames, start, 2, axis=1), "gx", [(0, 1), (1, 0)])
-        left, right = exchange(low, high, "gy", gy)
-        facing = [lax.dynamic_slice_in_dim(v, start, 2, axis=0) for v in (low, high)]
-        sides = [cols, left, right, *exchange(*facing, "gy", gy, "gx")]
+    if two:
+        halo = lax.ppermute(sent[0], "gx", [(0, 1), (1, 0)])
+        sides = [swapped(v, "gy", gy, i % 2 == 1, "gx" if i > 1 else None) for i, v in enumerate(sent[1:])]
     else:
         above, below = exchange(frames[:, :2], frames[:, height - 2 :], "gx", gx)
         halo = jnp.concatenate([above, below], axis=1)
         over, under = exchange(cols[:2], cols[height - 2 :], "gx", gx)
         cols = jnp.concatenate([over, cols, under])
-        sides = [cols, *exchange(cols[:, : 2 * n_frames], cols[:, 2 * n_frames :], "gy", gy)]
+        sides = exchange(cols[:, : 2 * n_frames], cols[:, 2 * n_frames :], "gy", gy)
 
     rows_a = height - 1 if two else height - 2
     rows_b = 2 if two else 4
-    wide = (12 * chan, 2 * chan)
+    wt = pltpu.VMEM((12 * chan, 2 * chan), BF16)
     rowbuf = pltpu.VMEM((16, across + 16, chan), F32)
     cells = n_frames * across
     flops = 2 * 9 * chan * chan * cells
-    pa, fa, wt_in = call(
+    pa, fa = call(
         functools.partial(inner_kernel, two),
-        (
-            near_mem((rows_a, n_frames, across, chan), F32), near_mem((rows_a * across + 16, chan), BF16),
-            near_mem(wide, BF16),
-        ),
-        [rowbuf, pltpu.VMEM((height, cells, 3 * chan), BF16)],
-        flops * height, [frames, in_weight, decays],
+        (near_mem((rows_a, n_frames, across, chan), F32), near_mem((rows_a * across + 16, chan), BF16)),
+        [wt, rowbuf, pltpu.VMEM((height, cells, 3 * chan), BF16)],
+        flops * height, [frames, decays, w_in],
     )
 
+    if two:
+        fa, *sides = lax.optimization_barrier((fa, *sides))
     total = jnp.prod(decays, axis=0)[None]
     if ta == 4:
         ra = swapped(fa, "ta", ta, False)
@@ -403,22 +449,21 @@
         za = lax.ppermute(joined(fa, ra), "ta", across_two)
 
     n_cols = (height // 2 + 1) * 4
-    pb, pc, fb, wt_out = call(
+    pb, pc, fb, w_out = call(
         functools.partial(edge_kernel, two, gx, gy),
         (
             near_mem((rows_b, n_frames, across, chan), F32),
             near_mem((2, n_cols * n_frames, chan), F32),
             near_mem((rows_b * across + 64, chan), BF16),
-            near_mem(wide, BF16),
+            near_mem(out_weight.shape, BF16),
         ),
         [
-            rowbuf, pltpu.VMEM((2 * rows_b, cells, 3 * chan), BF16),
+            wt, rowbuf, pltpu.VMEM((2 * rows_b, cells, 3 * chan), BF16),
             pltpu.VMEM((n_cols * n_frames, 12 * chan), BF16), pltpu.VMEM((2, n_cols * n_frames, chan), F32),
-            pltpu.VMEM((8 * n_frames, chan), F32),
+            pltpu.VMEM((8 * n_frames, chan), F32), pltpu.SemaphoreType.DMA,
         ],
-        flops * rows_b, [frames, halo, wt_in, decays, out_weight, *sides],
+        flops * rows_b, [sent[0] if two else frames, decays, w_in, halo, cols, *sides], [out_weight],
     )
-
     if ta == 4:
         rb = swapped(fb, "ta", ta, False)
         zb = lax.ppermute(joined(fb, rb), "ta", across_two)
@@ -430,12 +475,12 @@
         functools.partial(outer_kernel, two, ta),
         jax.ShapeDtypeStruct(frames.shape, BF16),
         [
-            rowbuf, pltpu.VMEM((height + 2, cells, 3 * chan), BF16),
+            pltpu.VMEM(frames.shape, BF16), wt, rowbuf, pltpu.VMEM((height + 2, cells, 3 * chan), BF16),
             pltpu.VMEM((n_frames, 2, (n_cols + 7) // 8 * 8, chan), F32),
             pltpu.VMEM((rows_a * across, chan), F32), pltpu.VMEM((rows_b * across + 64, chan), F32),
-            pltpu.VMEM((height // 2, n_frames, 2, across, chan), BF16), pltpu.SemaphoreType.DMA((height // 2,)),
+            pltpu.VMEM((height // 2, n_frames, 2, across, chan), BF16), pltpu.SemaphoreType.DMA((1 + height // 2,)),
         ],
-        flops * height, [frames, pa, pb, pc, ra, za, rb, zb, wt_out, decays], (VMEM, HBM),
+        flops * height, [pa, pb, pc, ra, za, rb, zb, decays, w_out], [frames_far], HBM,
     )
 
 

time: 35.5 us -> 32.1 us (0.904)
  local copies, waits for them, and re-layouts: 4.34 us -> 0 us
  waiting for transfers between devices: 5.99 us -> 8.17 us
  other arithmetic: 2.2 us -> 0.13 us
  Pallas kernels: 7.94 us -> 9.49 us
  starting transfers between devices: 14.7 us -> 14 us
    unnamed x12 -> x0, local copies, waits for them, and re-layouts: 3.62 us -> none
    pallas_call x4, Pallas kernels: 7.94 us -> 9.49 us  [call(): pl.pallas_call(body, out_shape=outs, in_specs=[VMEM] * len(near) + [HBM]...]
    select_n x3 -> x0, other arithmetic: 1.39 us -> none  [the longest x2 0.78 us: exchange(): return (jnp.where(odd, near, far), jnp.where(odd, far, near))]
    ppermute x4, waiting for transfers between devices: 2.7 us -> 3.94 us  [swapped(): return lax.ppermute(value, axis, pairs)]
    dynamic_slice x1 -> x0, local copies, waits for them, and re-layouts: 0.72 us -> none  [on_device(): lax.dynamic_slice_in_dim(frames, start, 2, axis=1)]
    slice x1 -> x0, other arithmetic: 0.68 us -> none  [on_device(): low, high = (cols[:, :2 * n_frames], cols[:, 2 * n_frames:])]
    ppermute x1, starting transfers between devices: 2.51 us -> 1.99 us  [on_device(): zb = lax.ppermute(joined(fb, rb), 'ta', across_two)]
    ppermute x1, waiting for transfers between devices: 0.53 us -> 1.04 us  [on_device(): zb = lax.ppermute(joined(fb, rb), 'ta', across_two)]
  transfers between devices with their start and end apart: 9 -> 9, of which waited for: 3 -> 4; matrix products, arithmetic and copies ran while one was open for 5% -> 0% of each run, Pallas kernels for 6% -> 6%
where the time goes in v5:
time: 32.1 us; the launch traced here: 31.9 us
  starting transfers between devices  14 us (44%)
  Pallas kernels  9.49 us (30%)
  waiting for transfers between devices  8.17 us (25%)
    pallas_call x4, Pallas kernels, call(): pl.pallas_call(body, out_shape=outs, in_specs=[VMEM] * len(near) + [HBM]...  9.49 us
    ppermute x2, starting transfers between devices, swapped(): return lax.ppermute(value, (mirror, axis), both)  4.21 us
    ppermute x4, waiting for transfers between devices, swapped(): return lax.ppermute(value, axis, pairs)  3.94 us
    ppermute x1, waiting for transfers between devices, on_device(): za = lax.ppermute(joined(fa, ra), 'ta', across_two)  3.18 us
    ppermute x4, starting transfers between devices, swapped(): return lax.ppermute(value, axis, pairs)  3.13 us
    ppermute x1, starting transfers between devices, on_device(): za = lax.ppermute(joined(fa, ra), 'ta', across_two)  2.65 us
    ppermute x1, starting transfers between devices, on_device(): halo = lax.ppermute(sent[0], 'gx', [(0, 1), (1, 0)])  2.06 us
    ppermute x1, starting transfers between devices, on_device(): zb = lax.ppermute(joined(fb, rb), 'ta', across_two)  1.99 us
  transfers between devices with their start and end apart: 9, of which 4 were waited for; matrix products, arithmetic and copies ran while one was open for 0% of the time, Pallas kernels for 6%

profile of v5, /device:TPU:0, one launch (start us, length us, event | category | flops | bytes accessed | tf_op | source)
XLA Modules:
  0.0 31.9 jit_solution(16643063822860333611)
XLA Ops:
  0.0 1.3 %shard_map.46 = (bf16[8,8,64,128]{3,2,1,0:T(8,128)(2,1)S(1)}, f32[8,128]{1,0:T(8,128)S(1)}, bf16[3,3,128,128]{3,2,1,0:T(8,128)(2,1)S(1)}, bf16[8,32,128]{2,1,0:T...) custom-call(bf16[8,8,64,128]{3,2,1,0:T(8,128)(2,1)} %frames_hbm.3, ...), custom_call_target="tpu_custom_call" | custom-call | bytes 4194304 | tf_op jit(solution)/shard_map/pallas_call | solution.py:338
  1.3 2.4 %collective-permute-start.3 = (bf16[2,16,128]{2,1,0:T(8,128)(2,1)S(1)}, bf16[2,16,128]{2,1,0:T(8,128)(2,1)S(1)}, u32[]{:S(2)}, u32[]{:S(2)}) collective-permute-start(bf16[2,16,128]{2,1,0:T(8,128)(2,1)S(1)} %get-tuple-element.34), channel_id=1, source_target_pairs={{0,20},{8,28},{4,16},{12,24},{16,4},{24,12},{20,0},{28,8},{1,21},{... | collective-permute-start | bytes 24584 | tf_op jit(solution)/shard_map/ppermute | solution.py:360
  3.8 1.8 %collective-permute-start.4 = (bf16[2,16,128]{2,1,0:T(8,128)(2,1)S(1)}, bf16[2,16,128]{2,1,0:T(8,128)(2,1)S(1)}, u32[]{:S(2)}, u32[]{:S(2)}) collective-permute-start(bf16[2,16,128]{2,1,0:T(8,128)(2,1)S(1)} %get-tuple-element.35), channel_id=1, source_target_pairs={{4,24},{12,16},{8,20},{0,28},{20,8},{28,0},{24,4},{16,12},{5,25},{... | collective-permute-start | bytes 24584 | tf_op jit(solution)/shard_map/ppermute | solution.py:360
  5.6 0.0 collective-permute-start.1
  5.6 0.1 collective-permute-start.2
  5.6 2.1 %collective-permute-start = (bf16[8,2,64,128]{3,2,1,0:T(8,128)(2,1)S(1)}, bf16[8,2,64,128]{3,2,1,0:T(8,128)(2,1)S(1)}, u32[]{:S(2)}, u32[]{:S(2)}) collective-permute-start(bf16[8,2,64,128]{3,2,1,0:T(8,128)(2,1)S(1)} %get-tuple-element.29.own_ref), channel_id=1, source_target_pairs={{0,16},{16,0},{1,17},{17,1},{2,18},{18,2},{3,19},{19,3},{4,20},{20... | collective-permute-start | bytes 786440 | tf_op jit(solution)/shard_map/ppermute | solution.py:415
  7.7 2.0 %shard_map.47 = (f32[7,8,64,128]{3,2,1,0:T(8,128)S(1)}, bf16[464,128]{1,0:T(8,128)(2,1)S(1)}) custom-call(bf16[8,8,64,128]{3,2,1,0:T(8,128)(2,1)S(1)} %get-tuple-element.25.frames_ref, f32[8,128]{1,0:T(8,128)S(1)} %get-tuple-element.26.dec_ref, bf16[3,3,128,128]{3,2,1,0:T(8,128)(2,1)S(1)} %get-tuple-element.27.w_ref), custom_call_target="tpu_custom_call" | custom-call | flops 1207959552 | bytes 4194304 | tf_op jit(solution)/shard_map/pallas_call | solution.py:338
  9.7 0.0 collective-permute-done.3.refs_2_
  9.7 0.0 collective-permute-done.4.refs_3_
  9.7 0.0 collective-permute-done.1.refs_0_
  9.7 0.0 collective-permute-done.2.refs_1_
  9.7 1.6 %collective-permute-start.5 = (bf16[464,128]{1,0:T(8,128)(2,1)S(1)}, bf16[464,128]{1,0:T(8,128)(2,1)S(1)}, u32[]{:S(2)}, u32[]{:S(2)}) collective-permute-start(bf16[464,128]{1,0:T(8,128)(2,1)S(1)} %get-tuple-element.42), channel_id=1, source_target_pairs={{0,1},{2,3},{1,0},{3,2},{4,5},{6,7},{5,4},{7,6},{8,9},{10,11},{9,8... | collective-permute-start | bytes 356360 | tf_op jit(solution)/shard_map/ppermute | solution.py:358
  11.4 3.5 %collective-permute-done.5.ra_ref = bf16[464,128]{1,0:T(8,128)(2,1)S(1)} collective-permute-done((bf16[464,128]{1,0:T(8,128)(2,1)S(1)}, bf16[464,128]{1,0:T(8,128)(2,1)S(1)}, u32[]{:S(2)}, u32[]{:S(2)}) %collective-permute-start.5) | collective-permute-done | bytes 118816 | tf_op jit(solution)/shard_map/ppermute | solution.py:358
  14.9 0.0 collective-permute-done.halo_ref
  14.9 1.8 %shard_map.48 = (f32[2,8,64,128]{3,2,1,0:T(8,128)S(1)}, f32[2,160,128]{2,1,0:T(8,128)S(1)}, bf16[192,128]{1,0:T(8,128)(2,1)S(1)}, bf16[3,3,128,128]{3,2,1,0:T(8,128)(2,1)S(1)}) custom-call(bf16[8,2,64,128]{3,2,1,0:T(8,128)(2,1)S(1)} %get-tuple-element.29.own_ref, f32[8,128]{1,0:T(8,128)S(1)} %get-tuple-element.26.dec_ref, ...), custom_call_target="tpu_custom_call" | custom-call | flops 301989888 | bytes 4194304 | tf_op jit(solution)/shard_map/pallas_call | solution.py:338
  16.6 1.4 %collective-permute-start.7 = (bf16[192,128]{1,0:T(8,128)(2,1)S(1)}, bf16[192,128]{1,0:T(8,128)(2,1)S(1)}, u32[]{:S(2)}, u32[]{:S(2)}) collective-permute-start(bf16[192,128]{1,0:T(8,128)(2,1)S(1)} %get-tuple-element.43), channel_id=1, source_target_pairs={{0,1},{2,3},{1,0},{3,2},{4,5},{6,7},{5,4},{7,6},{8,9},{10,11},{9,8... | collective-permute-start | bytes 147464 | tf_op jit(solution)/shard_map/ppermute | solution.py:358
  18.1 0.1 fusion.1
  18.2 2.7 %collective-permute-start.6 = (bf16[464,128]{1,0:T(8,128)(2,1)S(1)}, bf16[464,128]{1,0:T(8,128)(2,1)S(1)}, u32[]{:S(2)}, u32[]{:S(2)}) collective-permute-start(bf16[464,128]{1,0:T(8,128)(2,1)S(1)} %fusion.1), channel_id=1, source_target_pairs={{0,2},{2,0},{1,3},{3,1},{4,6},{6,4},{5,7},{7,5},{8,10},{10,8},{9,1... | collective-permute-start | bytes 356360 | tf_op jit(solution)/shard_map/ppermute | solution.py:449
  20.8 0.5 %collective-permute-done.7.rb_ref = bf16[192,128]{1,0:T(8,128)(2,1)S(1)} collective-permute-done((bf16[192,128]{1,0:T(8,128)(2,1)S(1)}, bf16[192,128]{1,0:T(8,128)(2,1)S(1)}, u32[]{:S(2)}, u32[]{:S(2)}) %collective-permute-start.7) | collective-permute-done | bytes 49184 | tf_op jit(solution)/shard_map/ppermute | solution.py:358
  21.3 2.0 %collective-permute-start.8 = (bf16[192,128]{1,0:T(8,128)(2,1)S(1)}, bf16[192,128]{1,0:T(8,128)(2,1)S(1)}, u32[]{:S(2)}, u32[]{:S(2)}) collective-permute-start(bf16[192,128]{1,0:T(8,128)(2,1)S(1)} %fusion.3), channel_id=1, source_target_pairs={{0,2},{2,0},{1,3},{3,1},{4,6},{6,4},{5,7},{7,5},{8,10},{10,8},{9,1... | collective-permute-start | bytes 147464 | tf_op jit(solution)/shard_map/ppermute | solution.py:469
  23.3 3.2 %collective-permute-done.6.za_ref = bf16[464,128]{1,0:T(8,128)(2,1)S(1)} collective-permute-done((bf16[464,128]{1,0:T(8,128)(2,1)S(1)}, bf16[464,128]{1,0:T(8,128)(2,1)S(1)}, u32[]{:S(2)}, u32[]{:S(2)}) %collective-permute-start.6) | collective-permute-done | bytes 118816 | tf_op jit(solution)/shard_map/ppermute | solution.py:449
  26.5 1.0 %collective-permute-done.8.zb_ref = bf16[192,128]{1,0:T(8,128)(2,1)S(1)} collective-permute-done((bf16[192,128]{1,0:T(8,128)(2,1)S(1)}, bf16[192,128]{1,0:T(8,128)(2,1)S(1)}, u32[]{:S(2)}, u32[]{:S(2)}) %collective-permute-start.8) | collective-permute-done | bytes 49184 | tf_op jit(solution)/shard_map/ppermute | solution.py:469
  27.5 4.4 %shard_map.49 = bf16[8,8,64,128]{3,2,1,0:T(8,128)(2,1)} custom-call(f32[7,8,64,128]{3,2,1,0:T(8,128)S(1)} %get-tuple-element.28.pa_ref, f32[2,8,64,128]{3,2,1,0:T(8,128)S(1)} %get-tuple-element.40.pb_ref, f32[2,160,128]{2,1,0:T(8,128)S(1)} %get-tuple-element.41.pc_ref, bf16[464,128]{1,0:T(8,128)(2,1)S(1)} %collective-permute-done.5.ra_ref, ...), custom_call_target="tpu_custom_call" | custom-call | flops 1207959552 | bytes 4194304 | tf_op jit(solution)/shard_map/pallas_call | solution.py:338
  (3 shorter events, 0.1 us)
Async XLA Ops:
  1.3 8.3 %collective-permute-start.3 = (bf16[2,16,128]{2,1,0:T(8,128)(2,1)S(1)}, bf16[2,16,128]{2,1,0:T(8,128)(2,1)S(1)}, u32[]{:S(2)}, u32[]{:S(2)}) collective-permute-start(bf16[2,16,128]{2,1,0:T(8,128)(2,1)S(1)} %get-tuple-element.34), channel_id=1, source_target_pairs={{0,20},{8,28},{4,16},{12,24},{16,4},{24,12},{20,0},{28,8},{1,21},{... | collective-permute-start | bytes 24584 | tf_op jit(solution)/shard_map/ppermute | solution.py:360
  3.8 5.9 %collective-permute-start.4 = (bf16[2,16,128]{2,1,0:T(8,128)(2,1)S(1)}, bf16[2,16,128]{2,1,0:T(8,128)(2,1)S(1)}, u32[]{:S(2)}, u32[]{:S(2)}) collective-permute-start(bf16[2,16,128]{2,1,0:T(8,128)(2,1)S(1)} %get-tuple-element.35), channel_id=1, source_target_pairs={{4,24},{12,16},{8,20},{0,28},{20,8},{28,0},{24,4},{16,12},{5,25},{... | collective-permute-start | bytes 24584 | tf_op jit(solution)/shard_map/ppermute | solution.py:360
  5.6 4.1 %collective-permute-start.1 = (bf16[8,16,128]{2,1,0:T(8,128)(2,1)S(1)}, bf16[8,16,128]{2,1,0:T(8,128)(2,1)S(1)}, u32[]{:S(2)}, u32[]{:S(2)}) collective-permute-start(bf16[8,16,128]{2,1,0:T(8,128)(2,1)S(1)} %get-tuple-element.32), channel_id=1, source_target_pairs={{0,4},{8,12},{4,0},{12,8},{1,5},{9,13},{5,1},{13,9},{2,6},{10,14},... | collective-permute-start | bytes 98312 | tf_op jit(solution)/shard_map/ppermute | solution.py:358
  5.6 4.1 %collective-permute-start.2 = (bf16[8,16,128]{2,1,0:T(8,128)(2,1)S(1)}, bf16[8,16,128]{2,1,0:T(8,128)(2,1)S(1)}, u32[]{:S(2)}, u32[]{:S(2)}) collective-permute-start(bf16[8,16,128]{2,1,0:T(8,128)(2,1)S(1)} %get-tuple-element.33), channel_id=1, source_target_pairs={{4,8},{12,0},{8,4},{0,12},{5,9},{13,1},{9,5},{1,13},{6,10},{14,2},... | collective-permute-start | bytes 98312 | tf_op jit(solution)/shard_map/ppermute | solution.py:358
  5.6 9.3 %collective-permute-start = (bf16[8,2,64,128]{3,2,1,0:T(8,128)(2,1)S(1)}, bf16[8,2,64,128]{3,2,1,0:T(8,128)(2,1)S(1)}, u32[]{:S(2)}, u32[]{:S(2)}) collective-permute-start(bf16[8,2,64,128]{3,2,1,0:T(8,128)(2,1)S(1)} %get-tuple-element.29.own_ref), channel_id=1, source_target_pairs={{0,16},{16,0},{1,17},{17,1},{2,18},{18,2},{3,19},{19,3},{4,20},{20... | collective-permute-start | bytes 786440 | tf_op jit(solution)/shard_map/ppermute | solution.py:415
  9.7 5.1 %collective-permute-start.5 = (bf16[464,128]{1,0:T(8,128)(2,1)S(1)}, bf16[464,128]{1,0:T(8,128)(2,1)S(1)}, u32[]{:S(2)}, u32[]{:S(2)}) collective-permute-start(bf16[464,128]{1,0:T(8,128)(2,1)S(1)} %get-tuple-element.42), channel_id=1, source_target_pairs={{0,1},{2,3},{1,0},{3,2},{4,5},{6,7},{5,4},{7,6},{8,9},{10,11},{9,8... | collective-permute-start | bytes 356360 | tf_op jit(solution)/shard_map/ppermute | solution.py:358
  16.6 4.6 %collective-permute-start.7 = (bf16[192,128]{1,0:T(8,128)(2,1)S(1)}, bf16[192,128]{1,0:T(8,128)(2,1)S(1)}, u32[]{:S(2)}, u32[]{:S(2)}) collective-permute-start(bf16[192,128]{1,0:T(8,128)(2,1)S(1)} %get-tuple-element.43), channel_id=1, source_target_pairs={{0,1},{2,3},{1,0},{3,2},{4,5},{6,7},{5,4},{7,6},{8,9},{10,11},{9,8... | collective-permute-start | bytes 147464 | tf_op jit(solution)/shard_map/ppermute | solution.py:358
  18.2 8.3 %collective-permute-start.6 = (bf16[464,128]{1,0:T(8,128)(2,1)S(1)}, bf16[464,128]{1,0:T(8,128)(2,1)S(1)}, u32[]{:S(2)}, u32[]{:S(2)}) collective-permute-start(bf16[464,128]{1,0:T(8,128)(2,1)S(1)} %fusion.1), channel_id=1, source_target_pairs={{0,2},{2,0},{1,3},{3,1},{4,6},{6,4},{5,7},{7,5},{8,10},{10,8},{9,1... | collective-permute-start | bytes 356360 | tf_op jit(solution)/shard_map/ppermute | solution.py:449
  21.3 6.2 %collective-permute-start.8 = (bf16[192,128]{1,0:T(8,128)(2,1)S(1)}, bf16[192,128]{1,0:T(8,128)(2,1)S(1)}, u32[]{:S(2)}, u32[]{:S(2)}) collective-permute-start(bf16[192,128]{1,0:T(8,128)(2,1)S(1)} %fusion.3), channel_id=1, source_target_pairs={{0,2},{2,0},{1,3},{3,1},{4,6},{6,4},{5,7},{7,5},{8,10},{10,8},{9,1... | collective-permute-start | bytes 147464 | tf_op jit(solution)/shard_map/ppermute | solution.py:469

commit v6 on v5

--- a/solution.py
+++ b/solution.py
@@ -89,17 +89,17 @@
     for r in range(height):
         cols_ref[r] = edge[r * 4 * frames : (r + 1) * 4 * frames, :].astype(BF16)
     if two:
-        halo_ref, near_ref, far_ref, near_corner, far_corner = sent
+        corner_ref, halo_ref, near_ref, far_ref = sent
         odd = lax.axis_index("gy") % 2 == 1
         start = jnp.where(lax.axis_index("gx") == 1, 0, height - 2)
         halo_ref[...] = frames_ref[:, pl.ds(start, 2)]
         half = 2 * frames
-        for refs, rows in (((near_ref, far_ref), range(height)), ((near_corner, far_corner), (start, start + 1))):
-            for i, r in enumerate(rows):
-                at = pl.multiple_of(r * 2 * half, 2 * half)
-                low, high = edge[pl.ds(at, half), :], edge[pl.ds(at + half, half), :]
-                refs[0][i] = jnp.where(odd, low, high).astype(BF16)
-                refs[1][i] = jnp.where(odd, high, low).astype(BF16)
+        for r in range(height):
+            low, high = edge[r * 2 * half : r * 2 * half + half, :], edge[r * 2 * half + half : (r + 1) * 2 * half, :]
+            near_ref[r] = jnp.where(odd, low, high).astype(BF16)
+            far_ref[r] = jnp.where(odd, high, low).astype(BF16)
+        for i in range(2):
+            corner_ref[i] = edge[pl.ds(pl.multiple_of((start + i) * 2 * half, 2 * half), 2 * half), :].astype(BF16)
     for copy in copies[1:]:
         copy.wait()
 
@@ -144,8 +144,8 @@
     f_ref[end - 16 : end, :] = parts.astype(BF16)
 
 
-def edge_kernel(two, gx, gy, own_ref, dec_ref, w_ref, halo_ref, e_ref, *refs):
-    *sides, next_hbm, p_ref, pc_ref, f_ref, next_ref, wt, rowbuf, x3, xc, yc, edge, sem = refs
+def edge_kernel(two, gx, gy, own_ref, dec_ref, w_ref, halo_ref, e_ref, corner_ref, *refs):
+    *sides, next_hbm, p_ref, pc_ref, f_ref, next_ref, wt, rowbuf, x3, xc, yc, sem = refs
     fetch = pltpu.make_async_copy(next_hbm, next_ref, sem)
     fetch.start()
     frames, across, chan = own_ref.shape[0], *own_ref.shape[2:]
@@ -183,9 +183,6 @@
         return jnp.where(odd, first, second), jnp.where(odd, second, first)
 
     n_pairs = height // 2 + 1
-    if two:
-        for i in range(2):
-            gather_edges(halo_ref, jnp.where(flip == 1, 1 - i, i), edge, i * 4 * frames)
     for p in range(n_pairs):
         for k in range(4):
             r = 2 * p - 2 + k
@@ -196,12 +193,12 @@
                 continue
             if two and r >= height:
                 at = jnp.where(flip == 1, 1 - (r - height), r - height)
-                own = edge[(r - height) * 4 * frames : (r - height + 1) * 4 * frames, :]
-                left, right = beside(at, *sides[2:])
+                own = corner_ref[at].astype(F32)
+                left, right = beside(height + at, *sides)
             else:
                 at = jnp.where(flip == 1, height - 1 - r, r) if two else r + 2
                 own = e_ref[at].astype(F32)
-                left, right = beside(at, *sides[:2])
+                left, right = beside(at, *sides)
             cols = [left[:frames], left[frames:]] + [own[c * frames : (c + 1) * frames] for c in range(4)]
             cols += [right[:frames], right[frames:]]
             for b in range(3):
@@ -350,29 +347,23 @@
     return lax.axis_index("gx") if two else 0
 
 
-def swapped(value, axis, count, odd_first=False, mirror=None):
+def swapped(value, axis, count, odd_first):
     off = 1 if odd_first else 0
     pairs = [((i + off) % count, (i + 1 + off) % count) for i in range(0, count, 2)]
-    pairs += [(b, a) for a, b in pairs]
-    if mirror is None:
-        return lax.ppermute(value, axis, pairs)
-    both = [(m * count + a, (1 - m) * count + b) for m in range(2) for a, b in pairs]
-    return lax.ppermute(value, (mirror, axis), both)
-
-
-def exchange(low, high, axis, count, mirror=None):
+    return lax.ppermute(value, axis, pairs + [(b, a) for a, b in pairs])
+
+
+def exchange(low, high, axis, count):
     at = lax.axis_index(axis)
     odd = at % 2 == 1
     if count % 2:
         ups, downs = [(i, i + 1) for i in range(count - 1)], [(i + 1, i) for i in range(count - 1)]
-        if mirror is not None:
-            high, low = (lax.ppermute(v, mirror, [(0, 1), (1, 0)]) for v in (high, low))
         return lax.ppermute(high, axis, ups), lax.ppermute(low, axis, downs)
-    near = swapped(jnp.where(odd, low, high), axis, count, False, mirror)
+    near = swapped(jnp.where(odd, low, high), axis, count, False)
     if count == 2:
         far = jnp.zeros_like(near)
     else:
-        far = swapped(jnp.where(odd, high, low), axis, count, True, mirror)
+        far = swapped(jnp.where(odd, high, low), axis, count, True)
         far = jnp.where((at == 0) | (at == count - 1), jnp.zeros_like(far), far)
     return jnp.where(odd, near, far), jnp.where(odd, far, near)
 
@@ -400,8 +391,8 @@
     near_mem = pltpu.VMEM
     sent = []
     if two:
-        side, corner = (height, 2 * n_frames, chan), (2, 2 * n_frames, chan)
-        sent = [near_mem(s, BF16) for s in ((n_frames, 2, across, chan), side, side, corner, corner)]
+        side = (height, 2 * n_frames, chan)
+        sent = [near_mem(s, BF16) for s in ((2, 4 * n_frames, chan), (n_frames, 2, across, chan), side, side)]
     frames, decays, w_in, cols, *sent = call(
         functools.partial(fetch_kernel, two),
         [
@@ -412,14 +403,16 @@
         0, [], [frames_far, decays_far, in_weight],
     )
     if two:
-        halo = lax.ppermute(sent[0], "gx", [(0, 1), (1, 0)])
-        sides = [swapped(v, "gy", gy, i % 2 == 1, "gx" if i > 1 else None) for i, v in enumerate(sent[1:])]
+        facing = [(0, 1), (1, 0)]
+        corner = lax.ppermute(sent[0], "gx", facing)
+        halo = lax.ppermute(sent[1], "gx", facing)
     else:
         above, below = exchange(frames[:, :2], frames[:, height - 2 :], "gx", gx)
         halo = jnp.concatenate([above, below], axis=1)
         over, under = exchange(cols[:2], cols[height - 2 :], "gx", gx)
         cols = jnp.concatenate([over, cols, under])
         sides = exchange(cols[:, : 2 * n_frames], cols[:, 2 * n_frames :], "gy", gy)
+        corner = cols[:2]
 
     rows_a = height - 1 if two else height - 2
     rows_b = 2 if two else 4
@@ -435,7 +428,12 @@
     )
 
     if two:
-        fa, *sides = lax.optimization_barrier((fa, *sides))
+        fa, corner = lax.optimization_barrier((fa, corner))
+        odd = lax.axis_index("gy") % 2 == 1
+        low, high = corner[:, : 2 * n_frames], corner[:, 2 * n_frames :]
+        near = jnp.concatenate([sent[2], jnp.where(odd, low, high)])
+        far = jnp.concatenate([sent[3], jnp.where(odd, high, low)])
+        sides = [swapped(near, "gy", gy, False), swapped(far, "gy", gy, True)]
     total = jnp.prod(decays, axis=0)[None]
     if ta == 4:
         ra = swapped(fa, "ta", ta, False)
@@ -446,7 +444,9 @@
             return jnp.where(t == 0, theirs + other * mine, mine + total * theirs).astype(BF16)
 
         across_two = [(0, 2), (2, 0), (1, 3), (3, 1)]
-        za = lax.ppermute(joined(fa, ra), "ta", across_two)
+        ga = joined(fa, ra)
+        za = lax.ppermute(ga, "ta", across_two)
+        _, *sides = lax.optimization_barrier((ga, *sides))
 
     n_cols = (height // 2 + 1) * 4
     pb, pc, fb, w_out = call(
@@ -460,12 +460,12 @@
         [
             wt, rowbuf, pltpu.VMEM((2 * rows_b, cells, 3 * chan), BF16),
             pltpu.VMEM((n_cols * n_frames, 12 * chan), BF16), pltpu.VMEM((2, n_cols * n_frames, chan), F32),
-            pltpu.VMEM((8 * n_frames, chan), F32), pltpu.SemaphoreType.DMA,
+            pltpu.SemaphoreType.DMA,
         ],
-        flops * rows_b, [sent[0] if two else frames, decays, w_in, halo, cols, *sides], [out_weight],
+        flops * rows_b, [sent[1] if two else frames, decays, w_in, halo, cols, corner, *sides], [out_weight],
     )
     if ta == 4:
-        rb = swapped(fb, "ta", ta, False)
+        za, rb = lax.optimization_barrier((za, swapped(fb, "ta", ta, False)))
         zb = lax.ppermute(joined(fb, rb), "ta", across_two)
     else:
         ra, rb = carry_general([fa, fb], total, ta)

time: 32.1 us -> 30.2 us (0.941)
  starting transfers between devices: 14 us -> 12 us
    ppermute x1, waiting for transfers between devices: 1.04 us -> 4.65 us  [on_device(): zb = lax.ppermute(joined(fb, rb), 'ta', across_two)]
    ppermute x8 -> x7, waiting for transfers between devices: 7.13 us -> 3.6 us  [the longest x4 2.46 us: swapped(): return lax.ppermute(value, axis, pairs + [(b, a) for a, b in pairs])]
    ppermute x1, starting transfers between devices: 1.99 us -> 0.41 us  [on_device(): zb = lax.ppermute(joined(fb, rb), 'ta', across_two)]
    ppermute x8 -> x7, starting transfers between devices: 12.1 us -> 11.6 us  [the longest x4 5.44 us: swapped(): return lax.ppermute(value, axis, pairs + [(b, a) for a, b in pairs])]
  transfers between devices with their start and end apart: 9 -> 8, of which waited for: 4 -> 4; matrix products, arithmetic and copies ran while one was open for 0% -> 0% of each run, Pallas kernels for 6% -> 12%
where the time goes in v6:
time: 30.2 us; the launch traced here: 30 us
  starting transfers between devices  12 us (40%)
  Pallas kernels  9.46 us (31%)
  waiting for transfers between devices  8.25 us (27%)
    pallas_call x4, Pallas kernels, call(): pl.pallas_call(body, out_shape=outs, in_specs=[VMEM] * len(near) + [HBM]...  9.46 us
    ppermute x4, starting transfers between devices, swapped(): return lax.ppermute(value, axis, pairs + [(b, a) for a, b in pairs])  5.44 us
    ppermute x1, waiting for transfers between devices, on_device(): zb = lax.ppermute(joined(fb, rb), 'ta', across_two)  4.65 us
    ppermute x1, starting transfers between devices, on_device(): za = lax.ppermute(ga, 'ta', across_two)  3.1 us
    ppermute x1, starting transfers between devices, on_device(): corner = lax.ppermute(sent[0], 'gx', facing)  3 us
    ppermute x4, waiting for transfers between devices, swapped(): return lax.ppermute(value, axis, pairs + [(b, a) for a, b in pairs])  2.46 us
    ppermute x1, waiting for transfers between devices, on_device(): za = lax.ppermute(ga, 'ta', across_two)  1.13 us
  transfers between devices with their start and end apart: 8, of which 4 were waited for; matrix products, arithmetic and copies ran while one was open for 0% of the time, Pallas kernels for 12%

profile of v6, /device:TPU:0, one launch (start us, length us, event | category | flops | bytes accessed | tf_op | source)
XLA Modules:
  0.0 30.0 jit_solution(10660782146189396414)
XLA Ops:
  0.0 1.3 %shard_map.46 = (bf16[8,8,64,128]{3,2,1,0:T(8,128)(2,1)S(1)}, f32[8,128]{1,0:T(8,128)S(1)}, bf16[3,3,128,128]{3,2,1,0:T(8,128)(2,1)S(1)}, bf16[8,32,128]{2,1,0:T...) custom-call(bf16[8,8,64,128]{3,2,1,0:T(8,128)(2,1)} %frames_hbm.3, ...), custom_call_target="tpu_custom_call" | custom-call | bytes 4194304 | tf_op jit(solution)/shard_map/pallas_call | solution.py:335
  1.3 3.0 %collective-permute-start.1 = (bf16[2,32,128]{2,1,0:T(8,128)(2,1)S(1)}, bf16[2,32,128]{2,1,0:T(8,128)(2,1)S(1)}, u32[]{:S(2)}, u32[]{:S(2)}) collective-permute-start(bf16[2,32,128]{2,1,0:T(8,128)(2,1)S(1)} %get-tuple-element.32), channel_id=1, source_target_pairs={{0,16},{16,0},{1,17},{17,1},{2,18},{18,2},{3,19},{19,3},{4,20},{20... | collective-permute-start | bytes 49160 | tf_op jit(solution)/shard_map/ppermute | solution.py:407
  4.3 0.1 collective-permute-start
  4.4 2.0 %shard_map.47 = (f32[7,8,64,128]{3,2,1,0:T(8,128)S(1)}, bf16[464,128]{1,0:T(8,128)(2,1)S(1)}) custom-call(bf16[8,8,64,128]{3,2,1,0:T(8,128)(2,1)S(1)} %get-tuple-element.25.frames_ref, f32[8,128]{1,0:T(8,128)S(1)} %get-tuple-element.26.dec_ref, bf16[3,3,128,128]{3,2,1,0:T(8,128)(2,1)S(1)} %get-tuple-element.27.w_ref), custom_call_target="tpu_custom_call" | custom-call | flops 1207959552 | bytes 4194304 | tf_op jit(solution)/shard_map/pallas_call | solution.py:335
  6.4 0.0 collective-permute-done.1.corner_ref
  6.5 2.1 %collective-permute-start.2 = (bf16[464,128]{1,0:T(8,128)(2,1)S(1)}, bf16[464,128]{1,0:T(8,128)(2,1)S(1)}, u32[]{:S(2)}, u32[]{:S(2)}) collective-permute-start(bf16[464,128]{1,0:T(8,128)(2,1)S(1)} %get-tuple-element.34), channel_id=1, source_target_pairs={{0,1},{2,3},{1,0},{3,2},{4,5},{6,7},{5,4},{7,6},{8,9},{10,11},{9,8... | collective-permute-start | bytes 356360 | tf_op jit(solution)/shard_map/ppermute | solution.py:353
  8.6 0.1 collective-permute-start.3
  8.7 1.6 %collective-permute-start.4 = (bf16[10,16,128]{2,1,0:T(8,128)(2,1)S(1)}, bf16[10,16,128]{2,1,0:T(8,128)(2,1)S(1)}, u32[]{:S(2)}, u32[]{:S(2)}) collective-permute-start(bf16[10,16,128]{2,1,0:T(8,128)(2,1)S(1)} %pad_maximum_fusion.1), channel_id=1, source_target_pairs={{4,8},{12,0},{8,4},{0,12},{5,9},{13,1},{9,5},{1,13},{6,10},{14,2},... | collective-permute-start | bytes 122888 | tf_op jit(solution)/shard_map/ppermute | solution.py:353
  10.3 1.1 %collective-permute-done.2.ra_ref = bf16[464,128]{1,0:T(8,128)(2,1)S(1)} collective-permute-done((bf16[464,128]{1,0:T(8,128)(2,1)S(1)}, bf16[464,128]{1,0:T(8,128)(2,1)S(1)}, u32[]{:S(2)}, u32[]{:S(2)}) %collective-permute-start.2) | collective-permute-done | bytes 118816 | tf_op jit(solution)/shard_map/ppermute | solution.py:353
  11.4 0.1 fusion.1
  11.5 3.1 %collective-permute-start.5 = (bf16[464,128]{1,0:T(8,128)(2,1)S(1)}, bf16[464,128]{1,0:T(8,128)(2,1)S(1)}, u32[]{:S(2)}, u32[]{:S(2)}) collective-permute-start(bf16[464,128]{1,0:T(8,128)(2,1)S(1)} %fusion.1), channel_id=1, source_target_pairs={{0,2},{2,0},{1,3},{3,1},{4,6},{6,4},{5,7},{7,5},{8,10},{10,8},{9,1... | collective-permute-start | bytes 356360 | tf_op jit(solution)/shard_map/ppermute | solution.py:448
  14.6 0.0 collective-permute-done.3.refs_0_
  14.6 0.0 collective-permute-done.4.refs_1_
  14.6 0.0 collective-permute-done.halo_ref
  14.6 1.8 %shard_map.48 = (f32[2,8,64,128]{3,2,1,0:T(8,128)S(1)}, f32[2,160,128]{2,1,0:T(8,128)S(1)}, bf16[192,128]{1,0:T(8,128)(2,1)S(1)}, bf16[3,3,128,128]{3,2,1,0:T(8,128)(2,1)S(1)}) custom-call(bf16[8,2,64,128]{3,2,1,0:T(8,128)(2,1)S(1)} %get-tuple-element.29.own_ref, f32[8,128]{1,0:T(8,128)S(1)} %get-tuple-element.26.dec_ref, ...), custom_call_target="tpu_custom_call" | custom-call | flops 301989888 | bytes 4194304 | tf_op jit(solution)/shard_map/pallas_call | solution.py:335
  16.3 1.6 %collective-permute-start.6 = (bf16[192,128]{1,0:T(8,128)(2,1)S(1)}, bf16[192,128]{1,0:T(8,128)(2,1)S(1)}, u32[]{:S(2)}, u32[]{:S(2)}) collective-permute-start(bf16[192,128]{1,0:T(8,128)(2,1)S(1)} %get-tuple-element.41), channel_id=1, source_target_pairs={{0,1},{2,3},{1,0},{3,2},{4,5},{6,7},{5,4},{7,6},{8,9},{10,11},{9,8... | collective-permute-start | bytes 147464 | tf_op jit(solution)/shard_map/ppermute | solution.py:353
  18.0 1.1 %collective-permute-done.5.za_ref = bf16[464,128]{1,0:T(8,128)(2,1)S(1)} collective-permute-done((bf16[464,128]{1,0:T(8,128)(2,1)S(1)}, bf16[464,128]{1,0:T(8,128)(2,1)S(1)}, u32[]{:S(2)}, u32[]{:S(2)}) %collective-permute-start.5) | collective-permute-done | bytes 118816 | tf_op jit(solution)/shard_map/ppermute | solution.py:448
  19.1 1.4 %collective-permute-done.6.rb_ref = bf16[192,128]{1,0:T(8,128)(2,1)S(1)} collective-permute-done((bf16[192,128]{1,0:T(8,128)(2,1)S(1)}, bf16[192,128]{1,0:T(8,128)(2,1)S(1)}, u32[]{:S(2)}, u32[]{:S(2)}) %collective-permute-start.6) | collective-permute-done | bytes 49184 | tf_op jit(solution)/shard_map/ppermute | solution.py:353
  20.5 0.4 %collective-permute-start.7 = (bf16[192,128]{1,0:T(8,128)(2,1)S(1)}, bf16[192,128]{1,0:T(8,128)(2,1)S(1)}, u32[]{:S(2)}, u32[]{:S(2)}) collective-permute-start(bf16[192,128]{1,0:T(8,128)(2,1)S(1)} %fusion.3), channel_id=1, source_target_pairs={{0,2},{2,0},{1,3},{3,1},{4,6},{6,4},{5,7},{7,5},{8,10},{10,8},{9,1... | collective-permute-start | bytes 147464 | tf_op jit(solution)/shard_map/ppermute | solution.py:469
  20.9 4.6 %collective-permute-done.7.zb_ref = bf16[192,128]{1,0:T(8,128)(2,1)S(1)} collective-permute-done((bf16[192,128]{1,0:T(8,128)(2,1)S(1)}, bf16[192,128]{1,0:T(8,128)(2,1)S(1)}, u32[]{:S(2)}, u32[]{:S(2)}) %collective-permute-start.7) | collective-permute-done | bytes 49184 | tf_op jit(solution)/shard_map/ppermute | solution.py:469
  25.6 4.4 %shard_map.49 = bf16[8,8,64,128]{3,2,1,0:T(8,128)(2,1)} custom-call(f32[7,8,64,128]{3,2,1,0:T(8,128)S(1)} %get-tuple-element.28.pa_ref, f32[2,8,64,128]{3,2,1,0:T(8,128)S(1)} %get-tuple-element.39.pb_ref, f32[2,160,128]{2,1,0:T(8,128)S(1)} %get-tuple-element.40.pc_ref, bf16[464,128]{1,0:T(8,128)(2,1)S(1)} %collective-permute-done.2.ra_ref, ...), custom_call_target="tpu_custom_call" | custom-call | flops 1207959552 | bytes 4194304 | tf_op jit(solution)/shard_map/pallas_call | solution.py:335
  (6 shorter events, 0.1 us)
Async XLA Ops:
  1.3 5.1 %collective-permute-start.1 = (bf16[2,32,128]{2,1,0:T(8,128)(2,1)S(1)}, bf16[2,32,128]{2,1,0:T(8,128)(2,1)S(1)}, u32[]{:S(2)}, u32[]{:S(2)}) collective-permute-start(bf16[2,32,128]{2,1,0:T(8,128)(2,1)S(1)} %get-tuple-element.32), channel_id=1, source_target_pairs={{0,16},{16,0},{1,17},{17,1},{2,18},{18,2},{3,19},{19,3},{4,20},{20... | collective-permute-start | bytes 49160 | tf_op jit(solution)/shard_map/ppermute | solution.py:407
  4.3 10.2 %collective-permute-start = (bf16[8,2,64,128]{3,2,1,0:T(8,128)(2,1)S(1)}, bf16[8,2,64,128]{3,2,1,0:T(8,128)(2,1)S(1)}, u32[]{:S(2)}, u32[]{:S(2)}) collective-permute-start(bf16[8,2,64,128]{3,2,1,0:T(8,128)(2,1)S(1)} %get-tuple-element.29.own_ref), channel_id=1, source_target_pairs={{0,16},{16,0},{1,17},{17,1},{2,18},{18,2},{3,19},{19,3},{4,20},{20... | collective-permute-start | bytes 786440 | tf_op jit(solution)/shard_map/ppermute | solution.py:408
  6.5 4.9 %collective-permute-start.2 = (bf16[464,128]{1,0:T(8,128)(2,1)S(1)}, bf16[464,128]{1,0:T(8,128)(2,1)S(1)}, u32[]{:S(2)}, u32[]{:S(2)}) collective-permute-start(bf16[464,128]{1,0:T(8,128)(2,1)S(1)} %get-tuple-element.34), channel_id=1, source_target_pairs={{0,1},{2,3},{1,0},{3,2},{4,5},{6,7},{5,4},{7,6},{8,9},{10,11},{9,8... | collective-permute-start | bytes 356360 | tf_op jit(solution)/shard_map/ppermute | solution.py:353
  8.6 6.0 %collective-permute-start.3 = (bf16[10,16,128]{2,1,0:T(8,128)(2,1)S(1)}, bf16[10,16,128]{2,1,0:T(8,128)(2,1)S(1)}, u32[]{:S(2)}, u32[]{:S(2)}) collective-permute-start(bf16[10,16,128]{2,1,0:T(8,128)(2,1)S(1)} %pad_maximum_fusion), channel_id=1, source_target_pairs={{0,4},{8,12},{4,0},{12,8},{1,5},{9,13},{5,1},{13,9},{2,6},{10,14},... | collective-permute-start | bytes 122888 | tf_op jit(solution)/shard_map/ppermute | solution.py:353
  8.7 5.9 %collective-permute-start.4 = (bf16[10,16,128]{2,1,0:T(8,128)(2,1)S(1)}, bf16[10,16,128]{2,1,0:T(8,128)(2,1)S(1)}, u32[]{:S(2)}, u32[]{:S(2)}) collective-permute-start(bf16[10,16,128]{2,1,0:T(8,128)(2,1)S(1)} %pad_maximum_fusion.1), channel_id=1, source_target_pairs={{4,8},{12,0},{8,4},{0,12},{5,9},{13,1},{9,5},{1,13},{6,10},{14,2},... | collective-permute-start | bytes 122888 | tf_op jit(solution)/shard_map/ppermute | solution.py:353
  11.5 7.6 %collective-permute-start.5 = (bf16[464,128]{1,0:T(8,128)(2,1)S(1)}, bf16[464,128]{1,0:T(8,128)(2,1)S(1)}, u32[]{:S(2)}, u32[]{:S(2)}) collective-permute-start(bf16[464,128]{1,0:T(8,128)(2,1)S(1)} %fusion.1), channel_id=1, source_target_pairs={{0,2},{2,0},{1,3},{3,1},{4,6},{6,4},{5,7},{7,5},{8,10},{10,8},{9,1... | collective-permute-start | bytes 356360 | tf_op jit(solution)/shard_map/ppermute | solution.py:448
  16.3 4.2 %collective-permute-start.6 = (bf16[192,128]{1,0:T(8,128)(2,1)S(1)}, bf16[192,128]{1,0:T(8,128)(2,1)S(1)}, u32[]{:S(2)}, u32[]{:S(2)}) collective-permute-start(bf16[192,128]{1,0:T(8,128)(2,1)S(1)} %get-tuple-element.41), channel_id=1, source_target_pairs={{0,1},{2,3},{1,0},{3,2},{4,5},{6,7},{5,4},{7,6},{8,9},{10,11},{9,8... | collective-permute-start | bytes 147464 | tf_op jit(solution)/shard_map/ppermute | solution.py:353
  20.5 5.1 %collective-permute-start.7 = (bf16[192,128]{1,0:T(8,128)(2,1)S(1)}, bf16[192,128]{1,0:T(8,128)(2,1)S(1)}, u32[]{:S(2)}, u32[]{:S(2)}) collective-permute-start(bf16[192,128]{1,0:T(8,128)(2,1)S(1)} %fusion.3), channel_id=1, source_target_pairs={{0,2},{2,0},{1,3},{3,1},{4,6},{6,4},{5,7},{7,5},{8,10},{10,8},{9,1... | collective-permute-start | bytes 147464 | tf_op jit(solution)/shard_map/ppermute | solution.py:469

commit v7 on v6

--- a/solution.py
+++ b/solution.py
@@ -104,6 +104,17 @@
         copy.wait()
 
 
+def addends(decays, rows):
+    total = decays[0:1]
+    for f in range(1, decays.shape[0]):
+        total = total * decays[f : f + 1]
+    high = total.astype(BF16).astype(F32)
+    middle = (total - high).astype(BF16).astype(F32)
+    low = total - high - middle
+    row = lax.broadcasted_iota(jnp.int32, (rows, decays.shape[1]), 0)
+    return jnp.where(row == 0, high, jnp.where(row == 1, middle, jnp.where(row == 2, low, 0.0)))
+
+
 def inner_kernel(two, frames_ref, dec_ref, w_ref, p_ref, f_ref, wt, rowbuf, x3):
     frames, height, across, chan = frames_ref.shape
     flip = mirrored(two)
@@ -131,17 +142,8 @@
             at = base + rr - first_row
             if at >= 0:
                 f_ref[at * across : (at + 1) * across, :] = s.astype(BF16)
-    total = decays[0:1]
-    for f in range(1, frames):
-        total = total * decays[f : f + 1]
-    high = total.astype(BF16)
-    rest = total - high.astype(F32)
-    middle = rest.astype(BF16)
-    low = rest - middle.astype(F32)
-    row = lax.broadcasted_iota(jnp.int32, (16, chan), 0)
-    parts = jnp.where(row == 0, high.astype(F32), jnp.where(row == 1, middle.astype(F32), jnp.where(row == 2, low, 0.0)))
     end = f_ref.shape[0]
-    f_ref[end - 16 : end, :] = parts.astype(BF16)
+    f_ref[end - 16 : end, :] = addends(decays, 16).astype(BF16)
 
 
 def edge_kernel(two, gx, gy, own_ref, dec_ref, w_ref, halo_ref, e_ref, corner_ref, *refs):
@@ -242,7 +244,7 @@
         for h in range(2):
             pc_ref[h, pl.ds(f, count, stride=frames), :] = s[:, h * chan : (h + 1) * chan]
     base = len(pairs) * 2 * across
-    pad = jnp.zeros((32 - count, chan), F32)
+    pad = jnp.concatenate([jnp.zeros((24 - count, chan), F32), addends(decays, 8)], axis=0)
     for h in range(2):
         half = jnp.concatenate([s[:, h * chan : (h + 1) * chan], pad], axis=0)
         f_ref[base + 32 * h : base + 32 * (h + 1), :] = half.astype(BF16)
@@ -250,7 +252,7 @@
 
 
 def outer_kernel(
-    two, ta, pa_ref, pb_ref, pc_ref, ra_ref, za_ref, rb_ref, zb_ref, dec_ref, w_ref, frames_hbm,
+    two, ta, pa_ref, pb_ref, pc_ref, ra_ref, za_ref, b1_ref, b2_ref, b3_ref, dec_ref, w_ref, frames_hbm,
     out_ref, frames_ref, wt, rowbuf, x3, sc, ia, ib, done, sems,
 ):
     frames, height, across, chan = frames_ref.shape
@@ -260,21 +262,28 @@
     pair_weights(w_ref, wt, flip)
     decays = dec_ref[...]
     rows_a = pa_ref.shape[0]
+    base = pb_ref.shape[0] * across
+
+    def product(ref, at):
+        return jnp.sum(ref[at : at + 16, :].astype(F32)[8:16], axis=0, keepdims=True)
+
     if ta == 4:
         t = lax.axis_index("ta")
         end = ra_ref.shape[0]
         other = jnp.sum(ra_ref[end - 16 : end, :].astype(F32), axis=0, keepdims=True)
-        alpha = ((t == 1) | (t == 3)).astype(F32)
-        beta = jnp.where(t == 3, other, (t == 2).astype(F32))
+        last = (t == 3).astype(F32)
+        one, two_on = ((t == 1) | (t == 3)).astype(F32), (t == 2).astype(F32)
+        from_a = one, two_on + last * other
+        d1, d2, d3 = (product(ref, base + 16) for ref in (b1_ref, b2_ref, b3_ref))
+        from_b = one, two_on * d3 + last * d1, two_on + last * d1 * d2
     else:
-        alpha, beta = 1.0, 0.0
-    ia[...] = alpha * ra_ref[0 : rows_a * across].astype(F32) + beta * za_ref[0 : rows_a * across].astype(F32)
-    ib[...] = alpha * rb_ref[...].astype(F32) + beta * zb_ref[...].astype(F32)
+        from_a, from_b = (1.0, 0.0), (1.0, 0.0, 0.0)
+    ia[...] = sum(c * ref[0 : rows_a * across].astype(F32) for c, ref in zip(from_a, (ra_ref, za_ref)))
+    ib[...] = sum(c * ref[...].astype(F32) for c, ref in zip(from_b, (b1_ref, b2_ref, b3_ref)))
     running = [decays[0:1]]
     for f in range(1, frames):
         running.append(running[-1] * decays[f : f + 1])
     count = (height // 2 + 1) * 4
-    base = pb_ref.shape[0] * across
     for f in range(frames):
         for h in range(2):
             part = pc_ref[h, pl.ds(f, count, stride=frames), :]
@@ -465,11 +474,10 @@
         flops * rows_b, [sent[1] if two else frames, decays, w_in, halo, cols, corner, *sides], [out_weight],
     )
     if ta == 4:
-        za, rb = lax.optimization_barrier((za, swapped(fb, "ta", ta, False)))
-        zb = lax.ppermute(joined(fb, rb), "ta", across_two)
+        edges = [swapped(fb, "ta", ta, False), lax.ppermute(fb, "ta", across_two), swapped(fb, "ta", ta, True)]
     else:
         ra, rb = carry_general([fa, fb], total, ta)
-        za, zb = ra, rb
+        za, edges = ra, [rb] * 3
 
     return call(
         functools.partial(outer_kernel, two, ta),
@@ -480,7 +488,7 @@
             pltpu.VMEM((rows_a * across, chan), F32), pltpu.VMEM((rows_b * across + 64, chan), F32),
             pltpu.VMEM((height // 2, n_frames, 2, across, chan), BF16), pltpu.SemaphoreType.DMA((1 + height // 2,)),
         ],
-        flops * height, [pa, pb, pc, ra, za, rb, zb, decays, w_out], [frames_far], HBM,
+        flops * height, [pa, pb, pc, ra, za, *edges, decays, w_out], [frames_far], HBM,
     )
 
 

time: 30.2 us -> 28.4 us (0.940)
  waiting for transfers between devices: 8.25 us -> 4.13 us
  starting transfers between devices: 12 us -> 14.4 us
    ppermute x1, waiting for transfers between devices: 4.65 us -> 0.94 us  [on_device(): lax.ppermute(fb, 'ta', across_two)]
    ppermute x1, starting transfers between devices: 0.41 us -> 1.69 us  [on_device(): lax.ppermute(fb, 'ta', across_two)]
    ppermute x1, waiting for transfers between devices: 1.13 us -> 0.01 us  [on_device(): za = lax.ppermute(ga, 'ta', across_two)]
    ppermute x4 -> x5, starting transfers between devices: 5.44 us -> 6.56 us  [swapped(): return lax.ppermute(value, axis, pairs + [(b, a) for a, b in pairs])]
    ppermute x4 -> x5, waiting for transfers between devices: 2.46 us -> 3.19 us  [swapped(): return lax.ppermute(value, axis, pairs + [(b, a) for a, b in pairs])]
  transfers between devices with their start and end apart: 8 -> 9, of which waited for: 4 -> 4; matrix products, arithmetic and copies ran while one was open for 0% -> 0% of each run, Pallas kernels for 12% -> 13%
where the time goes in v7:
time: 28.4 us; the launch traced here: 28.2 us
  starting transfers between devices  14.4 us (51%)
  Pallas kernels  9.46 us (33%)
  waiting for transfers between devices  4.13 us (15%)
    pallas_call x4, Pallas kernels, call(): pl.pallas_call(body, out_shape=outs, in_specs=[VMEM] * len(near) + [HBM]...  9.46 us
    ppermute x5, starting transfers between devices, swapped(): return lax.ppermute(value, axis, pairs + [(b, a) for a, b in pairs])  6.56 us
    ppermute x5, waiting for transfers between devices, swapped(): return lax.ppermute(value, axis, pairs + [(b, a) for a, b in pairs])  3.19 us
    ppermute x1, starting transfers between devices, on_device(): za = lax.ppermute(ga, 'ta', across_two)  3.1 us
    ppermute x1, starting transfers between devices, on_device(): corner = lax.ppermute(sent[0], 'gx', facing)  3 us
    ppermute x1, starting transfers between devices, on_device(): lax.ppermute(fb, 'ta', across_two)  1.69 us
    ppermute x1, waiting for transfers between devices, on_device(): lax.ppermute(fb, 'ta', across_two)  0.94 us
  transfers between devices with their start and end apart: 9, of which 4 were waited for; matrix products, arithmetic and copies ran while one was open for 0% of the time, Pallas kernels for 13%

profile of v7, /device:TPU:0, one launch (start us, length us, event | category | flops | bytes accessed | tf_op | source)
XLA Modules:
  0.0 28.2 jit_solution(15840995290878142242)
XLA Ops:
  0.0 1.3 %shard_map.46 = (bf16[8,8,64,128]{3,2,1,0:T(8,128)(2,1)S(1)}, f32[8,128]{1,0:T(8,128)S(1)}, bf16[3,3,128,128]{3,2,1,0:T(8,128)(2,1)S(1)}, bf16[8,32,128]{2,1,0:T...) custom-call(bf16[8,8,64,128]{3,2,1,0:T(8,128)(2,1)} %frames_hbm.3, ...), custom_call_target="tpu_custom_call" | custom-call | bytes 4194304 | tf_op jit(solution)/shard_map/pallas_call | solution.py:344
  1.3 3.0 %collective-permute-start.1 = (bf16[2,32,128]{2,1,0:T(8,128)(2,1)S(1)}, bf16[2,32,128]{2,1,0:T(8,128)(2,1)S(1)}, u32[]{:S(2)}, u32[]{:S(2)}) collective-permute-start(bf16[2,32,128]{2,1,0:T(8,128)(2,1)S(1)} %get-tuple-element.30), channel_id=1, source_target_pairs={{0,16},{16,0},{1,17},{17,1},{2,18},{18,2},{3,19},{19,3},{4,20},{20... | collective-permute-start | bytes 49160 | tf_op jit(solution)/shard_map/ppermute | solution.py:416
  4.3 0.1 collective-permute-start
  4.4 2.0 %shard_map.47 = (f32[7,8,64,128]{3,2,1,0:T(8,128)S(1)}, bf16[464,128]{1,0:T(8,128)(2,1)S(1)}) custom-call(bf16[8,8,64,128]{3,2,1,0:T(8,128)(2,1)S(1)} %get-tuple-element.23.frames_ref, f32[8,128]{1,0:T(8,128)S(1)} %get-tuple-element.24.dec_ref, bf16[3,3,128,128]{3,2,1,0:T(8,128)(2,1)S(1)} %get-tuple-element.25.w_ref), custom_call_target="tpu_custom_call" | custom-call | flops 1207959552 | bytes 4194304 | tf_op jit(solution)/shard_map/pallas_call | solution.py:344
  6.4 0.0 collective-permute-done.1.corner_ref
  6.5 2.1 %collective-permute-start.2 = (bf16[464,128]{1,0:T(8,128)(2,1)S(1)}, bf16[464,128]{1,0:T(8,128)(2,1)S(1)}, u32[]{:S(2)}, u32[]{:S(2)}) collective-permute-start(bf16[464,128]{1,0:T(8,128)(2,1)S(1)} %get-tuple-element.32), channel_id=1, source_target_pairs={{0,1},{2,3},{1,0},{3,2},{4,5},{6,7},{5,4},{7,6},{8,9},{10,11},{9,8... | collective-permute-start | bytes 356360 | tf_op jit(solution)/shard_map/ppermute | solution.py:362
  8.6 0.1 collective-permute-start.3
  8.7 1.6 %collective-permute-start.4 = (bf16[10,16,128]{2,1,0:T(8,128)(2,1)S(1)}, bf16[10,16,128]{2,1,0:T(8,128)(2,1)S(1)}, u32[]{:S(2)}, u32[]{:S(2)}) collective-permute-start(bf16[10,16,128]{2,1,0:T(8,128)(2,1)S(1)} %pad_maximum_fusion.1), channel_id=1, source_target_pairs={{4,8},{12,0},{8,4},{0,12},{5,9},{13,1},{9,5},{1,13},{6,10},{14,2},... | collective-permute-start | bytes 122888 | tf_op jit(solution)/shard_map/ppermute | solution.py:362
  10.3 1.1 %collective-permute-done.2.ra_ref = bf16[464,128]{1,0:T(8,128)(2,1)S(1)} collective-permute-done((bf16[464,128]{1,0:T(8,128)(2,1)S(1)}, bf16[464,128]{1,0:T(8,128)(2,1)S(1)}, u32[]{:S(2)}, u32[]{:S(2)}) %collective-permute-start.2) | collective-permute-done | bytes 118816 | tf_op jit(solution)/shard_map/ppermute | solution.py:362
  11.4 0.1 fusion.1
  11.5 3.1 %collective-permute-start.5 = (bf16[464,128]{1,0:T(8,128)(2,1)S(1)}, bf16[464,128]{1,0:T(8,128)(2,1)S(1)}, u32[]{:S(2)}, u32[]{:S(2)}) collective-permute-start(bf16[464,128]{1,0:T(8,128)(2,1)S(1)} %fusion.1), channel_id=1, source_target_pairs={{0,2},{2,0},{1,3},{3,1},{4,6},{6,4},{5,7},{7,5},{8,10},{10,8},{9,1... | collective-permute-start | bytes 356360 | tf_op jit(solution)/shard_map/ppermute | solution.py:457
  14.6 0.0 collective-permute-done.3.refs_0_
  14.6 0.0 collective-permute-done.4.refs_1_
  14.6 0.0 collective-permute-done.halo_ref
  14.6 1.8 %shard_map.48 = (f32[2,8,64,128]{3,2,1,0:T(8,128)S(1)}, f32[2,160,128]{2,1,0:T(8,128)S(1)}, bf16[192,128]{1,0:T(8,128)(2,1)S(1)}, bf16[3,3,128,128]{3,2,1,0:T(8,128)(2,1)S(1)}) custom-call(bf16[8,2,64,128]{3,2,1,0:T(8,128)(2,1)S(1)} %get-tuple-element.27.own_ref, f32[8,128]{1,0:T(8,128)S(1)} %get-tuple-element.24.dec_ref, ...), custom_call_target="tpu_custom_call" | custom-call | flops 301989888 | bytes 4194304 | tf_op jit(solution)/shard_map/pallas_call | solution.py:344
  16.3 1.4 %collective-permute-start.8 = (bf16[192,128]{1,0:T(8,128)(2,1)S(1)}, bf16[192,128]{1,0:T(8,128)(2,1)S(1)}, u32[]{:S(2)}, u32[]{:S(2)}) collective-permute-start(bf16[192,128]{1,0:T(8,128)(2,1)S(1)} %get-tuple-element.39), channel_id=1, source_target_pairs={{1,2},{3,0},{2,1},{0,3},{5,6},{7,4},{6,5},{4,7},{9,10},{11,8},{10,... | collective-permute-start | bytes 147464 | tf_op jit(solution)/shard_map/ppermute | solution.py:362
  17.7 1.7 %collective-permute-start.7 = (bf16[192,128]{1,0:T(8,128)(2,1)S(1)}, bf16[192,128]{1,0:T(8,128)(2,1)S(1)}, u32[]{:S(2)}, u32[]{:S(2)}) collective-permute-start(bf16[192,128]{1,0:T(8,128)(2,1)S(1)} %get-tuple-element.39), channel_id=1, source_target_pairs={{0,2},{2,0},{1,3},{3,1},{4,6},{6,4},{5,7},{7,5},{8,10},{10,8},{9,1... | collective-permute-start | bytes 147464 | tf_op jit(solution)/shard_map/ppermute | solution.py:477
  19.4 1.3 %collective-permute-start.6 = (bf16[192,128]{1,0:T(8,128)(2,1)S(1)}, bf16[192,128]{1,0:T(8,128)(2,1)S(1)}, u32[]{:S(2)}, u32[]{:S(2)}) collective-permute-start(bf16[192,128]{1,0:T(8,128)(2,1)S(1)} %get-tuple-element.39), channel_id=1, source_target_pairs={{0,1},{2,3},{1,0},{3,2},{4,5},{6,7},{5,4},{7,6},{8,9},{10,11},{9,8... | collective-permute-start | bytes 147464 | tf_op jit(solution)/shard_map/ppermute | solution.py:362
  20.8 0.0 collective-permute-done.5.za_ref
  20.8 1.9 %collective-permute-done.8.b3_ref = bf16[192,128]{1,0:T(8,128)(2,1)S(1)} collective-permute-done((bf16[192,128]{1,0:T(8,128)(2,1)S(1)}, bf16[192,128]{1,0:T(8,128)(2,1)S(1)}, u32[]{:S(2)}, u32[]{:S(2)}) %collective-permute-start.8) | collective-permute-done | bytes 49184 | tf_op jit(solution)/shard_map/ppermute | solution.py:362
  22.7 0.9 %collective-permute-done.7.b2_ref = bf16[192,128]{1,0:T(8,128)(2,1)S(1)} collective-permute-done((bf16[192,128]{1,0:T(8,128)(2,1)S(1)}, bf16[192,128]{1,0:T(8,128)(2,1)S(1)}, u32[]{:S(2)}, u32[]{:S(2)}) %collective-permute-start.7) | collective-permute-done | bytes 49184 | tf_op jit(solution)/shard_map/ppermute | solution.py:477
  23.7 0.2 collective-permute-done.6.b1_ref
  23.8 4.4 %shard_map.49 = bf16[8,8,64,128]{3,2,1,0:T(8,128)(2,1)} custom-call(f32[7,8,64,128]{3,2,1,0:T(8,128)S(1)} %get-tuple-element.26.pa_ref, f32[2,8,64,128]{3,2,1,0:T(8,128)S(1)} %get-tuple-element.37.pb_ref, f32[2,160,128]{2,1,0:T(8,128)S(1)} %get-tuple-element.38.pc_ref, bf16[464,128]{1,0:T(8,128)(2,1)S(1)} %collective-permute-done.2.ra_ref, ...), custom_call_target="tpu_custom_call" | custom-call | flops 1207959552 | bytes 4194304 | tf_op jit(solution)/shard_map/pallas_call | solution.py:344
  (5 shorter events, 0.1 us)
Async XLA Ops:
  1.3 5.1 %collective-permute-start.1 = (bf16[2,32,128]{2,1,0:T(8,128)(2,1)S(1)}, bf16[2,32,128]{2,1,0:T(8,128)(2,1)S(1)}, u32[]{:S(2)}, u32[]{:S(2)}) collective-permute-start(bf16[2,32,128]{2,1,0:T(8,128)(2,1)S(1)} %get-tuple-element.30), channel_id=1, source_target_pairs={{0,16},{16,0},{1,17},{17,1},{2,18},{18,2},{3,19},{19,3},{4,20},{20... | collective-permute-start | bytes 49160 | tf_op jit(solution)/shard_map/ppermute | solution.py:416
  4.3 10.2 %collective-permute-start = (bf16[8,2,64,128]{3,2,1,0:T(8,128)(2,1)S(1)}, bf16[8,2,64,128]{3,2,1,0:T(8,128)(2,1)S(1)}, u32[]{:S(2)}, u32[]{:S(2)}) collective-permute-start(bf16[8,2,64,128]{3,2,1,0:T(8,128)(2,1)S(1)} %get-tuple-element.27.own_ref), channel_id=1, source_target_pairs={{0,16},{16,0},{1,17},{17,1},{2,18},{18,2},{3,19},{19,3},{4,20},{20... | collective-permute-start | bytes 786440 | tf_op jit(solution)/shard_map/ppermute | solution.py:417
  6.5 4.9 %collective-permute-start.2 = (bf16[464,128]{1,0:T(8,128)(2,1)S(1)}, bf16[464,128]{1,0:T(8,128)(2,1)S(1)}, u32[]{:S(2)}, u32[]{:S(2)}) collective-permute-start(bf16[464,128]{1,0:T(8,128)(2,1)S(1)} %get-tuple-element.32), channel_id=1, source_target_pairs={{0,1},{2,3},{1,0},{3,2},{4,5},{6,7},{5,4},{7,6},{8,9},{10,11},{9,8... | collective-permute-start | bytes 356360 | tf_op jit(solution)/shard_map/ppermute | solution.py:362
  8.6 6.0 %collective-permute-start.3 = (bf16[10,16,128]{2,1,0:T(8,128)(2,1)S(1)}, bf16[10,16,128]{2,1,0:T(8,128)(2,1)S(1)}, u32[]{:S(2)}, u32[]{:S(2)}) collective-permute-start(bf16[10,16,128]{2,1,0:T(8,128)(2,1)S(1)} %pad_maximum_fusion), channel_id=1, source_target_pairs={{0,4},{8,12},{4,0},{12,8},{1,5},{9,13},{5,1},{13,9},{2,6},{10,14},... | collective-permute-start | bytes 122888 | tf_op jit(solution)/shard_map/ppermute | solution.py:362
  8.7 5.9 %collective-permute-start.4 = (bf16[10,16,128]{2,1,0:T(8,128)(2,1)S(1)}, bf16[10,16,128]{2,1,0:T(8,128)(2,1)S(1)}, u32[]{:S(2)}, u32[]{:S(2)}) collective-permute-start(bf16[10,16,128]{2,1,0:T(8,128)(2,1)S(1)} %pad_maximum_fusion.1), channel_id=1, source_target_pairs={{4,8},{12,0},{8,4},{0,12},{5,9},{13,1},{9,5},{1,13},{6,10},{14,2},... | collective-permute-start | bytes 122888 | tf_op jit(solution)/shard_map/ppermute | solution.py:362
  11.5 9.3 %collective-permute-start.5 = (bf16[464,128]{1,0:T(8,128)(2,1)S(1)}, bf16[464,128]{1,0:T(8,128)(2,1)S(1)}, u32[]{:S(2)}, u32[]{:S(2)}) collective-permute-start(bf16[464,128]{1,0:T(8,128)(2,1)S(1)} %fusion.1), channel_id=1, source_target_pairs={{0,2},{2,0},{1,3},{3,1},{4,6},{6,4},{5,7},{7,5},{8,10},{10,8},{9,1... | collective-permute-start | bytes 356360 | tf_op jit(solution)/shard_map/ppermute | solution.py:457
  16.3 6.4 %collective-permute-start.8 = (bf16[192,128]{1,0:T(8,128)(2,1)S(1)}, bf16[192,128]{1,0:T(8,128)(2,1)S(1)}, u32[]{:S(2)}, u32[]{:S(2)}) collective-permute-start(bf16[192,128]{1,0:T(8,128)(2,1)S(1)} %get-tuple-element.39), channel_id=1, source_target_pairs={{1,2},{3,0},{2,1},{0,3},{5,6},{7,4},{6,5},{4,7},{9,10},{11,8},{10,... | collective-permute-start | bytes 147464 | tf_op jit(solution)/shard_map/ppermute | solution.py:362
  17.7 5.9 %collective-permute-start.7 = (bf16[192,128]{1,0:T(8,128)(2,1)S(1)}, bf16[192,128]{1,0:T(8,128)(2,1)S(1)}, u32[]{:S(2)}, u32[]{:S(2)}) collective-permute-start(bf16[192,128]{1,0:T(8,128)(2,1)S(1)} %get-tuple-element.39), channel_id=1, source_target_pairs={{0,2},{2,0},{1,3},{3,1},{4,6},{6,4},{5,7},{7,5},{8,10},{10,8},{9,1... | collective-permute-start | bytes 147464 | tf_op jit(solution)/shard_map/ppermute | solution.py:477
  19.4 4.4 %collective-permute-start.6 = (bf16[192,128]{1,0:T(8,128)(2,1)S(1)}, bf16[192,128]{1,0:T(8,128)(2,1)S(1)}, u32[]{:S(2)}, u32[]{:S(2)}) collective-permute-start(bf16[192,128]{1,0:T(8,128)(2,1)S(1)} %get-tuple-element.39), channel_id=1, source_target_pairs={{0,1},{2,3},{1,0},{3,2},{4,5},{6,7},{5,4},{7,6},{8,9},{10,11},{9,8... | collective-permute-start | bytes 147464 | tf_op jit(solution)/shard_map/ppermute | solution.py:362

commit v8 on v7

--- a/solution.py
+++ b/solution.py
@@ -136,7 +136,7 @@
 
         def keep(rr, f, s, base=base):
             if base + rr >= first_row:
-                p_ref[base + rr - first_row, f] = s
+                p_ref[base + rr - first_row, f] = s.astype(BF16)
 
         for rr, s in enumerate(scan_rows(y, decays, scales, across, keep)):
             at = base + rr - first_row
@@ -147,8 +147,8 @@
 
 
 def edge_kernel(two, gx, gy, own_ref, dec_ref, w_ref, halo_ref, e_ref, corner_ref, *refs):
-    *sides, next_hbm, p_ref, pc_ref, f_ref, next_ref, wt, rowbuf, x3, xc, yc, sem = refs
-    fetch = pltpu.make_async_copy(next_hbm, next_ref, sem)
+    *sides, next_hbm, p_ref, pc_ref, f_ref, next_wt, next_w, wt, rowbuf, x3, xc, yc, sem = refs
+    fetch = pltpu.make_async_copy(next_hbm, next_w, sem)
     fetch.start()
     frames, across, chan = own_ref.shape[0], *own_ref.shape[2:]
     height = e_ref.shape[0] if two else own_ref.shape[1]
@@ -249,17 +249,15 @@
         half = jnp.concatenate([s[:, h * chan : (h + 1) * chan], pad], axis=0)
         f_ref[base + 32 * h : base + 32 * (h + 1), :] = half.astype(BF16)
     fetch.wait()
+    pair_weights(next_w, next_wt, flip)
 
 
 def outer_kernel(
-    two, ta, pa_ref, pb_ref, pc_ref, ra_ref, za_ref, b1_ref, b2_ref, b3_ref, dec_ref, w_ref, frames_hbm,
-    out_ref, frames_ref, wt, rowbuf, x3, sc, ia, ib, done, sems,
+    two, ta, pa_ref, pb_ref, pc_ref, ra_ref, za_ref, b1_ref, b2_ref, b3_ref, dec_ref, wt, frames_ref,
+    out_ref, rowbuf, x3, sc, ia, ib, done, sems,
 ):
     frames, height, across, chan = frames_ref.shape
-    fetch = pltpu.make_async_copy(frames_hbm, frames_ref, sems.at[0])
-    fetch.start()
     flip = mirrored(two)
-    pair_weights(w_ref, wt, flip)
     decays = dec_ref[...]
     rows_a = pa_ref.shape[0]
     base = pb_ref.shape[0] * across
@@ -300,13 +298,11 @@
         incoming = src[1][at * across : (at + 1) * across, :]
         for f in range(frames):
             slot = (n * frames + f) % rowbuf.shape[0]
-            rowbuf[slot, 8 : 8 + across, :] = src[0][at, f] + running[f] * incoming
+            rowbuf[slot, 8 : 8 + across, :] = src[0][at, f].astype(F32) + running[f] * incoming
             corner = (n // 2) * 4
             h = n % 2
-            rowbuf[slot, 7:8, :] = sc[f, h, corner : corner + 1, :]
-            rowbuf[slot, 8:9, :] = sc[f, h, corner + 1 : corner + 2, :]
-            rowbuf[slot, 7 + across : 8 + across, :] = sc[f, h, corner + 2 : corner + 3, :]
-            rowbuf[slot, 8 + across : 9 + across, :] = sc[f, h, corner + 3 : corner + 4, :]
+            rowbuf[slot, 7:9, :] = sc[f, h, corner : corner + 2, :]
+            rowbuf[slot, 7 + across : 9 + across, :] = sc[f, h, corner + 2 : corner + 4, :]
             three_taps(rowbuf, slot, x3, n, f, rowbuf[slot, 8 : 8 + across, :].astype(BF16))
 
     def finish(p, y):
@@ -317,23 +313,18 @@
                 mixed = y[f * across : (f + 1) * across, rr * chan : (rr + 1) * chan]
                 frame = frames_ref[f, first + row].astype(F32)
                 done[p, f, row] = (frame + jax.nn.gelu(mixed)).astype(BF16)
-        copy = pltpu.make_async_copy(done.at[p], out_ref.at[:, pl.ds(first, 2)], sems.at[1 + p])
+        copy = pltpu.make_async_copy(done.at[p], out_ref.at[:, pl.ds(first, 2)], sems.at[p])
         copy.start()
         return copy
 
-    copies, waiting = [], []
+    copies = []
     for n in range(2):
         build(n)
     for p in range(height // 2):
         build(2 * p + 2)
         build(2 * p + 3)
         slots = [n if n > 0 or not two else None for n in range(2 * p, 2 * p + 4)]
-        waiting.append((p, pair_dot(x3, slots, wt)))
-        if p == 1:
-            fetch.wait()
-        if p >= 1:
-            copies += [finish(*w) for w in waiting]
-            waiting = []
+        copies.append(finish(p, pair_dot(x3, slots, wt)))
     for copy in copies:
         copy.wait()
 
@@ -431,7 +422,7 @@
     flops = 2 * 9 * chan * chan * cells
     pa, fa = call(
         functools.partial(inner_kernel, two),
-        (near_mem((rows_a, n_frames, across, chan), F32), near_mem((rows_a * across + 16, chan), BF16)),
+        (near_mem((rows_a, n_frames, across, chan), BF16), near_mem((rows_a * across + 16, chan), BF16)),
         [wt, rowbuf, pltpu.VMEM((height, cells, 3 * chan), BF16)],
         flops * height, [frames, decays, w_in],
     )
@@ -458,16 +449,16 @@
         _, *sides = lax.optimization_barrier((ga, *sides))
 
     n_cols = (height // 2 + 1) * 4
-    pb, pc, fb, w_out = call(
+    pb, pc, fb, wt_out = call(
         functools.partial(edge_kernel, two, gx, gy),
         (
             near_mem((rows_b, n_frames, across, chan), F32),
             near_mem((2, n_cols * n_frames, chan), F32),
             near_mem((rows_b * across + 64, chan), BF16),
-            near_mem(out_weight.shape, BF16),
+            near_mem((12 * chan, 2 * chan), BF16),
         ),
         [
-            wt, rowbuf, pltpu.VMEM((2 * rows_b, cells, 3 * chan), BF16),
+            pltpu.VMEM(out_weight.shape, BF16), wt, rowbuf, pltpu.VMEM((2 * rows_b, cells, 3 * chan), BF16),
             pltpu.VMEM((n_cols * n_frames, 12 * chan), BF16), pltpu.VMEM((2, n_cols * n_frames, chan), F32),
             pltpu.SemaphoreType.DMA,
         ],
@@ -483,12 +474,12 @@
         functools.partial(outer_kernel, two, ta),
         jax.ShapeDtypeStruct(frames.shape, BF16),
         [
-            pltpu.VMEM(frames.shape, BF16), wt, rowbuf, pltpu.VMEM((height + 2, cells, 3 * chan), BF16),
+            rowbuf, pltpu.VMEM((height + 2, cells, 3 * chan), BF16),
             pltpu.VMEM((n_frames, 2, (n_cols + 7) // 8 * 8, chan), F32),
             pltpu.VMEM((rows_a * across, chan), F32), pltpu.VMEM((rows_b * across + 64, chan), F32),
-            pltpu.VMEM((height // 2, n_frames, 2, across, chan), BF16), pltpu.SemaphoreType.DMA((1 + height // 2,)),
+            pltpu.VMEM((height // 2, n_frames, 2, across, chan), BF16), pltpu.SemaphoreType.DMA((height // 2,)),
         ],
-        flops * height, [pa, pb, pc, ra, za, *edges, decays, w_out], [frames_far], HBM,
+        flops * height, [pa, pb, pc, ra, za, *edges, decays, wt_out, frames], out_place=HBM,
     )
 
 

time: 28.4 us -> 27.6 us (0.972)
  Pallas kernels: 9.46 us -> 8.65 us
    pallas_call x4, Pallas kernels: 9.46 us -> 8.65 us  [call(): pl.pallas_call(body, out_shape=outs, in_specs=[VMEM] * len(near) + [HBM]...]
  transfers between devices with their start and end apart: 9 -> 9, of which waited for: 4 -> 4; matrix products, arithmetic and copies ran while one was open for 0% -> 0% of each run, Pallas kernels for 13% -> 14%
where the time goes in v8:
time: 27.6 us; the launch traced here: 27.4 us
  starting transfers between devices  14.4 us (52%)
  Pallas kernels  8.65 us (31%)
  waiting for transfers between devices  4.13 us (15%)
    pallas_call x4, Pallas kernels, call(): pl.pallas_call(body, out_shape=outs, in_specs=[VMEM] * len(near) + [HBM]...  8.65 us
    ppermute x5, starting transfers between devices, swapped(): return lax.ppermute(value, axis, pairs + [(b, a) for a, b in pairs])  6.56 us
    ppermute x5, waiting for transfers between devices, swapped(): return lax.ppermute(value, axis, pairs + [(b, a) for a, b in pairs])  3.19 us
    ppermute x1, starting transfers between devices, on_device(): za = lax.ppermute(ga, 'ta', across_two)  3.1 us
    ppermute x1, starting transfers between devices, on_device(): corner = lax.ppermute(sent[0], 'gx', facing)  3 us
    ppermute x1, starting transfers between devices, on_device(): lax.ppermute(fb, 'ta', across_two)  1.69 us
    ppermute x1, waiting for transfers between devices, on_device(): lax.ppermute(fb, 'ta', across_two)  0.94 us
  transfers between devices with their start and end apart: 9, of which 4 were waited for; matrix products, arithmetic and copies ran while one was open for 0% of the time, Pallas kernels for 14%

profile of v8, /device:TPU:0, one launch (start us, length us, event | category | flops | bytes accessed | tf_op | source)
XLA Modules:
  0.0 27.4 jit_solution(15527028635322039431)
XLA Ops:
  0.0 1.3 %shard_map.46 = (bf16[8,8,64,128]{3,2,1,0:T(8,128)(2,1)S(1)}, f32[8,128]{1,0:T(8,128)S(1)}, bf16[3,3,128,128]{3,2,1,0:T(8,128)(2,1)S(1)}, bf16[8,32,128]{2,1,0:T...) custom-call(bf16[8,8,64,128]{3,2,1,0:T(8,128)(2,1)} %frames_hbm.1, ...), custom_call_target="tpu_custom_call" | custom-call | bytes 4194304 | tf_op jit(solution)/shard_map/pallas_call | solution.py:335
  1.3 3.0 %collective-permute-start.1 = (bf16[2,32,128]{2,1,0:T(8,128)(2,1)S(1)}, bf16[2,32,128]{2,1,0:T(8,128)(2,1)S(1)}, u32[]{:S(2)}, u32[]{:S(2)}) collective-permute-start(bf16[2,32,128]{2,1,0:T(8,128)(2,1)S(1)} %get-tuple-element.30), channel_id=1, source_target_pairs={{0,16},{16,0},{1,17},{17,1},{2,18},{18,2},{3,19},{19,3},{4,20},{20... | collective-permute-start | bytes 49160 | tf_op jit(solution)/shard_map/ppermute | solution.py:407
  4.3 0.1 collective-permute-start
  4.4 2.0 %shard_map.47 = (bf16[7,8,64,128]{3,2,1,0:T(8,128)(2,1)S(1)}, bf16[464,128]{1,0:T(8,128)(2,1)S(1)}) custom-call(bf16[8,8,64,128]{3,2,1,0:T(8,128)(2,1)S(1)} %get-tuple-element.23.frames_ref, f32[8,128]{1,0:T(8,128)S(1)} %get-tuple-element.24.dec_ref, bf16[3,3,128,128]{3,2,1,0:T(8,128)(2,1)S(1)} %get-tuple-element.25.w_ref), custom_call_target="tpu_custom_call" | custom-call | flops 1207959552 | bytes 4194304 | tf_op jit(solution)/shard_map/pallas_call | solution.py:335
  6.4 0.0 collective-permute-done.1.corner_ref
  6.4 2.1 %collective-permute-start.2 = (bf16[464,128]{1,0:T(8,128)(2,1)S(1)}, bf16[464,128]{1,0:T(8,128)(2,1)S(1)}, u32[]{:S(2)}, u32[]{:S(2)}) collective-permute-start(bf16[464,128]{1,0:T(8,128)(2,1)S(1)} %get-tuple-element.32), channel_id=1, source_target_pairs={{0,1},{2,3},{1,0},{3,2},{4,5},{6,7},{5,4},{7,6},{8,9},{10,11},{9,8... | collective-permute-start | bytes 356360 | tf_op jit(solution)/shard_map/ppermute | solution.py:353
  8.6 0.1 collective-permute-start.3
  8.6 1.6 %collective-permute-start.4 = (bf16[10,16,128]{2,1,0:T(8,128)(2,1)S(1)}, bf16[10,16,128]{2,1,0:T(8,128)(2,1)S(1)}, u32[]{:S(2)}, u32[]{:S(2)}) collective-permute-start(bf16[10,16,128]{2,1,0:T(8,128)(2,1)S(1)} %pad_maximum_fusion.1), channel_id=1, source_target_pairs={{4,8},{12,0},{8,4},{0,12},{5,9},{13,1},{9,5},{1,13},{6,10},{14,2},... | collective-permute-start | bytes 122888 | tf_op jit(solution)/shard_map/ppermute | solution.py:353
  10.3 1.1 %collective-permute-done.2.ra_ref = bf16[464,128]{1,0:T(8,128)(2,1)S(1)} collective-permute-done((bf16[464,128]{1,0:T(8,128)(2,1)S(1)}, bf16[464,128]{1,0:T(8,128)(2,1)S(1)}, u32[]{:S(2)}, u32[]{:S(2)}) %collective-permute-start.2) | collective-permute-done | bytes 118816 | tf_op jit(solution)/shard_map/ppermute | solution.py:353
  11.4 0.1 fusion.1
  11.4 3.1 %collective-permute-start.5 = (bf16[464,128]{1,0:T(8,128)(2,1)S(1)}, bf16[464,128]{1,0:T(8,128)(2,1)S(1)}, u32[]{:S(2)}, u32[]{:S(2)}) collective-permute-start(bf16[464,128]{1,0:T(8,128)(2,1)S(1)} %fusion.1), channel_id=1, source_target_pairs={{0,2},{2,0},{1,3},{3,1},{4,6},{6,4},{5,7},{7,5},{8,10},{10,8},{9,1... | collective-permute-start | bytes 356360 | tf_op jit(solution)/shard_map/ppermute | solution.py:448
  14.5 0.0 collective-permute-done.3.refs_0_
  14.6 0.0 collective-permute-done.4.refs_1_
  14.6 0.0 collective-permute-done.halo_ref
  14.6 1.9 %shard_map.48 = (f32[2,8,64,128]{3,2,1,0:T(8,128)S(1)}, f32[2,160,128]{2,1,0:T(8,128)S(1)}, bf16[192,128]{1,0:T(8,128)(2,1)S(1)}, bf16[1536,256]{1,0:T(8,128)(2,1)S(1)}) custom-call(bf16[8,2,64,128]{3,2,1,0:T(8,128)(2,1)S(1)} %get-tuple-element.27.own_ref, f32[8,128]{1,0:T(8,128)S(1)} %get-tuple-element.24.dec_ref, ...), custom_call_target="tpu_custom_call" | custom-call | flops 301989888 | bytes 4194304 | tf_op jit(solution)/shard_map/pallas_call | solution.py:335
  16.4 1.4 %collective-permute-start.8 = (bf16[192,128]{1,0:T(8,128)(2,1)S(1)}, bf16[192,128]{1,0:T(8,128)(2,1)S(1)}, u32[]{:S(2)}, u32[]{:S(2)}) collective-permute-start(bf16[192,128]{1,0:T(8,128)(2,1)S(1)} %get-tuple-element.39), channel_id=1, source_target_pairs={{1,2},{3,0},{2,1},{0,3},{5,6},{7,4},{6,5},{4,7},{9,10},{11,8},{10,... | collective-permute-start | bytes 147464 | tf_op jit(solution)/shard_map/ppermute | solution.py:353
  17.9 1.7 %collective-permute-start.7 = (bf16[192,128]{1,0:T(8,128)(2,1)S(1)}, bf16[192,128]{1,0:T(8,128)(2,1)S(1)}, u32[]{:S(2)}, u32[]{:S(2)}) collective-permute-start(bf16[192,128]{1,0:T(8,128)(2,1)S(1)} %get-tuple-element.39), channel_id=1, source_target_pairs={{0,2},{2,0},{1,3},{3,1},{4,6},{6,4},{5,7},{7,5},{8,10},{10,8},{9,1... | collective-permute-start | bytes 147464 | tf_op jit(solution)/shard_map/ppermute | solution.py:468
  19.5 1.4 %collective-permute-start.6 = (bf16[192,128]{1,0:T(8,128)(2,1)S(1)}, bf16[192,128]{1,0:T(8,128)(2,1)S(1)}, u32[]{:S(2)}, u32[]{:S(2)}) collective-permute-start(bf16[192,128]{1,0:T(8,128)(2,1)S(1)} %get-tuple-element.39), channel_id=1, source_target_pairs={{0,1},{2,3},{1,0},{3,2},{4,5},{6,7},{5,4},{7,6},{8,9},{10,11},{9,8... | collective-permute-start | bytes 147464 | tf_op jit(solution)/shard_map/ppermute | solution.py:353
  20.9 0.0 collective-permute-done.5.za_ref
  20.9 1.9 %collective-permute-done.8.b3_ref = bf16[192,128]{1,0:T(8,128)(2,1)S(1)} collective-permute-done((bf16[192,128]{1,0:T(8,128)(2,1)S(1)}, bf16[192,128]{1,0:T(8,128)(2,1)S(1)}, u32[]{:S(2)}, u32[]{:S(2)}) %collective-permute-start.8) | collective-permute-done | bytes 49184 | tf_op jit(solution)/shard_map/ppermute | solution.py:353
  22.8 0.9 %collective-permute-done.7.b2_ref = bf16[192,128]{1,0:T(8,128)(2,1)S(1)} collective-permute-done((bf16[192,128]{1,0:T(8,128)(2,1)S(1)}, bf16[192,128]{1,0:T(8,128)(2,1)S(1)}, u32[]{:S(2)}, u32[]{:S(2)}) %collective-permute-start.7) | collective-permute-done | bytes 49184 | tf_op jit(solution)/shard_map/ppermute | solution.py:468
  23.8 0.2 collective-permute-done.6.b1_ref
  23.9 3.5 %shard_map.49 = bf16[8,8,64,128]{3,2,1,0:T(8,128)(2,1)} custom-call(bf16[7,8,64,128]{3,2,1,0:T(8,128)(2,1)S(1)} %get-tuple-element.26.pa_ref, f32[2,8,64,128]{3,2,1,0:T(8,128)S(1)} %get-tuple-element.37.pb_ref, f32[2,160,128]{2,1,0:T(8,128)S(1)} %get-tuple-element.38.pc_ref, bf16[464,128]{1,0:T(8,128)(2,1)S(1)} %collective-permute-done.2.ra_ref, ...), custom_call_target="tpu_custom_call" | custom-call | flops 1207959552 | bytes 4194304 | tf_op jit(solution)/shard_map/pallas_call | solution.py:335
  (5 shorter events, 0.1 us)
Async XLA Ops:
  1.3 5.1 %collective-permute-start.1 = (bf16[2,32,128]{2,1,0:T(8,128)(2,1)S(1)}, bf16[2,32,128]{2,1,0:T(8,128)(2,1)S(1)}, u32[]{:S(2)}, u32[]{:S(2)}) collective-permute-start(bf16[2,32,128]{2,1,0:T(8,128)(2,1)S(1)} %get-tuple-element.30), channel_id=1, source_target_pairs={{0,16},{16,0},{1,17},{17,1},{2,18},{18,2},{3,19},{19,3},{4,20},{20... | collective-permute-start | bytes 49160 | tf_op jit(solution)/shard_map/ppermute | solution.py:407
  4.3 10.2 %collective-permute-start = (bf16[8,2,64,128]{3,2,1,0:T(8,128)(2,1)S(1)}, bf16[8,2,64,128]{3,2,1,0:T(8,128)(2,1)S(1)}, u32[]{:S(2)}, u32[]{:S(2)}) collective-permute-start(bf16[8,2,64,128]{3,2,1,0:T(8,128)(2,1)S(1)} %get-tuple-element.27.own_ref), channel_id=1, source_target_pairs={{0,16},{16,0},{1,17},{17,1},{2,18},{18,2},{3,19},{19,3},{4,20},{20... | collective-permute-start | bytes 786440 | tf_op jit(solution)/shard_map/ppermute | solution.py:408
  6.4 4.9 %collective-permute-start.2 = (bf16[464,128]{1,0:T(8,128)(2,1)S(1)}, bf16[464,128]{1,0:T(8,128)(2,1)S(1)}, u32[]{:S(2)}, u32[]{:S(2)}) collective-permute-start(bf16[464,128]{1,0:T(8,128)(2,1)S(1)} %get-tuple-element.32), channel_id=1, source_target_pairs={{0,1},{2,3},{1,0},{3,2},{4,5},{6,7},{5,4},{7,6},{8,9},{10,11},{9,8... | collective-permute-start | bytes 356360 | tf_op jit(solution)/shard_map/ppermute | solution.py:353
  8.6 6.0 %collective-permute-start.3 = (bf16[10,16,128]{2,1,0:T(8,128)(2,1)S(1)}, bf16[10,16,128]{2,1,0:T(8,128)(2,1)S(1)}, u32[]{:S(2)}, u32[]{:S(2)}) collective-permute-start(bf16[10,16,128]{2,1,0:T(8,128)(2,1)S(1)} %pad_maximum_fusion), channel_id=1, source_target_pairs={{0,4},{8,12},{4,0},{12,8},{1,5},{9,13},{5,1},{13,9},{2,6},{10,14},... | collective-permute-start | bytes 122888 | tf_op jit(solution)/shard_map/ppermute | solution.py:353
  8.6 5.9 %collective-permute-start.4 = (bf16[10,16,128]{2,1,0:T(8,128)(2,1)S(1)}, bf16[10,16,128]{2,1,0:T(8,128)(2,1)S(1)}, u32[]{:S(2)}, u32[]{:S(2)}) collective-permute-start(bf16[10,16,128]{2,1,0:T(8,128)(2,1)S(1)} %pad_maximum_fusion.1), channel_id=1, source_target_pairs={{4,8},{12,0},{8,4},{0,12},{5,9},{13,1},{9,5},{1,13},{6,10},{14,2},... | collective-permute-start | bytes 122888 | tf_op jit(solution)/shard_map/ppermute | solution.py:353
  11.4 9.4 %collective-permute-start.5 = (bf16[464,128]{1,0:T(8,128)(2,1)S(1)}, bf16[464,128]{1,0:T(8,128)(2,1)S(1)}, u32[]{:S(2)}, u32[]{:S(2)}) collective-permute-start(bf16[464,128]{1,0:T(8,128)(2,1)S(1)} %fusion.1), channel_id=1, source_target_pairs={{0,2},{2,0},{1,3},{3,1},{4,6},{6,4},{5,7},{7,5},{8,10},{10,8},{9,1... | collective-permute-start | bytes 356360 | tf_op jit(solution)/shard_map/ppermute | solution.py:448
  16.4 6.4 %collective-permute-start.8 = (bf16[192,128]{1,0:T(8,128)(2,1)S(1)}, bf16[192,128]{1,0:T(8,128)(2,1)S(1)}, u32[]{:S(2)}, u32[]{:S(2)}) collective-permute-start(bf16[192,128]{1,0:T(8,128)(2,1)S(1)} %get-tuple-element.39), channel_id=1, source_target_pairs={{1,2},{3,0},{2,1},{0,3},{5,6},{7,4},{6,5},{4,7},{9,10},{11,8},{10,... | collective-permute-start | bytes 147464 | tf_op jit(solution)/shard_map/ppermute | solution.py:353
  17.9 5.9 %collective-permute-start.7 = (bf16[192,128]{1,0:T(8,128)(2,1)S(1)}, bf16[192,128]{1,0:T(8,128)(2,1)S(1)}, u32[]{:S(2)}, u32[]{:S(2)}) collective-permute-start(bf16[192,128]{1,0:T(8,128)(2,1)S(1)} %get-tuple-element.39), channel_id=1, source_target_pairs={{0,2},{2,0},{1,3},{3,1},{4,6},{6,4},{5,7},{7,5},{8,10},{10,8},{9,1... | collective-permute-start | bytes 147464 | tf_op jit(solution)/shard_map/ppermute | solution.py:468
  19.5 4.4 %collective-permute-start.6 = (bf16[192,128]{1,0:T(8,128)(2,1)S(1)}, bf16[192,128]{1,0:T(8,128)(2,1)S(1)}, u32[]{:S(2)}, u32[]{:S(2)}) collective-permute-start(bf16[192,128]{1,0:T(8,128)(2,1)S(1)} %get-tuple-element.39), channel_id=1, source_target_pairs={{0,1},{2,3},{1,0},{3,2},{4,5},{6,7},{5,4},{7,6},{8,9},{10,11},{9,8... | collective-permute-start | bytes 147464 | tf_op jit(solution)/shard_map/ppermute | solution.py:353

commit v9 on v8

--- a/solution.py
+++ b/solution.py
@@ -42,10 +42,11 @@
     x3[row, at, 2 * chan : 3 * chan] = rowbuf[slot, 9 : 9 + across, :].astype(BF16)
 
 
-def pair_dot(x3, slots, wt):
+def pair_dot(x3, slots, wt, lo=0, hi=None):
     width = x3.shape[2]
     first = next(k for k in range(4) if slots[k] is not None)
-    rows = jnp.concatenate([x3[s] for s in slots[first:]], axis=1)
+    hi = hi or x3.shape[1]
+    rows = jnp.concatenate([x3[s, lo:hi, :] for s in slots[first:]], axis=1)
     return jnp.dot(rows, wt[first * width : 4 * width, :], preferred_element_type=F32)
 
 
@@ -121,15 +122,20 @@
     pair_weights(w_ref, wt, flip)
     clear_margins(rowbuf)
     decays, scales = load_decays(dec_ref)
-    for r in range(height):
+    def build(r):
         natural = jnp.where(flip == 1, height - 1 - r, r)
         for f in range(frames):
             slot = (r * frames + f) % rowbuf.shape[0]
             x = frames_ref[f, natural]
             rowbuf[slot, 8 : 8 + across, :] = x.astype(F32)
             three_taps(rowbuf, slot, x3, r, f, x)
+
     first, first_row = (0, 1) if two else (1, 0)
+    for r in range(2 * first):
+        build(r)
     for p in range(first, height // 2):
+        build(2 * p)
+        build(2 * p + 1)
         slots = [r if r >= 0 else None for r in range(2 * p - 2, 2 * p + 2)]
         y = pair_dot(x3, slots, wt)
         base = 2 * (p - first)
@@ -244,10 +250,9 @@
         for h in range(2):
             pc_ref[h, pl.ds(f, count, stride=frames), :] = s[:, h * chan : (h + 1) * chan]
     base = len(pairs) * 2 * across
-    pad = jnp.concatenate([jnp.zeros((24 - count, chan), F32), addends(decays, 8)], axis=0)
-    for h in range(2):
-        half = jnp.concatenate([s[:, h * chan : (h + 1) * chan], pad], axis=0)
-        f_ref[base + 32 * h : base + 32 * (h + 1), :] = half.astype(BF16)
+    gap = (-2 * count - 8) % 16
+    tail = [s[:, :chan], s[:, chan:]] + ([jnp.zeros((gap, chan), F32)] if gap else [])
+    f_ref[base:, :] = jnp.concatenate(tail + [addends(decays, 8)], axis=0).astype(BF16)
     fetch.wait()
     pair_weights(next_w, next_wt, flip)
 
@@ -262,8 +267,9 @@
     rows_a = pa_ref.shape[0]
     base = pb_ref.shape[0] * across
 
-    def product(ref, at):
-        return jnp.sum(ref[at : at + 16, :].astype(F32)[8:16], axis=0, keepdims=True)
+    def product(ref):
+        end = ref.shape[0]
+        return jnp.sum(ref[end - 16 : end, :].astype(F32)[8:16], axis=0, keepdims=True)
 
     if ta == 4:
         t = lax.axis_index("ta")
@@ -272,7 +278,7 @@
         last = (t == 3).astype(F32)
         one, two_on = ((t == 1) | (t == 3)).astype(F32), (t == 2).astype(F32)
         from_a = one, two_on + last * other
-        d1, d2, d3 = (product(ref, base + 16) for ref in (b1_ref, b2_ref, b3_ref))
+        d1, d2, d3 = (product(ref) for ref in (b1_ref, b2_ref, b3_ref))
         from_b = one, two_on * d3 + last * d1, two_on + last * d1 * d2
     else:
         from_a, from_b = (1.0, 0.0), (1.0, 0.0, 0.0)
@@ -285,8 +291,8 @@
     for f in range(frames):
         for h in range(2):
             part = pc_ref[h, pl.ds(f, count, stride=frames), :]
-            sc[f, h, 0:count, :] = part + running[f] * ib[base + 32 * h : base + 32 * h + count, :]
-    def build(n):
+            sc[f, h, 0:count, :] = part + running[f] * ib[base + count * h : base + count * (h + 1), :]
+    def build(n, fs):
         if two and n == 0:
             return
         if two:
@@ -296,7 +302,7 @@
         else:
             src, at = (pb_ref, ib), n if n < 2 else n - height + 2
         incoming = src[1][at * across : (at + 1) * across, :]
-        for f in range(frames):
+        for f in fs:
             slot = (n * frames + f) % rowbuf.shape[0]
             rowbuf[slot, 8 : 8 + across, :] = src[0][at, f].astype(F32) + running[f] * incoming
             corner = (n // 2) * 4
@@ -305,26 +311,34 @@
             rowbuf[slot, 7 + across : 9 + across, :] = sc[f, h, corner + 2 : corner + 4, :]
             three_taps(rowbuf, slot, x3, n, f, rowbuf[slot, 8 : 8 + across, :].astype(BF16))
 
-    def finish(p, y):
-        first = jnp.where(flip == 1, height - 2 - 2 * p, 2 * p)
+    def finish(p, fs, y):
         for rr in range(2):
-            row = jnp.where(flip == 1, 1 - rr, rr)
-            for f in range(frames):
-                mixed = y[f * across : (f + 1) * across, rr * chan : (rr + 1) * chan]
-                frame = frames_ref[f, first + row].astype(F32)
-                done[p, f, row] = (frame + jax.nn.gelu(mixed)).astype(BF16)
-        copy = pltpu.make_async_copy(done.at[p], out_ref.at[:, pl.ds(first, 2)], sems.at[p])
-        copy.start()
-        return copy
-
-    copies = []
-    for n in range(2):
-        build(n)
+            natural = jnp.where(flip == 1, height - 1 - (2 * p + rr), 2 * p + rr)
+            for i, f in enumerate(fs):
+                mixed = y[i * across : (i + 1) * across, rr * chan : (rr + 1) * chan]
+                frame = frames_ref[f, natural].astype(F32)
+                done[2 * p + rr, f] = (frame + jax.nn.gelu(mixed)).astype(BF16)
+            if fs[-1] == frames - 1:
+                copy = pltpu.make_async_copy(done.at[2 * p + rr], out_ref.at[:, natural], sems.at[2 * p + rr])
+                copy.start()
+                copies.append(copy)
+
+    copies, waiting = [], None
+    parts = [range(i, i + 4) for i in range(0, frames, 4)]
+    for fs in parts:
+        for n in range(4):
+            build(n, fs)
     for p in range(height // 2):
-        build(2 * p + 2)
-        build(2 * p + 3)
         slots = [n if n > 0 or not two else None for n in range(2 * p, 2 * p + 4)]
-        copies.append(finish(p, pair_dot(x3, slots, wt)))
+        for fs in parts:
+            y = pair_dot(x3, slots, wt, fs[0] * across, (fs[-1] + 1) * across)
+            if waiting:
+                finish(*waiting)
+            waiting = (p, fs, y)
+            for n in (2 * p + 4, 2 * p + 5):
+                if n < height + 2:
+                    build(n, fs)
+    finish(*waiting)
     for copy in copies:
         copy.wait()
 
@@ -431,8 +445,8 @@
         fa, corner = lax.optimization_barrier((fa, corner))
         odd = lax.axis_index("gy") % 2 == 1
         low, high = corner[:, : 2 * n_frames], corner[:, 2 * n_frames :]
-        near = jnp.concatenate([sent[2], jnp.where(odd, low, high)])
-        far = jnp.concatenate([sent[3], jnp.where(odd, high, low)])
+        near = jnp.concatenate([sent[2]] + [jnp.where(odd, low, high)] * 2)
+        far = jnp.concatenate([sent[3]] + [jnp.where(odd, high, low)] * 2)
         sides = [swapped(near, "gy", gy, False), swapped(far, "gy", gy, True)]
     total = jnp.prod(decays, axis=0)[None]
     if ta == 4:
@@ -449,12 +463,13 @@
         _, *sides = lax.optimization_barrier((ga, *sides))
 
     n_cols = (height // 2 + 1) * 4
+    tail_rows = (2 * n_cols + 8 + 15) // 16 * 16
     pb, pc, fb, wt_out = call(
         functools.partial(edge_kernel, two, gx, gy),
         (
             near_mem((rows_b, n_frames, across, chan), F32),
             near_mem((2, n_cols * n_frames, chan), F32),
-            near_mem((rows_b * across + 64, chan), BF16),
+            near_mem((rows_b * across + tail_rows, chan), BF16),
             near_mem((12 * chan, 2 * chan), BF16),
         ),
         [
@@ -476,8 +491,8 @@
         [
             rowbuf, pltpu.VMEM((height + 2, cells, 3 * chan), BF16),
             pltpu.VMEM((n_frames, 2, (n_cols + 7) // 8 * 8, chan), F32),
-            pltpu.VMEM((rows_a * across, chan), F32), pltpu.VMEM((rows_b * across + 64, chan), F32),
-            pltpu.VMEM((height // 2, n_frames, 2, across, chan), BF16), pltpu.SemaphoreType.DMA((height // 2,)),
+            pltpu.VMEM((rows_a * across, chan), F32), pltpu.VMEM((rows_b * across + tail_rows, chan), F32),
+            pltpu.VMEM((height, n_frames, across, chan), BF16), pltpu.SemaphoreType.DMA((height,)),
         ],
         flops * height, [pa, pb, pc, ra, za, *edges, decays, wt_out, frames], out_place=HBM,
     )

time: 27.6 us -> 27.3 us (0.989)
  no operation moved by 1% of the time
where the time goes in v9:
time: 27.3 us; the launch traced here: 27.1 us
  starting transfers between devices  14.5 us (53%)
  Pallas kernels  8.53 us (31%)
  waiting for transfers between devices  3.88 us (14%)
    pallas_call x4, Pallas kernels, call(): pl.pallas_call(body, out_shape=outs, in_specs=[VMEM] * len(near) + [HBM]...  8.53 us
    ppermute x5, starting transfers between devices, swapped(): return lax.ppermute(value, axis, pairs + [(b, a) for a, b in pairs])  6.62 us
    ppermute x5, waiting for transfers between devices, swapped(): return lax.ppermute(value, axis, pairs + [(b, a) for a, b in pairs])  3.13 us
    ppermute x1, starting transfers between devices, on_device(): za = lax.ppermute(ga, 'ta', across_two)  3.1 us
    ppermute x1, starting transfers between devices, on_device(): corner = lax.ppermute(sent[0], 'gx', facing)  3 us
    ppermute x1, starting transfers between devices, on_device(): lax.ppermute(fb, 'ta', across_two)  1.69 us
    ppermute x1, waiting for transfers between devices, on_device(): lax.ppermute(fb, 'ta', across_two)  0.74 us
  transfers between devices with their start and end apart: 9, of which 4 were waited for; matrix products, arithmetic and copies ran while one was open for 0% of the time, Pallas kernels for 14%

profile of v9, /device:TPU:0, one launch (start us, length us, event | category | flops | bytes accessed | tf_op | source)
XLA Modules:
  0.0 27.1 jit_solution(3225690081291778226)
XLA Ops:
  0.0 1.3 %shard_map.46 = (bf16[8,8,64,128]{3,2,1,0:T(8,128)(2,1)S(1)}, f32[8,128]{1,0:T(8,128)S(1)}, bf16[3,3,128,128]{3,2,1,0:T(8,128)(2,1)S(1)}, bf16[8,32,128]{2,1,0:T...) custom-call(bf16[8,8,64,128]{3,2,1,0:T(8,128)(2,1)} %frames_hbm.1, ...), custom_call_target="tpu_custom_call" | custom-call | bytes 4194304 | tf_op jit(solution)/shard_map/pallas_call | solution.py:349
  1.3 3.0 %collective-permute-start.1 = (bf16[2,32,128]{2,1,0:T(8,128)(2,1)S(1)}, bf16[2,32,128]{2,1,0:T(8,128)(2,1)S(1)}, u32[]{:S(2)}, u32[]{:S(2)}) collective-permute-start(bf16[2,32,128]{2,1,0:T(8,128)(2,1)S(1)} %get-tuple-element.30), channel_id=1, source_target_pairs={{0,16},{16,0},{1,17},{17,1},{2,18},{18,2},{3,19},{19,3},{4,20},{20... | collective-permute-start | bytes 49160 | tf_op jit(solution)/shard_map/ppermute | solution.py:421
  4.3 0.1 collective-permute-start
  4.4 2.0 %shard_map.47 = (bf16[7,8,64,128]{3,2,1,0:T(8,128)(2,1)S(1)}, bf16[464,128]{1,0:T(8,128)(2,1)S(1)}) custom-call(bf16[8,8,64,128]{3,2,1,0:T(8,128)(2,1)S(1)} %get-tuple-element.23.frames_ref, f32[8,128]{1,0:T(8,128)S(1)} %get-tuple-element.24.dec_ref, bf16[3,3,128,128]{3,2,1,0:T(8,128)(2,1)S(1)} %get-tuple-element.25.w_ref), custom_call_target="tpu_custom_call" | custom-call | flops 1207959552 | bytes 4194304 | tf_op jit(solution)/shard_map/pallas_call | solution.py:349
  6.4 0.0 collective-permute-done.1.corner_ref
  6.4 2.1 %collective-permute-start.2 = (bf16[464,128]{1,0:T(8,128)(2,1)S(1)}, bf16[464,128]{1,0:T(8,128)(2,1)S(1)}, u32[]{:S(2)}, u32[]{:S(2)}) collective-permute-start(bf16[464,128]{1,0:T(8,128)(2,1)S(1)} %get-tuple-element.32), channel_id=1, source_target_pairs={{0,1},{2,3},{1,0},{3,2},{4,5},{6,7},{5,4},{7,6},{8,9},{10,11},{9,8... | collective-permute-start | bytes 356360 | tf_op jit(solution)/shard_map/ppermute | solution.py:367
  8.6 0.1 collective-permute-start.3
  8.7 1.7 %collective-permute-start.4 = (bf16[12,16,128]{2,1,0:T(8,128)(2,1)S(1)}, bf16[12,16,128]{2,1,0:T(8,128)(2,1)S(1)}, u32[]{:S(2)}, u32[]{:S(2)}) collective-permute-start(bf16[12,16,128]{2,1,0:T(8,128)(2,1)S(1)} %pad_maximum_fusion.1), channel_id=1, source_target_pairs={{4,8},{12,0},{8,4},{0,12},{5,9},{13,1},{9,5},{1,13},{6,10},{14,2},... | collective-permute-start | bytes 147464 | tf_op jit(solution)/shard_map/ppermute | solution.py:367
  10.3 1.0 %collective-permute-done.2.ra_ref = bf16[464,128]{1,0:T(8,128)(2,1)S(1)} collective-permute-done((bf16[464,128]{1,0:T(8,128)(2,1)S(1)}, bf16[464,128]{1,0:T(8,128)(2,1)S(1)}, u32[]{:S(2)}, u32[]{:S(2)}) %collective-permute-start.2) | collective-permute-done | bytes 118816 | tf_op jit(solution)/shard_map/ppermute | solution.py:367
  11.4 0.1 fusion.1
  11.4 3.1 %collective-permute-start.5 = (bf16[464,128]{1,0:T(8,128)(2,1)S(1)}, bf16[464,128]{1,0:T(8,128)(2,1)S(1)}, u32[]{:S(2)}, u32[]{:S(2)}) collective-permute-start(bf16[464,128]{1,0:T(8,128)(2,1)S(1)} %fusion.1), channel_id=1, source_target_pairs={{0,2},{2,0},{1,3},{3,1},{4,6},{6,4},{5,7},{7,5},{8,10},{10,8},{9,1... | collective-permute-start | bytes 356360 | tf_op jit(solution)/shard_map/ppermute | solution.py:462
  14.5 0.0 collective-permute-done.3.refs_0_
  14.6 0.0 collective-permute-done.4.refs_1_
  14.6 0.0 collective-permute-done.halo_ref
  14.6 1.9 %shard_map.48 = (f32[2,8,64,128]{3,2,1,0:T(8,128)S(1)}, f32[2,160,128]{2,1,0:T(8,128)S(1)}, bf16[176,128]{1,0:T(8,128)(2,1)S(1)}, bf16[1536,256]{1,0:T(8,128)(2,1)S(1)}) custom-call(bf16[8,2,64,128]{3,2,1,0:T(8,128)(2,1)S(1)} %get-tuple-element.27.own_ref, f32[8,128]{1,0:T(8,128)S(1)} %get-tuple-element.24.dec_ref, ...), custom_call_target="tpu_custom_call" | custom-call | flops 301989888 | bytes 4194304 | tf_op jit(solution)/shard_map/pallas_call | solution.py:349
  16.4 1.4 %collective-permute-start.8 = (bf16[176,128]{1,0:T(8,128)(2,1)S(1)}, bf16[176,128]{1,0:T(8,128)(2,1)S(1)}, u32[]{:S(2)}, u32[]{:S(2)}) collective-permute-start(bf16[176,128]{1,0:T(8,128)(2,1)S(1)} %get-tuple-element.39), channel_id=1, source_target_pairs={{1,2},{3,0},{2,1},{0,3},{5,6},{7,4},{6,5},{4,7},{9,10},{11,8},{10,... | collective-permute-start | bytes 135176 | tf_op jit(solution)/shard_map/ppermute | solution.py:367
  17.9 1.7 %collective-permute-start.7 = (bf16[176,128]{1,0:T(8,128)(2,1)S(1)}, bf16[176,128]{1,0:T(8,128)(2,1)S(1)}, u32[]{:S(2)}, u32[]{:S(2)}) collective-permute-start(bf16[176,128]{1,0:T(8,128)(2,1)S(1)} %get-tuple-element.39), channel_id=1, source_target_pairs={{0,2},{2,0},{1,3},{3,1},{4,6},{6,4},{5,7},{7,5},{8,10},{10,8},{9,1... | collective-permute-start | bytes 135176 | tf_op jit(solution)/shard_map/ppermute | solution.py:483
  19.5 1.4 %collective-permute-start.6 = (bf16[176,128]{1,0:T(8,128)(2,1)S(1)}, bf16[176,128]{1,0:T(8,128)(2,1)S(1)}, u32[]{:S(2)}, u32[]{:S(2)}) collective-permute-start(bf16[176,128]{1,0:T(8,128)(2,1)S(1)} %get-tuple-element.39), channel_id=1, source_target_pairs={{0,1},{2,3},{1,0},{3,2},{4,5},{6,7},{5,4},{7,6},{8,9},{10,11},{9,8... | collective-permute-start | bytes 135176 | tf_op jit(solution)/shard_map/ppermute | solution.py:367
  20.9 0.0 collective-permute-done.5.za_ref
  20.9 2.0 %collective-permute-done.8.b3_ref = bf16[176,128]{1,0:T(8,128)(2,1)S(1)} collective-permute-done((bf16[176,128]{1,0:T(8,128)(2,1)S(1)}, bf16[176,128]{1,0:T(8,128)(2,1)S(1)}, u32[]{:S(2)}, u32[]{:S(2)}) %collective-permute-start.8) | collective-permute-done | bytes 45088 | tf_op jit(solution)/shard_map/ppermute | solution.py:367
  22.9 0.7 %collective-permute-done.7.b2_ref = bf16[176,128]{1,0:T(8,128)(2,1)S(1)} collective-permute-done((bf16[176,128]{1,0:T(8,128)(2,1)S(1)}, bf16[176,128]{1,0:T(8,128)(2,1)S(1)}, u32[]{:S(2)}, u32[]{:S(2)}) %collective-permute-start.7) | collective-permute-done | bytes 45088 | tf_op jit(solution)/shard_map/ppermute | solution.py:483
  23.7 0.1 collective-permute-done.6.b1_ref
  23.7 3.4 %shard_map.49 = bf16[8,8,64,128]{3,2,1,0:T(8,128)(2,1)} custom-call(bf16[7,8,64,128]{3,2,1,0:T(8,128)(2,1)S(1)} %get-tuple-element.26.pa_ref, f32[2,8,64,128]{3,2,1,0:T(8,128)S(1)} %get-tuple-element.37.pb_ref, f32[2,160,128]{2,1,0:T(8,128)S(1)} %get-tuple-element.38.pc_ref, bf16[464,128]{1,0:T(8,128)(2,1)S(1)} %collective-permute-done.2.ra_ref, ...), custom_call_target="tpu_custom_call" | custom-call | flops 1207959552 | bytes 4194304 | tf_op jit(solution)/shard_map/pallas_call | solution.py:349
  (5 shorter events, 0.1 us)
Async XLA Ops:
  1.3 5.1 %collective-permute-start.1 = (bf16[2,32,128]{2,1,0:T(8,128)(2,1)S(1)}, bf16[2,32,128]{2,1,0:T(8,128)(2,1)S(1)}, u32[]{:S(2)}, u32[]{:S(2)}) collective-permute-start(bf16[2,32,128]{2,1,0:T(8,128)(2,1)S(1)} %get-tuple-element.30), channel_id=1, source_target_pairs={{0,16},{16,0},{1,17},{17,1},{2,18},{18,2},{3,19},{19,3},{4,20},{20... | collective-permute-start | bytes 49160 | tf_op jit(solution)/shard_map/ppermute | solution.py:421
  4.3 10.2 %collective-permute-start = (bf16[8,2,64,128]{3,2,1,0:T(8,128)(2,1)S(1)}, bf16[8,2,64,128]{3,2,1,0:T(8,128)(2,1)S(1)}, u32[]{:S(2)}, u32[]{:S(2)}) collective-permute-start(bf16[8,2,64,128]{3,2,1,0:T(8,128)(2,1)S(1)} %get-tuple-element.27.own_ref), channel_id=1, source_target_pairs={{0,16},{16,0},{1,17},{17,1},{2,18},{18,2},{3,19},{19,3},{4,20},{20... | collective-permute-start | bytes 786440 | tf_op jit(solution)/shard_map/ppermute | solution.py:422
  6.4 4.9 %collective-permute-start.2 = (bf16[464,128]{1,0:T(8,128)(2,1)S(1)}, bf16[464,128]{1,0:T(8,128)(2,1)S(1)}, u32[]{:S(2)}, u32[]{:S(2)}) collective-permute-start(bf16[464,128]{1,0:T(8,128)(2,1)S(1)} %get-tuple-element.32), channel_id=1, source_target_pairs={{0,1},{2,3},{1,0},{3,2},{4,5},{6,7},{5,4},{7,6},{8,9},{10,11},{9,8... | collective-permute-start | bytes 356360 | tf_op jit(solution)/shard_map/ppermute | solution.py:367
  8.6 6.0 %collective-permute-start.3 = (bf16[12,16,128]{2,1,0:T(8,128)(2,1)S(1)}, bf16[12,16,128]{2,1,0:T(8,128)(2,1)S(1)}, u32[]{:S(2)}, u32[]{:S(2)}) collective-permute-start(bf16[12,16,128]{2,1,0:T(8,128)(2,1)S(1)} %pad_maximum_fusion), channel_id=1, source_target_pairs={{0,4},{8,12},{4,0},{12,8},{1,5},{9,13},{5,1},{13,9},{2,6},{10,14},... | collective-permute-start | bytes 147464 | tf_op jit(solution)/shard_map/ppermute | solution.py:367
  8.7 5.9 %collective-permute-start.4 = (bf16[12,16,128]{2,1,0:T(8,128)(2,1)S(1)}, bf16[12,16,128]{2,1,0:T(8,128)(2,1)S(1)}, u32[]{:S(2)}, u32[]{:S(2)}) collective-permute-start(bf16[12,16,128]{2,1,0:T(8,128)(2,1)S(1)} %pad_maximum_fusion.1), channel_id=1, source_target_pairs={{4,8},{12,0},{8,4},{0,12},{5,9},{13,1},{9,5},{1,13},{6,10},{14,2},... | collective-permute-start | bytes 147464 | tf_op jit(solution)/shard_map/ppermute | solution.py:367
  11.4 9.5 %collective-permute-start.5 = (bf16[464,128]{1,0:T(8,128)(2,1)S(1)}, bf16[464,128]{1,0:T(8,128)(2,1)S(1)}, u32[]{:S(2)}, u32[]{:S(2)}) collective-permute-start(bf16[464,128]{1,0:T(8,128)(2,1)S(1)} %fusion.1), channel_id=1, source_target_pairs={{0,2},{2,0},{1,3},{3,1},{4,6},{6,4},{5,7},{7,5},{8,10},{10,8},{9,1... | collective-permute-start | bytes 356360 | tf_op jit(solution)/shard_map/ppermute | solution.py:462
  16.4 6.5 %collective-permute-start.8 = (bf16[176,128]{1,0:T(8,128)(2,1)S(1)}, bf16[176,128]{1,0:T(8,128)(2,1)S(1)}, u32[]{:S(2)}, u32[]{:S(2)}) collective-permute-start(bf16[176,128]{1,0:T(8,128)(2,1)S(1)} %get-tuple-element.39), channel_id=1, source_target_pairs={{1,2},{3,0},{2,1},{0,3},{5,6},{7,4},{6,5},{4,7},{9,10},{11,8},{10,... | collective-permute-start | bytes 135176 | tf_op jit(solution)/shard_map/ppermute | solution.py:367
  17.9 5.8 %collective-permute-start.7 = (bf16[176,128]{1,0:T(8,128)(2,1)S(1)}, bf16[176,128]{1,0:T(8,128)(2,1)S(1)}, u32[]{:S(2)}, u32[]{:S(2)}) collective-permute-start(bf16[176,128]{1,0:T(8,128)(2,1)S(1)} %get-tuple-element.39), channel_id=1, source_target_pairs={{0,2},{2,0},{1,3},{3,1},{4,6},{6,4},{5,7},{7,5},{8,10},{10,8},{9,1... | collective-permute-start | bytes 135176 | tf_op jit(solution)/shard_map/ppermute | solution.py:483
  19.5 4.2 %collective-permute-start.6 = (bf16[176,128]{1,0:T(8,128)(2,1)S(1)}, bf16[176,128]{1,0:T(8,128)(2,1)S(1)}, u32[]{:S(2)}, u32[]{:S(2)}) collective-permute-start(bf16[176,128]{1,0:T(8,128)(2,1)S(1)} %get-tuple-element.39), channel_id=1, source_target_pairs={{0,1},{2,3},{1,0},{3,2},{4,5},{6,7},{5,4},{7,6},{8,9},{10,11},{9,8... | collective-permute-start | bytes 135176 | tf_op jit(solution)/shard_map/ppermute | solution.py:367

commit v10 on v9

--- a/solution.py
+++ b/solution.py
@@ -257,8 +257,21 @@
     pair_weights(next_w, next_wt, flip)
 
 
-def outer_kernel(
-    two, ta, pa_ref, pb_ref, pc_ref, ra_ref, za_ref, b1_ref, b2_ref, b3_ref, dec_ref, wt, frames_ref,
+def outer_kernel(two, ta, early, n_in, *refs):
+    pa_ref, pb_ref, pc_ref, dec_ref, wt, frames_ref, *others = refs[:n_in]
+    out_ref, *scratch = refs[n_in:]
+    if ta != 4:
+        finish_frames(two, ta, early, pa_ref, pb_ref, pc_ref, dec_ref, wt, frames_ref, others, out_ref, *scratch)
+        return
+    here = lax.axis_index("ta") == 0 if early else lax.axis_index("ta") > 0
+
+    @pl.when(here)
+    def _():
+        finish_frames(two, ta, early, pa_ref, pb_ref, pc_ref, dec_ref, wt, frames_ref, others, out_ref, *scratch)
+
+
+def finish_frames(
+    two, ta, early, pa_ref, pb_ref, pc_ref, dec_ref, wt, frames_ref, others,
     out_ref, rowbuf, x3, sc, ia, ib, done, sems,
 ):
     frames, height, across, chan = frames_ref.shape
@@ -271,19 +284,24 @@
         end = ref.shape[0]
         return jnp.sum(ref[end - 16 : end, :].astype(F32)[8:16], axis=0, keepdims=True)
 
-    if ta == 4:
-        t = lax.axis_index("ta")
+    t = lax.axis_index("ta")
+    if early:
+        ia[...] = jnp.zeros_like(ia)
+        ib[...] = jnp.zeros_like(ib)
+    elif ta != 4:
+        ia[...] = others[0][0 : rows_a * across].astype(F32)
+        ib[...] = others[1][...].astype(F32)
+    else:
+        ra_ref, b1_ref, b2_ref, b3_ref, za_ref = others[:5]
         end = ra_ref.shape[0]
         other = jnp.sum(ra_ref[end - 16 : end, :].astype(F32), axis=0, keepdims=True)
         last = (t == 3).astype(F32)
-        one, two_on = ((t == 1) | (t == 3)).astype(F32), (t == 2).astype(F32)
+        one, two_on = (t == 1).astype(F32) + last, (t == 2).astype(F32)
         from_a = one, two_on + last * other
         d1, d2, d3 = (product(ref) for ref in (b1_ref, b2_ref, b3_ref))
         from_b = one, two_on * d3 + last * d1, two_on + last * d1 * d2
-    else:
-        from_a, from_b = (1.0, 0.0), (1.0, 0.0, 0.0)
-    ia[...] = sum(c * ref[0 : rows_a * across].astype(F32) for c, ref in zip(from_a, (ra_ref, za_ref)))
-    ib[...] = sum(c * ref[...].astype(F32) for c, ref in zip(from_b, (b1_ref, b2_ref, b3_ref)))
+        ia[...] = sum(c * ref[0 : rows_a * across].astype(F32) for c, ref in zip(from_a, (ra_ref, za_ref)))
+        ib[...] = sum(c * ref[...].astype(F32) for c, ref in zip(from_b, (b1_ref, b2_ref, b3_ref)))
     running = [decays[0:1]]
     for f in range(1, frames):
         running.append(running[-1] * decays[f : f + 1])
@@ -343,7 +361,7 @@
         copy.wait()
 
 
-def call(body, outs, scratch, flops, near, far=(), out_place=VMEM):
+def call(body, outs, scratch, flops, near, far=(), out_place=VMEM, aliases=None):
     near = [pltpu.with_memory_space_constraint(a, pltpu.VMEM) for a in near]
     far = [pltpu.with_memory_space_constraint(a, pltpu.HBM) for a in far]
     return pl.pallas_call(
@@ -352,6 +370,7 @@
         in_specs=[VMEM] * len(near) + [HBM] * len(far),
         out_specs=jax.tree.map(lambda _: out_place, outs),
         scratch_shapes=scratch,
+        input_output_aliases=aliases or {},
         compiler_params=pltpu.CompilerParams(vmem_limit_bytes=24 * 2**20),
         cost_estimate=pl.CostEstimate(flops=flops, bytes_accessed=4 * 2**20, transcendentals=0),
     )(*near, *far)
@@ -485,17 +504,24 @@
         ra, rb = carry_general([fa, fb], total, ta)
         za, edges = ra, [rb] * 3
 
-    return call(
-        functools.partial(outer_kernel, two, ta),
-        jax.ShapeDtypeStruct(frames.shape, BF16),
-        [
-            rowbuf, pltpu.VMEM((height + 2, cells, 3 * chan), BF16),
-            pltpu.VMEM((n_frames, 2, (n_cols + 7) // 8 * 8, chan), F32),
-            pltpu.VMEM((rows_a * across, chan), F32), pltpu.VMEM((rows_b * across + tail_rows, chan), F32),
-            pltpu.VMEM((height, n_frames, across, chan), BF16), pltpu.SemaphoreType.DMA((height,)),
-        ],
-        flops * height, [pa, pb, pc, ra, za, *edges, decays, wt_out, frames], out_place=HBM,
-    )
+    def last_kernel(early, near, far=()):
+        return call(
+            functools.partial(outer_kernel, two, ta, early, len(near) + len(far)),
+            jax.ShapeDtypeStruct(frames.shape, BF16),
+            [
+                rowbuf, pltpu.VMEM((height + 2, cells, 3 * chan), BF16),
+                pltpu.VMEM((n_frames, 2, (n_cols + 7) // 8 * 8, chan), F32),
+                pltpu.VMEM((rows_a * across, chan), F32), pltpu.VMEM((rows_b * across + tail_rows, chan), F32),
+                pltpu.VMEM((height, n_frames, across, chan), BF16), pltpu.SemaphoreType.DMA((height,)),
+            ],
+            flops * height, near, far, HBM, {len(near): 0} if far else None,
+        )
+
+    common = [pa, pb, pc, decays, wt_out, frames]
+    if ta != 4:
+        return last_kernel(False, common + [ra, edges[0]])
+    begun = last_kernel(True, common)
+    return last_kernel(False, common + [ra, *edges, za], [begun])
 
 
 def solution(mesh):

time: 27.3 us -> 25.4 us (0.930)
  the two profiles are of different devices: /device:TPU:0 before, /device:TPU:8 now
where the time goes in v10:
time: 25.4 us; the launch traced here: 25.2 us
  starting transfers between devices  10.5 us (41%)
  Pallas kernels  8.55 us (34%)
  waiting for transfers between devices  5.89 us (23%)
    pallas_call x5, Pallas kernels, call(): pl.pallas_call(body, out_shape=outs, in_specs=[VMEM] * len(near) + [HBM]...  8.55 us
    ppermute x5, waiting for transfers between devices, swapped(): return lax.ppermute(value, axis, pairs + [(b, a) for a, b in pairs])  4.58 us
    ppermute x5, starting transfers between devices, swapped(): return lax.ppermute(value, axis, pairs + [(b, a) for a, b in pairs])  2.99 us
    ppermute x1, starting transfers between devices, on_device(): lax.ppermute(fb, 'ta', across_two)  2.8 us
    ppermute x1, starting transfers between devices, on_device(): za = lax.ppermute(ga, 'ta', across_two)  2.65 us
    ppermute x1, starting transfers between devices, on_device(): corner = lax.ppermute(sent[0], 'gx', facing)  1.56 us
    ppermute x1, waiting for transfers between devices, on_device(): lax.ppermute(fb, 'ta', across_two)  0.79 us
    ppermute x1, starting transfers between devices, on_device(): halo = lax.ppermute(sent[1], 'gx', facing)  0.53 us
  transfers between devices with their start and end apart: 9, of which 5 were waited for; matrix products, arithmetic and copies ran while one was open for 1% of the time, Pallas kernels for 16%

profile of v10, /device:TPU:8, one launch (start us, length us, event | category | flops | bytes accessed | tf_op | source)
XLA Modules:
  0.0 25.2 jit_solution(16846365894744878130)
XLA Ops:
  0.0 1.3 %shard_map.46 = (bf16[8,8,64,128]{3,2,1,0:T(8,128)(2,1)S(1)}, f32[8,128]{1,0:T(8,128)S(1)}, bf16[3,3,128,128]{3,2,1,0:T(8,128)(2,1)S(1)}, bf16[8,32,128]{2,1,0:T...) custom-call(bf16[8,8,64,128]{3,2,1,0:T(8,128)(2,1)} %frames_hbm.1, ...), custom_call_target="tpu_custom_call" | custom-call | bytes 4194304 | tf_op jit(solution)/shard_map/pallas_call | solution.py:367
  1.3 1.6 %collective-permute-start.1 = (bf16[2,32,128]{2,1,0:T(8,128)(2,1)S(1)}, bf16[2,32,128]{2,1,0:T(8,128)(2,1)S(1)}, u32[]{:S(2)}, u32[]{:S(2)}) collective-permute-start(bf16[2,32,128]{2,1,0:T(8,128)(2,1)S(1)} %get-tuple-element.30), channel_id=1, source_target_pairs={{0,16},{16,0},{1,17},{17,1},{2,18},{18,2},{3,19},{19,3},{4,20},{20... | collective-permute-start | bytes 49160 | tf_op jit(solution)/shard_map/ppermute | solution.py:440
  2.9 0.5 %collective-permute-start = (bf16[8,2,64,128]{3,2,1,0:T(8,128)(2,1)S(1)}, bf16[8,2,64,128]{3,2,1,0:T(8,128)(2,1)S(1)}, u32[]{:S(2)}, u32[]{:S(2)}) collective-permute-start(bf16[8,2,64,128]{3,2,1,0:T(8,128)(2,1)S(1)} %get-tuple-element.27.own_ref), channel_id=1, source_target_pairs={{0,16},{16,0},{1,17},{17,1},{2,18},{18,2},{3,19},{19,3},{4,20},{20... | collective-permute-start | bytes 786440 | tf_op jit(solution)/shard_map/ppermute | solution.py:441
  3.4 2.0 %shard_map.47 = (bf16[7,8,64,128]{3,2,1,0:T(8,128)(2,1)S(1)}, bf16[464,128]{1,0:T(8,128)(2,1)S(1)}) custom-call(bf16[8,8,64,128]{3,2,1,0:T(8,128)(2,1)S(1)} %get-tuple-element.23.frames_ref.refs_5_, f32[8,128]{1,0:T(8,128)S(1)} %get-tuple-element.24.dec_ref.refs_3_, bf16[3,3,128,128]{3,2,1,0:T(8,128)(2,1)S(1)} %get-tuple-element.25.w_ref), custom_call_target="tpu_custom_call" | custom-call | flops 1207959552 | bytes 4194304 | tf_op jit(solution)/shard_map/pallas_call | solution.py:367
  5.4 0.0 collective-permute-done.1.corner_ref
  5.5 0.1 collective-permute-start.2
  5.6 0.1 collective-permute-start.3
  5.7 2.1 %collective-permute-start.4 = (bf16[12,16,128]{2,1,0:T(8,128)(2,1)S(1)}, bf16[12,16,128]{2,1,0:T(8,128)(2,1)S(1)}, u32[]{:S(2)}, u32[]{:S(2)}) collective-permute-start(bf16[12,16,128]{2,1,0:T(8,128)(2,1)S(1)} %pad_maximum_fusion.1), channel_id=1, source_target_pairs={{4,8},{12,0},{8,4},{0,12},{5,9},{13,1},{9,5},{1,13},{6,10},{14,2},... | collective-permute-start | bytes 147464 | tf_op jit(solution)/shard_map/ppermute | solution.py:386
  7.8 2.6 %collective-permute-done.2.refs_6_ = bf16[464,128]{1,0:T(8,128)(2,1)S(1)} collective-permute-done((bf16[464,128]{1,0:T(8,128)(2,1)S(1)}, bf16[464,128]{1,0:T(8,128)(2,1)S(1)}, u32[]{:S(2)}, u32[]{:S(2)}) %collective-permute-start.2) | collective-permute-done | bytes 118816 | tf_op jit(solution)/shard_map/ppermute | solution.py:386
  10.4 0.1 fusion.1
  10.4 2.7 %collective-permute-start.8 = (bf16[464,128]{1,0:T(8,128)(2,1)S(1)}, bf16[464,128]{1,0:T(8,128)(2,1)S(1)}, u32[]{:S(2)}, u32[]{:S(2)}) collective-permute-start(bf16[464,128]{1,0:T(8,128)(2,1)S(1)} %fusion.1), channel_id=1, source_target_pairs={{0,2},{2,0},{1,3},{3,1},{4,6},{6,4},{5,7},{7,5},{8,10},{10,8},{9,1... | collective-permute-start | bytes 356360 | tf_op jit(solution)/shard_map/ppermute | solution.py:481
  13.1 0.0 collective-permute-done.3.refs_0_
  13.1 0.0 collective-permute-done.4.refs_1_
  13.1 0.0 collective-permute-done.halo_ref
  13.1 1.9 %shard_map.48 = (f32[2,8,64,128]{3,2,1,0:T(8,128)S(1)}, f32[2,160,128]{2,1,0:T(8,128)S(1)}, bf16[176,128]{1,0:T(8,128)(2,1)S(1)}, bf16[1536,256]{1,0:T(8,128)(2,1)S(1)}) custom-call(bf16[8,2,64,128]{3,2,1,0:T(8,128)(2,1)S(1)} %get-tuple-element.27.own_ref, f32[8,128]{1,0:T(8,128)S(1)} %get-tuple-element.24.dec_ref.refs_3_, ...), custom_call_target="tpu_custom_call" | custom-call | flops 301989888 | bytes 4194304 | tf_op jit(solution)/shard_map/pallas_call | solution.py:367
  15.0 0.1 collective-permute-start.7
  15.1 2.8 %collective-permute-start.6 = (bf16[176,128]{1,0:T(8,128)(2,1)S(1)}, bf16[176,128]{1,0:T(8,128)(2,1)S(1)}, u32[]{:S(2)}, u32[]{:S(2)}) collective-permute-start(bf16[176,128]{1,0:T(8,128)(2,1)S(1)} %get-tuple-element.40), channel_id=1, source_target_pairs={{0,2},{2,0},{1,3},{3,1},{4,6},{6,4},{5,7},{7,5},{8,10},{10,8},{9,1... | collective-permute-start | bytes 135176 | tf_op jit(solution)/shard_map/ppermute | solution.py:502
  17.9 0.7 %collective-permute-start.5 = (bf16[176,128]{1,0:T(8,128)(2,1)S(1)}, bf16[176,128]{1,0:T(8,128)(2,1)S(1)}, u32[]{:S(2)}, u32[]{:S(2)}) collective-permute-start(bf16[176,128]{1,0:T(8,128)(2,1)S(1)} %get-tuple-element.40), channel_id=1, source_target_pairs={{0,1},{2,3},{1,0},{3,2},{4,5},{6,7},{5,4},{7,6},{8,9},{10,11},{9,8... | collective-permute-start | bytes 135176 | tf_op jit(solution)/shard_map/ppermute | solution.py:386
  18.5 0.1 shard_map.49.refs_11_
  18.6 0.5 %collective-permute-done.8.refs_10_ = bf16[464,128]{1,0:T(8,128)(2,1)S(1)} collective-permute-done((bf16[464,128]{1,0:T(8,128)(2,1)S(1)}, bf16[464,128]{1,0:T(8,128)(2,1)S(1)}, u32[]{:S(2)}, u32[]{:S(2)}) %collective-permute-start.8) | collective-permute-done | bytes 118816 | tf_op jit(solution)/shard_map/ppermute | solution.py:481
  19.1 1.0 %collective-permute-done.7.refs_9_ = bf16[176,128]{1,0:T(8,128)(2,1)S(1)} collective-permute-done((bf16[176,128]{1,0:T(8,128)(2,1)S(1)}, bf16[176,128]{1,0:T(8,128)(2,1)S(1)}, u32[]{:S(2)}, u32[]{:S(2)}) %collective-permute-start.7) | collective-permute-done | bytes 45088 | tf_op jit(solution)/shard_map/ppermute | solution.py:386
  20.1 0.8 %collective-permute-done.6.refs_8_ = bf16[176,128]{1,0:T(8,128)(2,1)S(1)} collective-permute-done((bf16[176,128]{1,0:T(8,128)(2,1)S(1)}, bf16[176,128]{1,0:T(8,128)(2,1)S(1)}, u32[]{:S(2)}, u32[]{:S(2)}) %collective-permute-start.6) | collective-permute-done | bytes 45088 | tf_op jit(solution)/shard_map/ppermute | solution.py:502
  20.9 1.0 %collective-permute-done.5.refs_7_ = bf16[176,128]{1,0:T(8,128)(2,1)S(1)} collective-permute-done((bf16[176,128]{1,0:T(8,128)(2,1)S(1)}, bf16[176,128]{1,0:T(8,128)(2,1)S(1)}, u32[]{:S(2)}, u32[]{:S(2)}) %collective-permute-start.5) | collective-permute-done | bytes 45088 | tf_op jit(solution)/shard_map/ppermute | solution.py:386
  21.9 3.3 %shard_map.50 = bf16[8,8,64,128]{3,2,1,0:T(8,128)(2,1)} custom-call(bf16[7,8,64,128]{3,2,1,0:T(8,128)(2,1)S(1)} %get-tuple-element.26.refs_0_, f32[2,8,64,128]{3,2,1,0:T(8,128)S(1)} %get-tuple-element.37.refs_1_, f32[2,160,128]{2,1,0:T(8,128)S(1)} %get-tuple-element.38.refs_2_, ...), custom_call_target="tpu_custom_call", output_to_operand_aliasing={{}: (11, {})} | custom-call | flops 1207959552 | bytes 4194304 | tf_op jit(solution)/shard_map/pallas_call | solution.py:367
  (5 shorter events, 0.1 us)
Async XLA Ops:
  1.3 4.1 %collective-permute-start.1 = (bf16[2,32,128]{2,1,0:T(8,128)(2,1)S(1)}, bf16[2,32,128]{2,1,0:T(8,128)(2,1)S(1)}, u32[]{:S(2)}, u32[]{:S(2)}) collective-permute-start(bf16[2,32,128]{2,1,0:T(8,128)(2,1)S(1)} %get-tuple-element.30), channel_id=1, source_target_pairs={{0,16},{16,0},{1,17},{17,1},{2,18},{18,2},{3,19},{19,3},{4,20},{20... | collective-permute-start | bytes 49160 | tf_op jit(solution)/shard_map/ppermute | solution.py:440
  2.9 10.2 %collective-permute-start = (bf16[8,2,64,128]{3,2,1,0:T(8,128)(2,1)S(1)}, bf16[8,2,64,128]{3,2,1,0:T(8,128)(2,1)S(1)}, u32[]{:S(2)}, u32[]{:S(2)}) collective-permute-start(bf16[8,2,64,128]{3,2,1,0:T(8,128)(2,1)S(1)} %get-tuple-element.27.own_ref), channel_id=1, source_target_pairs={{0,16},{16,0},{1,17},{17,1},{2,18},{18,2},{3,19},{19,3},{4,20},{20... | collective-permute-start | bytes 786440 | tf_op jit(solution)/shard_map/ppermute | solution.py:441
  5.5 4.9 %collective-permute-start.2 = (bf16[464,128]{1,0:T(8,128)(2,1)S(1)}, bf16[464,128]{1,0:T(8,128)(2,1)S(1)}, u32[]{:S(2)}, u32[]{:S(2)}) collective-permute-start(bf16[464,128]{1,0:T(8,128)(2,1)S(1)} %get-tuple-element.32), channel_id=1, source_target_pairs={{0,1},{2,3},{1,0},{3,2},{4,5},{6,7},{5,4},{7,6},{8,9},{10,11},{9,8... | collective-permute-start | bytes 356360 | tf_op jit(solution)/shard_map/ppermute | solution.py:386
  5.6 7.5 %collective-permute-start.3 = (bf16[12,16,128]{2,1,0:T(8,128)(2,1)S(1)}, bf16[12,16,128]{2,1,0:T(8,128)(2,1)S(1)}, u32[]{:S(2)}, u32[]{:S(2)}) collective-permute-start(bf16[12,16,128]{2,1,0:T(8,128)(2,1)S(1)} %pad_maximum_fusion), channel_id=1, source_target_pairs={{0,4},{8,12},{4,0},{12,8},{1,5},{9,13},{5,1},{13,9},{2,6},{10,14},... | collective-permute-start | bytes 147464 | tf_op jit(solution)/shard_map/ppermute | solution.py:386
  5.7 7.4 %collective-permute-start.4 = (bf16[12,16,128]{2,1,0:T(8,128)(2,1)S(1)}, bf16[12,16,128]{2,1,0:T(8,128)(2,1)S(1)}, u32[]{:S(2)}, u32[]{:S(2)}) collective-permute-start(bf16[12,16,128]{2,1,0:T(8,128)(2,1)S(1)} %pad_maximum_fusion.1), channel_id=1, source_target_pairs={{4,8},{12,0},{8,4},{0,12},{5,9},{13,1},{9,5},{1,13},{6,10},{14,2},... | collective-permute-start | bytes 147464 | tf_op jit(solution)/shard_map/ppermute | solution.py:386
  10.4 8.7 %collective-permute-start.8 = (bf16[464,128]{1,0:T(8,128)(2,1)S(1)}, bf16[464,128]{1,0:T(8,128)(2,1)S(1)}, u32[]{:S(2)}, u32[]{:S(2)}) collective-permute-start(bf16[464,128]{1,0:T(8,128)(2,1)S(1)} %fusion.1), channel_id=1, source_target_pairs={{0,2},{2,0},{1,3},{3,1},{4,6},{6,4},{5,7},{7,5},{8,10},{10,8},{9,1... | collective-permute-start | bytes 356360 | tf_op jit(solution)/shard_map/ppermute | solution.py:481
  15.0 5.1 %collective-permute-start.7 = (bf16[176,128]{1,0:T(8,128)(2,1)S(1)}, bf16[176,128]{1,0:T(8,128)(2,1)S(1)}, u32[]{:S(2)}, u32[]{:S(2)}) collective-permute-start(bf16[176,128]{1,0:T(8,128)(2,1)S(1)} %get-tuple-element.40), channel_id=1, source_target_pairs={{1,2},{3,0},{2,1},{0,3},{5,6},{7,4},{6,5},{4,7},{9,10},{11,8},{10,... | collective-permute-start | bytes 135176 | tf_op jit(solution)/shard_map/ppermute | solution.py:386
  15.1 5.9 %collective-permute-start.6 = (bf16[176,128]{1,0:T(8,128)(2,1)S(1)}, bf16[176,128]{1,0:T(8,128)(2,1)S(1)}, u32[]{:S(2)}, u32[]{:S(2)}) collective-permute-start(bf16[176,128]{1,0:T(8,128)(2,1)S(1)} %get-tuple-element.40), channel_id=1, source_target_pairs={{0,2},{2,0},{1,3},{3,1},{4,6},{6,4},{5,7},{7,5},{8,10},{10,8},{9,1... | collective-permute-start | bytes 135176 | tf_op jit(solution)/shard_map/ppermute | solution.py:502
  17.9 4.0 %collective-permute-start.5 = (bf16[176,128]{1,0:T(8,128)(2,1)S(1)}, bf16[176,128]{1,0:T(8,128)(2,1)S(1)}, u32[]{:S(2)}, u32[]{:S(2)}) collective-permute-start(bf16[176,128]{1,0:T(8,128)(2,1)S(1)} %get-tuple-element.40), channel_id=1, source_target_pairs={{0,1},{2,3},{1,0},{3,2},{4,5},{6,7},{5,4},{7,6},{8,9},{10,11},{9,8... | collective-permute-start | bytes 135176 | tf_op jit(solution)/shard_map/ppermute | solution.py:386

commit v11 on v10

--- a/solution.py
+++ b/solution.py
@@ -153,9 +153,7 @@
 
 
 def edge_kernel(two, gx, gy, own_ref, dec_ref, w_ref, halo_ref, e_ref, corner_ref, *refs):
-    *sides, next_hbm, p_ref, pc_ref, f_ref, next_wt, next_w, wt, rowbuf, x3, xc, yc, sem = refs
-    fetch = pltpu.make_async_copy(next_hbm, next_w, sem)
-    fetch.start()
+    *sides, p_ref, pc_ref, f_ref, wt, rowbuf, x3, xc, yc = refs
     frames, across, chan = own_ref.shape[0], *own_ref.shape[2:]
     height = e_ref.shape[0] if two else own_ref.shape[1]
     flip = mirrored(two)
@@ -253,8 +251,13 @@
     gap = (-2 * count - 8) % 16
     tail = [s[:, :chan], s[:, chan:]] + ([jnp.zeros((gap, chan), F32)] if gap else [])
     f_ref[base:, :] = jnp.concatenate(tail + [addends(decays, 8)], axis=0).astype(BF16)
-    fetch.wait()
-    pair_weights(next_w, next_wt, flip)
+
+
+def prepare_kernel(two, after_ref, w_hbm, wt, w_ref, sem):
+    copy = pltpu.make_async_copy(w_hbm, w_ref, sem)
+    copy.start()
+    copy.wait()
+    pair_weights(w_ref, wt, mirrored(two))
 
 
 def outer_kernel(two, ta, early, n_in, *refs):
@@ -477,32 +480,35 @@
             return jnp.where(t == 0, theirs + other * mine, mine + total * theirs).astype(BF16)
 
         across_two = [(0, 2), (2, 0), (1, 3), (3, 1)]
-        ga = joined(fa, ra)
+        ga = joined(fa[: rows_a * across], ra[: rows_a * across])
         za = lax.ppermute(ga, "ta", across_two)
         _, *sides = lax.optimization_barrier((ga, *sides))
 
     n_cols = (height // 2 + 1) * 4
     tail_rows = (2 * n_cols + 8 + 15) // 16 * 16
-    pb, pc, fb, wt_out = call(
+    pb, pc, fb = call(
         functools.partial(edge_kernel, two, gx, gy),
         (
             near_mem((rows_b, n_frames, across, chan), F32),
             near_mem((2, n_cols * n_frames, chan), F32),
             near_mem((rows_b * across + tail_rows, chan), BF16),
-            near_mem((12 * chan, 2 * chan), BF16),
         ),
         [
-            pltpu.VMEM(out_weight.shape, BF16), wt, rowbuf, pltpu.VMEM((2 * rows_b, cells, 3 * chan), BF16),
+            wt, rowbuf, pltpu.VMEM((2 * rows_b, cells, 3 * chan), BF16),
             pltpu.VMEM((n_cols * n_frames, 12 * chan), BF16), pltpu.VMEM((2, n_cols * n_frames, chan), F32),
-            pltpu.SemaphoreType.DMA,
         ],
-        flops * rows_b, [sent[1] if two else frames, decays, w_in, halo, cols, corner, *sides], [out_weight],
+        flops * rows_b, [sent[1] if two else frames, decays, w_in, halo, cols, corner, *sides],
     )
     if ta == 4:
         edges = [swapped(fb, "ta", ta, False), lax.ppermute(fb, "ta", across_two), swapped(fb, "ta", ta, True)]
     else:
         ra, rb = carry_general([fa, fb], total, ta)
         za, edges = ra, [rb] * 3
+
+    wt_out = call(
+        functools.partial(prepare_kernel, two), near_mem((12 * chan, 2 * chan), BF16),
+        [pltpu.VMEM(out_weight.shape, BF16), pltpu.SemaphoreType.DMA], 0, [fb], [out_weight],
+    )
 
     def last_kernel(early, near, far=()):
         return call(

time: 25.4 us -> 24.8 us (0.976)
  the two profiles are of different devices: /device:TPU:8 before, /device:TPU:0 now
where the time goes in v11:
time: 24.8 us; the launch traced here: 24.6 us
  starting transfers between devices  14.5 us (58%)
  Pallas kernels  8.82 us (36%)
  waiting for transfers between devices  1.04 us (4%)
    pallas_call x6, Pallas kernels, call(): pl.pallas_call(body, out_shape=outs, in_specs=[VMEM] * len(near) + [HBM]...  8.82 us
    ppermute x5, starting transfers between devices, swapped(): return lax.ppermute(value, axis, pairs + [(b, a) for a, b in pairs])  6.62 us
    ppermute x1, starting transfers between devices, on_device(): za = lax.ppermute(ga, 'ta', across_two)  3.1 us
    ppermute x1, starting transfers between devices, on_device(): corner = lax.ppermute(sent[0], 'gx', facing)  3 us
    ppermute x1, starting transfers between devices, on_device(): lax.ppermute(fb, 'ta', across_two)  1.68 us
    ppermute x5, waiting for transfers between devices, swapped(): return lax.ppermute(value, axis, pairs + [(b, a) for a, b in pairs])  1.03 us
  transfers between devices with their start and end apart: 9, of which 1 were waited for; matrix products, arithmetic and copies ran while one was open for 1% of the time, Pallas kernels for 30%

profile of v11, /device:TPU:0, one launch (start us, length us, event | category | flops | bytes accessed | tf_op | source)
XLA Modules:
  0.0 24.6 jit_solution(923220715127382972)
XLA Ops:
  0.0 1.3 %shard_map.46 = (bf16[8,8,64,128]{3,2,1,0:T(8,128)(2,1)S(1)}, f32[8,128]{1,0:T(8,128)S(1)}, bf16[3,3,128,128]{3,2,1,0:T(8,128)(2,1)S(1)}, bf16[8,32,128]{2,1,0:T...) custom-call(bf16[8,8,64,128]{3,2,1,0:T(8,128)(2,1)} %frames_hbm.1, ...), custom_call_target="tpu_custom_call" | custom-call | bytes 4194304 | tf_op jit(solution)/shard_map/pallas_call | solution.py:370
  1.3 3.0 %collective-permute-start.1 = (bf16[2,32,128]{2,1,0:T(8,128)(2,1)S(1)}, bf16[2,32,128]{2,1,0:T(8,128)(2,1)S(1)}, u32[]{:S(2)}, u32[]{:S(2)}) collective-permute-start(bf16[2,32,128]{2,1,0:T(8,128)(2,1)S(1)} %get-tuple-element.29), channel_id=1, source_target_pairs={{0,16},{16,0},{1,17},{17,1},{2,18},{18,2},{3,19},{19,3},{4,20},{20... | collective-permute-start | bytes 49160 | tf_op jit(solution)/shard_map/ppermute | solution.py:443
  4.3 0.1 collective-permute-start
  4.4 2.0 %shard_map.47 = (bf16[7,8,64,128]{3,2,1,0:T(8,128)(2,1)S(1)}, bf16[464,128]{1,0:T(8,128)(2,1)S(1)}) custom-call(bf16[8,8,64,128]{3,2,1,0:T(8,128)(2,1)S(1)} %get-tuple-element.22.frames_ref.refs_5_, f32[8,128]{1,0:T(8,128)S(1)} %get-tuple-element.23.dec_ref.refs_3_, bf16[3,3,128,128]{3,2,1,0:T(8,128)(2,1)S(1)} %get-tuple-element.24.w_ref), custom_call_target="tpu_custom_call" | custom-call | flops 1207959552 | bytes 4194304 | tf_op jit(solution)/shard_map/pallas_call | solution.py:370
  6.4 0.0 collective-permute-done.1.corner_ref
  6.5 2.1 %collective-permute-start.2 = (bf16[464,128]{1,0:T(8,128)(2,1)S(1)}, bf16[464,128]{1,0:T(8,128)(2,1)S(1)}, u32[]{:S(2)}, u32[]{:S(2)}) collective-permute-start(bf16[464,128]{1,0:T(8,128)(2,1)S(1)} %get-tuple-element.31), channel_id=1, source_target_pairs={{0,1},{2,3},{1,0},{3,2},{4,5},{6,7},{5,4},{7,6},{8,9},{10,11},{9,8... | collective-permute-start | bytes 356360 | tf_op jit(solution)/shard_map/ppermute | solution.py:389
  8.6 0.1 collective-permute-start.3
  8.7 1.7 %collective-permute-start.4 = (bf16[12,16,128]{2,1,0:T(8,128)(2,1)S(1)}, bf16[12,16,128]{2,1,0:T(8,128)(2,1)S(1)}, u32[]{:S(2)}, u32[]{:S(2)}) collective-permute-start(bf16[12,16,128]{2,1,0:T(8,128)(2,1)S(1)} %pad_maximum_fusion.1), channel_id=1, source_target_pairs={{4,8},{12,0},{8,4},{0,12},{5,9},{13,1},{9,5},{1,13},{6,10},{14,2},... | collective-permute-start | bytes 147464 | tf_op jit(solution)/shard_map/ppermute | solution.py:389
  10.4 1.0 %collective-permute-done.2.refs_6_ = bf16[464,128]{1,0:T(8,128)(2,1)S(1)} collective-permute-done((bf16[464,128]{1,0:T(8,128)(2,1)S(1)}, bf16[464,128]{1,0:T(8,128)(2,1)S(1)}, u32[]{:S(2)}, u32[]{:S(2)}) %collective-permute-start.2) | collective-permute-done | bytes 118816 | tf_op jit(solution)/shard_map/ppermute | solution.py:389
  11.4 0.1 fusion.1
  11.5 3.1 %collective-permute-start.8 = (bf16[448,128]{1,0:T(8,128)(2,1)S(1)}, bf16[448,128]{1,0:T(8,128)(2,1)S(1)}, u32[]{:S(2)}, u32[]{:S(2)}) collective-permute-start(bf16[448,128]{1,0:T(8,128)(2,1)S(1)} %fusion.1), channel_id=1, source_target_pairs={{0,2},{2,0},{1,3},{3,1},{4,6},{6,4},{5,7},{7,5},{8,10},{10,8},{9,1... | collective-permute-start | bytes 344072 | tf_op jit(solution)/shard_map/ppermute | solution.py:484
  14.6 0.0 collective-permute-done.3.refs_0_
  14.6 0.0 collective-permute-done.4.refs_1_
  14.6 0.0 collective-permute-done.halo_ref
  14.6 1.0 %shard_map.48 = (f32[2,8,64,128]{3,2,1,0:T(8,128)S(1)}, f32[2,160,128]{2,1,0:T(8,128)S(1)}, bf16[176,128]{1,0:T(8,128)(2,1)S(1)}) custom-call(bf16[8,2,64,128]{3,2,1,0:T(8,128)(2,1)S(1)} %get-tuple-element.26.own_ref, f32[8,128]{1,0:T(8,128)S(1)} %get-tuple-element.23.dec_ref.refs_3_, bf16[3,3,128,128]{3,2,1,0:T(8,128)(2,1)S(1)} %get-tuple-element.24.w_ref, ...), custom_call_target="tpu_custom_call" | custom-call | flops 301989888 | bytes 4194304 | tf_op jit(solution)/shard_map/pallas_call | solution.py:370
  15.6 1.4 %collective-permute-start.7 = (bf16[176,128]{1,0:T(8,128)(2,1)S(1)}, bf16[176,128]{1,0:T(8,128)(2,1)S(1)}, u32[]{:S(2)}, u32[]{:S(2)}) collective-permute-start(bf16[176,128]{1,0:T(8,128)(2,1)S(1)} %get-tuple-element.38.after_ref), channel_id=1, source_target_pairs={{1,2},{3,0},{2,1},{0,3},{5,6},{7,4},{6,5},{4,7},{9,10},{11,8},{10,... | collective-permute-start | bytes 135176 | tf_op jit(solution)/shard_map/ppermute | solution.py:389
  17.0 1.7 %collective-permute-start.6 = (bf16[176,128]{1,0:T(8,128)(2,1)S(1)}, bf16[176,128]{1,0:T(8,128)(2,1)S(1)}, u32[]{:S(2)}, u32[]{:S(2)}) collective-permute-start(bf16[176,128]{1,0:T(8,128)(2,1)S(1)} %get-tuple-element.38.after_ref), channel_id=1, source_target_pairs={{0,2},{2,0},{1,3},{3,1},{4,6},{6,4},{5,7},{7,5},{8,10},{10,8},{9,1... | collective-permute-start | bytes 135176 | tf_op jit(solution)/shard_map/ppermute | solution.py:503
  18.7 1.3 %collective-permute-start.5 = (bf16[176,128]{1,0:T(8,128)(2,1)S(1)}, bf16[176,128]{1,0:T(8,128)(2,1)S(1)}, u32[]{:S(2)}, u32[]{:S(2)}) collective-permute-start(bf16[176,128]{1,0:T(8,128)(2,1)S(1)} %get-tuple-element.38.after_ref), channel_id=1, source_target_pairs={{0,1},{2,3},{1,0},{3,2},{4,5},{6,7},{5,4},{7,6},{8,9},{10,11},{9,8... | collective-permute-start | bytes 135176 | tf_op jit(solution)/shard_map/ppermute | solution.py:389
  20.1 1.1 %shard_map.49.refs_4_ = bf16[1536,256]{1,0:T(8,128)(2,1)S(1)} custom-call(bf16[176,128]{1,0:T(8,128)(2,1)S(1)} %get-tuple-element.38.after_ref, bf16[3,3,128,128]{3,2,1,0:T(8,128)(2,1)} %w_hbm.3), custom_call_target="tpu_custom_call" | custom-call | bytes 4194304 | tf_op jit(solution)/shard_map/pallas_call | solution.py:370
  21.2 3.3 %shard_map.50.refs_11_ = bf16[8,8,64,128]{3,2,1,0:T(8,128)(2,1)} custom-call(bf16[7,8,64,128]{3,2,1,0:T(8,128)(2,1)S(1)} %get-tuple-element.25.refs_0_, f32[2,8,64,128]{3,2,1,0:T(8,128)S(1)} %get-tuple-element.36.refs_1_, f32[2,160,128]{2,1,0:T(8,128)S(1)} %get-tuple-element.37.refs_2_, f32[8,128]{1,0:T(8,128)S(1)} %get-tuple-element.23.dec_ref.refs_3_, ...), custom_call_target="tpu_custom_call" | custom-call | flops 1207959552 | bytes 4194304 | tf_op jit(solution)/shard_map/pallas_call | solution.py:370
  24.5 0.0 collective-permute-done.8.refs_10_
  24.5 0.0 collective-permute-done.7.refs_9_
  24.5 0.0 collective-permute-done.6.refs_8_
  24.5 0.0 collective-permute-done.5.refs_7_
  24.5 0.1 shard_map.51
  (5 shorter events, 0.1 us)
Async XLA Ops:
  1.3 5.1 %collective-permute-start.1 = (bf16[2,32,128]{2,1,0:T(8,128)(2,1)S(1)}, bf16[2,32,128]{2,1,0:T(8,128)(2,1)S(1)}, u32[]{:S(2)}, u32[]{:S(2)}) collective-permute-start(bf16[2,32,128]{2,1,0:T(8,128)(2,1)S(1)} %get-tuple-element.29), channel_id=1, source_target_pairs={{0,16},{16,0},{1,17},{17,1},{2,18},{18,2},{3,19},{19,3},{4,20},{20... | collective-permute-start | bytes 49160 | tf_op jit(solution)/shard_map/ppermute | solution.py:443
  4.3 10.2 %collective-permute-start = (bf16[8,2,64,128]{3,2,1,0:T(8,128)(2,1)S(1)}, bf16[8,2,64,128]{3,2,1,0:T(8,128)(2,1)S(1)}, u32[]{:S(2)}, u32[]{:S(2)}) collective-permute-start(bf16[8,2,64,128]{3,2,1,0:T(8,128)(2,1)S(1)} %get-tuple-element.26.own_ref), channel_id=1, source_target_pairs={{0,16},{16,0},{1,17},{17,1},{2,18},{18,2},{3,19},{19,3},{4,20},{20... | collective-permute-start | bytes 786440 | tf_op jit(solution)/shard_map/ppermute | solution.py:444
  6.5 4.9 %collective-permute-start.2 = (bf16[464,128]{1,0:T(8,128)(2,1)S(1)}, bf16[464,128]{1,0:T(8,128)(2,1)S(1)}, u32[]{:S(2)}, u32[]{:S(2)}) collective-permute-start(bf16[464,128]{1,0:T(8,128)(2,1)S(1)} %get-tuple-element.31), channel_id=1, source_target_pairs={{0,1},{2,3},{1,0},{3,2},{4,5},{6,7},{5,4},{7,6},{8,9},{10,11},{9,8... | collective-permute-start | bytes 356360 | tf_op jit(solution)/shard_map/ppermute | solution.py:389
  8.6 6.0 %collective-permute-start.3 = (bf16[12,16,128]{2,1,0:T(8,128)(2,1)S(1)}, bf16[12,16,128]{2,1,0:T(8,128)(2,1)S(1)}, u32[]{:S(2)}, u32[]{:S(2)}) collective-permute-start(bf16[12,16,128]{2,1,0:T(8,128)(2,1)S(1)} %pad_maximum_fusion), channel_id=1, source_target_pairs={{0,4},{8,12},{4,0},{12,8},{1,5},{9,13},{5,1},{13,9},{2,6},{10,14},... | collective-permute-start | bytes 147464 | tf_op jit(solution)/shard_map/ppermute | solution.py:389
  8.7 5.9 %collective-permute-start.4 = (bf16[12,16,128]{2,1,0:T(8,128)(2,1)S(1)}, bf16[12,16,128]{2,1,0:T(8,128)(2,1)S(1)}, u32[]{:S(2)}, u32[]{:S(2)}) collective-permute-start(bf16[12,16,128]{2,1,0:T(8,128)(2,1)S(1)} %pad_maximum_fusion.1), channel_id=1, source_target_pairs={{4,8},{12,0},{8,4},{0,12},{5,9},{13,1},{9,5},{1,13},{6,10},{14,2},... | collective-permute-start | bytes 147464 | tf_op jit(solution)/shard_map/ppermute | solution.py:389
  11.5 13.0 %collective-permute-start.8 = (bf16[448,128]{1,0:T(8,128)(2,1)S(1)}, bf16[448,128]{1,0:T(8,128)(2,1)S(1)}, u32[]{:S(2)}, u32[]{:S(2)}) collective-permute-start(bf16[448,128]{1,0:T(8,128)(2,1)S(1)} %fusion.1), channel_id=1, source_target_pairs={{0,2},{2,0},{1,3},{3,1},{4,6},{6,4},{5,7},{7,5},{8,10},{10,8},{9,1... | collective-permute-start | bytes 344072 | tf_op jit(solution)/shard_map/ppermute | solution.py:484
  15.6 8.9 %collective-permute-start.7 = (bf16[176,128]{1,0:T(8,128)(2,1)S(1)}, bf16[176,128]{1,0:T(8,128)(2,1)S(1)}, u32[]{:S(2)}, u32[]{:S(2)}) collective-permute-start(bf16[176,128]{1,0:T(8,128)(2,1)S(1)} %get-tuple-element.38.after_ref), channel_id=1, source_target_pairs={{1,2},{3,0},{2,1},{0,3},{5,6},{7,4},{6,5},{4,7},{9,10},{11,8},{10,... | collective-permute-start | bytes 135176 | tf_op jit(solution)/shard_map/ppermute | solution.py:389
  17.0 7.4 %collective-permute-start.6 = (bf16[176,128]{1,0:T(8,128)(2,1)S(1)}, bf16[176,128]{1,0:T(8,128)(2,1)S(1)}, u32[]{:S(2)}, u32[]{:S(2)}) collective-permute-start(bf16[176,128]{1,0:T(8,128)(2,1)S(1)} %get-tuple-element.38.after_ref), channel_id=1, source_target_pairs={{0,2},{2,0},{1,3},{3,1},{4,6},{6,4},{5,7},{7,5},{8,10},{10,8},{9,1... | collective-permute-start | bytes 135176 | tf_op jit(solution)/shard_map/ppermute | solution.py:503
  18.7 5.8 %collective-permute-start.5 = (bf16[176,128]{1,0:T(8,128)(2,1)S(1)}, bf16[176,128]{1,0:T(8,128)(2,1)S(1)}, u32[]{:S(2)}, u32[]{:S(2)}) collective-permute-start(bf16[176,128]{1,0:T(8,128)(2,1)S(1)} %get-tuple-element.38.after_ref), channel_id=1, source_target_pairs={{0,1},{2,3},{1,0},{3,2},{4,5},{6,7},{5,4},{7,6},{8,9},{10,11},{9,8... | collective-permute-start | bytes 135176 | tf_op jit(solution)/shard_map/ppermute | solution.py:389

commit v12 on v11

--- a/solution.py
+++ b/solution.py
@@ -227,7 +227,7 @@
 
     wide = jnp.dot(xc[...], wt[...], preferred_element_type=F32)
     for h in range(2):
-        yc[h] = wide[:, h * chan : (h + 1) * chan]
+        yc[h, 0 : wide.shape[0], :] = wide[:, h * chan : (h + 1) * chan]
     count = n_pairs * 4
     place = lax.broadcasted_iota(jnp.int32, (count, 2 * chan), 0)
     lane = lax.broadcasted_iota(jnp.int32, (count, 2 * chan), 1)
@@ -435,7 +435,7 @@
             near_mem(frames_far.shape, BF16), near_mem(decays_far.shape, F32), near_mem(in_weight.shape, BF16),
             near_mem((height, 4 * n_frames, chan), BF16), *sent,
         ],
-        [pltpu.VMEM((height * 4 * n_frames, chan), F32), pltpu.SemaphoreType.DMA((3,))],
+        [pltpu.VMEM(((height * 4 + 8) * n_frames, chan), F32), pltpu.SemaphoreType.DMA((3,))],
         0, [], [frames_far, decays_far, in_weight],
     )
     if two:
@@ -490,12 +490,12 @@
         functools.partial(edge_kernel, two, gx, gy),
         (
             near_mem((rows_b, n_frames, across, chan), F32),
-            near_mem((2, n_cols * n_frames, chan), F32),
+            near_mem((2, (n_cols + 7) // 8 * 8 * n_frames, chan), F32),
             near_mem((rows_b * across + tail_rows, chan), BF16),
         ),
         [
             wt, rowbuf, pltpu.VMEM((2 * rows_b, cells, 3 * chan), BF16),
-            pltpu.VMEM((n_cols * n_frames, 12 * chan), BF16), pltpu.VMEM((2, n_cols * n_frames, chan), F32),
+            pltpu.VMEM((n_cols * n_frames, 12 * chan), BF16), pltpu.VMEM((2, (n_cols + 7) // 8 * 8 * n_frames, chan), F32),
         ],
         flops * rows_b, [sent[1] if two else frames, decays, w_in, halo, cols, corner, *sides],
     )
@@ -516,7 +516,7 @@
             jax.ShapeDtypeStruct(frames.shape, BF16),
             [
                 rowbuf, pltpu.VMEM((height + 2, cells, 3 * chan), BF16),
-                pltpu.VMEM((n_frames, 2, (n_cols + 7) // 8 * 8, chan), F32),
+                pltpu.VMEM((n_frames, 2, (n_cols + 15) // 8 * 8, chan), F32),
                 pltpu.VMEM((rows_a * across, chan), F32), pltpu.VMEM((rows_b * across + tail_rows, chan), F32),
                 pltpu.VMEM((height, n_frames, across, chan), BF16), pltpu.SemaphoreType.DMA((height,)),
             ],

time: 24.8 us -> 24.8 us (level)
  no operation moved by 1% of the time
where the time goes in v12:
time: 24.8 us; the launch traced here: 24.6 us
  starting transfers between devices  14.5 us (58%)
  Pallas kernels  8.82 us (36%)
  waiting for transfers between devices  1.04 us (4%)
    pallas_call x6, Pallas kernels, call(): pl.pallas_call(body, out_shape=outs, in_specs=[VMEM] * len(near) + [HBM]...  8.82 us
    ppermute x5, starting transfers between devices, swapped(): return lax.ppermute(value, axis, pairs + [(b, a) for a, b in pairs])  6.62 us
    ppermute x1, starting transfers between devices, on_device(): za = lax.ppermute(ga, 'ta', across_two)  3.1 us
    ppermute x1, starting transfers between devices, on_device(): corner = lax.ppermute(sent[0], 'gx', facing)  3 us
    ppermute x1, starting transfers between devices, on_device(): lax.ppermute(fb, 'ta', across_two)  1.68 us
    ppermute x5, waiting for transfers between devices, swapped(): return lax.ppermute(value, axis, pairs + [(b, a) for a, b in pairs])  1.03 us
  transfers between devices with their start and end apart: 9, of which 1 were waited for; matrix products, arithmetic and copies ran while one was open for 1% of the time, Pallas kernels for 30%

profile of v12, /device:TPU:0, one launch (start us, length us, event | category | flops | bytes accessed | tf_op | source)
XLA Modules:
  0.0 24.6 jit_solution(3471736401430715875)
XLA Ops:
  0.0 1.3 %shard_map.46 = (bf16[8,8,64,128]{3,2,1,0:T(8,128)(2,1)S(1)}, f32[8,128]{1,0:T(8,128)S(1)}, bf16[3,3,128,128]{3,2,1,0:T(8,128)(2,1)S(1)}, bf16[8,32,128]{2,1,0:T...) custom-call(bf16[8,8,64,128]{3,2,1,0:T(8,128)(2,1)} %frames_hbm.1, ...), custom_call_target="tpu_custom_call" | custom-call | bytes 4194304 | tf_op jit(solution)/shard_map/pallas_call | solution.py:370
  1.3 3.0 %collective-permute-start.1 = (bf16[2,32,128]{2,1,0:T(8,128)(2,1)S(1)}, bf16[2,32,128]{2,1,0:T(8,128)(2,1)S(1)}, u32[]{:S(2)}, u32[]{:S(2)}) collective-permute-start(bf16[2,32,128]{2,1,0:T(8,128)(2,1)S(1)} %get-tuple-element.29), channel_id=1, source_target_pairs={{0,16},{16,0},{1,17},{17,1},{2,18},{18,2},{3,19},{19,3},{4,20},{20... | collective-permute-start | bytes 49160 | tf_op jit(solution)/shard_map/ppermute | solution.py:443
  4.3 0.1 collective-permute-start
  4.4 2.0 %shard_map.47 = (bf16[7,8,64,128]{3,2,1,0:T(8,128)(2,1)S(1)}, bf16[464,128]{1,0:T(8,128)(2,1)S(1)}) custom-call(bf16[8,8,64,128]{3,2,1,0:T(8,128)(2,1)S(1)} %get-tuple-element.22.frames_ref.refs_5_, f32[8,128]{1,0:T(8,128)S(1)} %get-tuple-element.23.dec_ref.refs_3_, bf16[3,3,128,128]{3,2,1,0:T(8,128)(2,1)S(1)} %get-tuple-element.24.w_ref), custom_call_target="tpu_custom_call" | custom-call | flops 1207959552 | bytes 4194304 | tf_op jit(solution)/shard_map/pallas_call | solution.py:370
  6.4 0.0 collective-permute-done.1.corner_ref
  6.5 2.1 %collective-permute-start.2 = (bf16[464,128]{1,0:T(8,128)(2,1)S(1)}, bf16[464,128]{1,0:T(8,128)(2,1)S(1)}, u32[]{:S(2)}, u32[]{:S(2)}) collective-permute-start(bf16[464,128]{1,0:T(8,128)(2,1)S(1)} %get-tuple-element.31), channel_id=1, source_target_pairs={{0,1},{2,3},{1,0},{3,2},{4,5},{6,7},{5,4},{7,6},{8,9},{10,11},{9,8... | collective-permute-start | bytes 356360 | tf_op jit(solution)/shard_map/ppermute | solution.py:389
  8.6 0.1 collective-permute-start.3
  8.7 1.7 %collective-permute-start.4 = (bf16[12,16,128]{2,1,0:T(8,128)(2,1)S(1)}, bf16[12,16,128]{2,1,0:T(8,128)(2,1)S(1)}, u32[]{:S(2)}, u32[]{:S(2)}) collective-permute-start(bf16[12,16,128]{2,1,0:T(8,128)(2,1)S(1)} %pad_maximum_fusion.1), channel_id=1, source_target_pairs={{4,8},{12,0},{8,4},{0,12},{5,9},{13,1},{9,5},{1,13},{6,10},{14,2},... | collective-permute-start | bytes 147464 | tf_op jit(solution)/shard_map/ppermute | solution.py:389
  10.4 1.0 %collective-permute-done.2.refs_6_ = bf16[464,128]{1,0:T(8,128)(2,1)S(1)} collective-permute-done((bf16[464,128]{1,0:T(8,128)(2,1)S(1)}, bf16[464,128]{1,0:T(8,128)(2,1)S(1)}, u32[]{:S(2)}, u32[]{:S(2)}) %collective-permute-start.2) | collective-permute-done | bytes 118816 | tf_op jit(solution)/shard_map/ppermute | solution.py:389
  11.4 0.1 fusion.1
  11.5 3.1 %collective-permute-start.8 = (bf16[448,128]{1,0:T(8,128)(2,1)S(1)}, bf16[448,128]{1,0:T(8,128)(2,1)S(1)}, u32[]{:S(2)}, u32[]{:S(2)}) collective-permute-start(bf16[448,128]{1,0:T(8,128)(2,1)S(1)} %fusion.1), channel_id=1, source_target_pairs={{0,2},{2,0},{1,3},{3,1},{4,6},{6,4},{5,7},{7,5},{8,10},{10,8},{9,1... | collective-permute-start | bytes 344072 | tf_op jit(solution)/shard_map/ppermute | solution.py:484
  14.6 0.0 collective-permute-done.3.refs_0_
  14.6 0.0 collective-permute-done.4.refs_1_
  14.6 0.0 collective-permute-done.halo_ref
  14.6 1.0 %shard_map.48 = (f32[2,8,64,128]{3,2,1,0:T(8,128)S(1)}, f32[2,192,128]{2,1,0:T(8,128)S(1)}, bf16[176,128]{1,0:T(8,128)(2,1)S(1)}) custom-call(bf16[8,2,64,128]{3,2,1,0:T(8,128)(2,1)S(1)} %get-tuple-element.26.own_ref, f32[8,128]{1,0:T(8,128)S(1)} %get-tuple-element.23.dec_ref.refs_3_, bf16[3,3,128,128]{3,2,1,0:T(8,128)(2,1)S(1)} %get-tuple-element.24.w_ref, ...), custom_call_target="tpu_custom_call" | custom-call | flops 301989888 | bytes 4194304 | tf_op jit(solution)/shard_map/pallas_call | solution.py:370
  15.6 1.4 %collective-permute-start.7 = (bf16[176,128]{1,0:T(8,128)(2,1)S(1)}, bf16[176,128]{1,0:T(8,128)(2,1)S(1)}, u32[]{:S(2)}, u32[]{:S(2)}) collective-permute-start(bf16[176,128]{1,0:T(8,128)(2,1)S(1)} %get-tuple-element.38.after_ref), channel_id=1, source_target_pairs={{1,2},{3,0},{2,1},{0,3},{5,6},{7,4},{6,5},{4,7},{9,10},{11,8},{10,... | collective-permute-start | bytes 135176 | tf_op jit(solution)/shard_map/ppermute | solution.py:389
  17.0 1.7 %collective-permute-start.6 = (bf16[176,128]{1,0:T(8,128)(2,1)S(1)}, bf16[176,128]{1,0:T(8,128)(2,1)S(1)}, u32[]{:S(2)}, u32[]{:S(2)}) collective-permute-start(bf16[176,128]{1,0:T(8,128)(2,1)S(1)} %get-tuple-element.38.after_ref), channel_id=1, source_target_pairs={{0,2},{2,0},{1,3},{3,1},{4,6},{6,4},{5,7},{7,5},{8,10},{10,8},{9,1... | collective-permute-start | bytes 135176 | tf_op jit(solution)/shard_map/ppermute | solution.py:503
  18.7 1.3 %collective-permute-start.5 = (bf16[176,128]{1,0:T(8,128)(2,1)S(1)}, bf16[176,128]{1,0:T(8,128)(2,1)S(1)}, u32[]{:S(2)}, u32[]{:S(2)}) collective-permute-start(bf16[176,128]{1,0:T(8,128)(2,1)S(1)} %get-tuple-element.38.after_ref), channel_id=1, source_target_pairs={{0,1},{2,3},{1,0},{3,2},{4,5},{6,7},{5,4},{7,6},{8,9},{10,11},{9,8... | collective-permute-start | bytes 135176 | tf_op jit(solution)/shard_map/ppermute | solution.py:389
  20.1 1.1 %shard_map.49.refs_4_ = bf16[1536,256]{1,0:T(8,128)(2,1)S(1)} custom-call(bf16[176,128]{1,0:T(8,128)(2,1)S(1)} %get-tuple-element.38.after_ref, bf16[3,3,128,128]{3,2,1,0:T(8,128)(2,1)} %w_hbm.3), custom_call_target="tpu_custom_call" | custom-call | bytes 4194304 | tf_op jit(solution)/shard_map/pallas_call | solution.py:370
  21.2 3.3 %shard_map.50.refs_11_ = bf16[8,8,64,128]{3,2,1,0:T(8,128)(2,1)} custom-call(bf16[7,8,64,128]{3,2,1,0:T(8,128)(2,1)S(1)} %get-tuple-element.25.refs_0_, f32[2,8,64,128]{3,2,1,0:T(8,128)S(1)} %get-tuple-element.36.refs_1_, f32[2,192,128]{2,1,0:T(8,128)S(1)} %get-tuple-element.37.refs_2_, f32[8,128]{1,0:T(8,128)S(1)} %get-tuple-element.23.dec_ref.refs_3_, ...), custom_call_target="tpu_custom_call" | custom-call | flops 1207959552 | bytes 4194304 | tf_op jit(solution)/shard_map/pallas_call | solution.py:370
  24.5 0.0 collective-permute-done.8.refs_10_
  24.5 0.0 collective-permute-done.7.refs_9_
  24.5 0.0 collective-permute-done.6.refs_8_
  24.5 0.0 collective-permute-done.5.refs_7_
  24.5 0.1 shard_map.51
  (5 shorter events, 0.1 us)
Async XLA Ops:
  1.3 5.1 %collective-permute-start.1 = (bf16[2,32,128]{2,1,0:T(8,128)(2,1)S(1)}, bf16[2,32,128]{2,1,0:T(8,128)(2,1)S(1)}, u32[]{:S(2)}, u32[]{:S(2)}) collective-permute-start(bf16[2,32,128]{2,1,0:T(8,128)(2,1)S(1)} %get-tuple-element.29), channel_id=1, source_target_pairs={{0,16},{16,0},{1,17},{17,1},{2,18},{18,2},{3,19},{19,3},{4,20},{20... | collective-permute-start | bytes 49160 | tf_op jit(solution)/shard_map/ppermute | solution.py:443
  4.3 10.2 %collective-permute-start = (bf16[8,2,64,128]{3,2,1,0:T(8,128)(2,1)S(1)}, bf16[8,2,64,128]{3,2,1,0:T(8,128)(2,1)S(1)}, u32[]{:S(2)}, u32[]{:S(2)}) collective-permute-start(bf16[8,2,64,128]{3,2,1,0:T(8,128)(2,1)S(1)} %get-tuple-element.26.own_ref), channel_id=1, source_target_pairs={{0,16},{16,0},{1,17},{17,1},{2,18},{18,2},{3,19},{19,3},{4,20},{20... | collective-permute-start | bytes 786440 | tf_op jit(solution)/shard_map/ppermute | solution.py:444
  6.5 4.9 %collective-permute-start.2 = (bf16[464,128]{1,0:T(8,128)(2,1)S(1)}, bf16[464,128]{1,0:T(8,128)(2,1)S(1)}, u32[]{:S(2)}, u32[]{:S(2)}) collective-permute-start(bf16[464,128]{1,0:T(8,128)(2,1)S(1)} %get-tuple-element.31), channel_id=1, source_target_pairs={{0,1},{2,3},{1,0},{3,2},{4,5},{6,7},{5,4},{7,6},{8,9},{10,11},{9,8... | collective-permute-start | bytes 356360 | tf_op jit(solution)/shard_map/ppermute | solution.py:389
  8.6 6.0 %collective-permute-start.3 = (bf16[12,16,128]{2,1,0:T(8,128)(2,1)S(1)}, bf16[12,16,128]{2,1,0:T(8,128)(2,1)S(1)}, u32[]{:S(2)}, u32[]{:S(2)}) collective-permute-start(bf16[12,16,128]{2,1,0:T(8,128)(2,1)S(1)} %pad_maximum_fusion), channel_id=1, source_target_pairs={{0,4},{8,12},{4,0},{12,8},{1,5},{9,13},{5,1},{13,9},{2,6},{10,14},... | collective-permute-start | bytes 147464 | tf_op jit(solution)/shard_map/ppermute | solution.py:389
  8.7 5.9 %collective-permute-start.4 = (bf16[12,16,128]{2,1,0:T(8,128)(2,1)S(1)}, bf16[12,16,128]{2,1,0:T(8,128)(2,1)S(1)}, u32[]{:S(2)}, u32[]{:S(2)}) collective-permute-start(bf16[12,16,128]{2,1,0:T(8,128)(2,1)S(1)} %pad_maximum_fusion.1), channel_id=1, source_target_pairs={{4,8},{12,0},{8,4},{0,12},{5,9},{13,1},{9,5},{1,13},{6,10},{14,2},... | collective-permute-start | bytes 147464 | tf_op jit(solution)/shard_map/ppermute | solution.py:389
  11.5 13.0 %collective-permute-start.8 = (bf16[448,128]{1,0:T(8,128)(2,1)S(1)}, bf16[448,128]{1,0:T(8,128)(2,1)S(1)}, u32[]{:S(2)}, u32[]{:S(2)}) collective-permute-start(bf16[448,128]{1,0:T(8,128)(2,1)S(1)} %fusion.1), channel_id=1, source_target_pairs={{0,2},{2,0},{1,3},{3,1},{4,6},{6,4},{5,7},{7,5},{8,10},{10,8},{9,1... | collective-permute-start | bytes 344072 | tf_op jit(solution)/shard_map/ppermute | solution.py:484
  15.6 8.9 %collective-permute-start.7 = (bf16[176,128]{1,0:T(8,128)(2,1)S(1)}, bf16[176,128]{1,0:T(8,128)(2,1)S(1)}, u32[]{:S(2)}, u32[]{:S(2)}) collective-permute-start(bf16[176,128]{1,0:T(8,128)(2,1)S(1)} %get-tuple-element.38.after_ref), channel_id=1, source_target_pairs={{1,2},{3,0},{2,1},{0,3},{5,6},{7,4},{6,5},{4,7},{9,10},{11,8},{10,... | collective-permute-start | bytes 135176 | tf_op jit(solution)/shard_map/ppermute | solution.py:389
  17.0 7.4 %collective-permute-start.6 = (bf16[176,128]{1,0:T(8,128)(2,1)S(1)}, bf16[176,128]{1,0:T(8,128)(2,1)S(1)}, u32[]{:S(2)}, u32[]{:S(2)}) collective-permute-start(bf16[176,128]{1,0:T(8,128)(2,1)S(1)} %get-tuple-element.38.after_ref), channel_id=1, source_target_pairs={{0,2},{2,0},{1,3},{3,1},{4,6},{6,4},{5,7},{7,5},{8,10},{10,8},{9,1... | collective-permute-start | bytes 135176 | tf_op jit(solution)/shard_map/ppermute | solution.py:503
  18.7 5.8 %collective-permute-start.5 = (bf16[176,128]{1,0:T(8,128)(2,1)S(1)}, bf16[176,128]{1,0:T(8,128)(2,1)S(1)}, u32[]{:S(2)}, u32[]{:S(2)}) collective-permute-start(bf16[176,128]{1,0:T(8,128)(2,1)S(1)} %get-tuple-element.38.after_ref), channel_id=1, source_target_pairs={{0,1},{2,3},{1,0},{3,2},{4,5},{6,7},{5,4},{7,6},{8,9},{10,11},{9,8... | collective-permute-start | bytes 135176 | tf_op jit(solution)/shard_map/ppermute | solution.py:389

commit v13 on v12

--- a/solution.py
+++ b/solution.py
@@ -137,7 +137,8 @@
         build(2 * p)
         build(2 * p + 1)
         slots = [r if r >= 0 else None for r in range(2 * p - 2, 2 * p + 2)]
-        y = pair_dot(x3, slots, wt)
+        half = frames // 2 * across
+        y = jnp.concatenate([pair_dot(x3, slots, wt, 0, half), pair_dot(x3, slots, wt, half, frames * across)])
         base = 2 * (p - first)
 
         def keep(rr, f, s, base=base):

time: 24.8 us -> 24.7 us (level)
  no operation moved by 1% of the time
where the time goes in v13:
time: 24.7 us; the launch traced here: 24.5 us
  starting transfers between devices  14.5 us (59%)
  Pallas kernels  8.75 us (35%)
  waiting for transfers between devices  1.04 us (4%)
    pallas_call x6, Pallas kernels, call(): pl.pallas_call(body, out_shape=outs, in_specs=[VMEM] * len(near) + [HBM]...  8.75 us
    ppermute x5, starting transfers between devices, swapped(): return lax.ppermute(value, axis, pairs + [(b, a) for a, b in pairs])  6.62 us
    ppermute x1, starting transfers between devices, on_device(): za = lax.ppermute(ga, 'ta', across_two)  3.1 us
    ppermute x1, starting transfers between devices, on_device(): corner = lax.ppermute(sent[0], 'gx', facing)  3 us
    ppermute x1, starting transfers between devices, on_device(): lax.ppermute(fb, 'ta', across_two)  1.69 us
    ppermute x5, waiting for transfers between devices, swapped(): return lax.ppermute(value, axis, pairs + [(b, a) for a, b in pairs])  1.03 us
  transfers between devices with their start and end apart: 9, of which 1 were waited for; matrix products, arithmetic and copies ran while one was open for 1% of the time, Pallas kernels for 30%

profile of v13, /device:TPU:0, one launch (start us, length us, event | category | flops | bytes accessed | tf_op | source)
XLA Modules:
  0.0 24.5 jit_solution(8096894274466633546)
XLA Ops:
  0.0 1.3 %shard_map.46 = (bf16[8,8,64,128]{3,2,1,0:T(8,128)(2,1)S(1)}, f32[8,128]{1,0:T(8,128)S(1)}, bf16[3,3,128,128]{3,2,1,0:T(8,128)(2,1)S(1)}, bf16[8,32,128]{2,1,0:T...) custom-call(bf16[8,8,64,128]{3,2,1,0:T(8,128)(2,1)} %frames_hbm.1, ...), custom_call_target="tpu_custom_call" | custom-call | bytes 4194304 | tf_op jit(solution)/shard_map/pallas_call | solution.py:371
  1.3 3.0 %collective-permute-start.1 = (bf16[2,32,128]{2,1,0:T(8,128)(2,1)S(1)}, bf16[2,32,128]{2,1,0:T(8,128)(2,1)S(1)}, u32[]{:S(2)}, u32[]{:S(2)}) collective-permute-start(bf16[2,32,128]{2,1,0:T(8,128)(2,1)S(1)} %get-tuple-element.29), channel_id=1, source_target_pairs={{0,16},{16,0},{1,17},{17,1},{2,18},{18,2},{3,19},{19,3},{4,20},{20... | collective-permute-start | bytes 49160 | tf_op jit(solution)/shard_map/ppermute | solution.py:444
  4.3 0.1 collective-permute-start
  4.4 1.9 %shard_map.47 = (bf16[7,8,64,128]{3,2,1,0:T(8,128)(2,1)S(1)}, bf16[464,128]{1,0:T(8,128)(2,1)S(1)}) custom-call(bf16[8,8,64,128]{3,2,1,0:T(8,128)(2,1)S(1)} %get-tuple-element.22.frames_ref.refs_5_, f32[8,128]{1,0:T(8,128)S(1)} %get-tuple-element.23.dec_ref.refs_3_, bf16[3,3,128,128]{3,2,1,0:T(8,128)(2,1)S(1)} %get-tuple-element.24.w_ref), custom_call_target="tpu_custom_call" | custom-call | flops 1207959552 | bytes 4194304 | tf_op jit(solution)/shard_map/pallas_call | solution.py:371
  6.4 0.0 collective-permute-done.1.corner_ref
  6.4 2.1 %collective-permute-start.2 = (bf16[464,128]{1,0:T(8,128)(2,1)S(1)}, bf16[464,128]{1,0:T(8,128)(2,1)S(1)}, u32[]{:S(2)}, u32[]{:S(2)}) collective-permute-start(bf16[464,128]{1,0:T(8,128)(2,1)S(1)} %get-tuple-element.31), channel_id=1, source_target_pairs={{0,1},{2,3},{1,0},{3,2},{4,5},{6,7},{5,4},{7,6},{8,9},{10,11},{9,8... | collective-permute-start | bytes 356360 | tf_op jit(solution)/shard_map/ppermute | solution.py:390
  8.5 0.1 collective-permute-start.3
  8.6 1.7 %collective-permute-start.4 = (bf16[12,16,128]{2,1,0:T(8,128)(2,1)S(1)}, bf16[12,16,128]{2,1,0:T(8,128)(2,1)S(1)}, u32[]{:S(2)}, u32[]{:S(2)}) collective-permute-start(bf16[12,16,128]{2,1,0:T(8,128)(2,1)S(1)} %pad_maximum_fusion.1), channel_id=1, source_target_pairs={{4,8},{12,0},{8,4},{0,12},{5,9},{13,1},{9,5},{1,13},{6,10},{14,2},... | collective-permute-start | bytes 147464 | tf_op jit(solution)/shard_map/ppermute | solution.py:390
  10.3 1.0 %collective-permute-done.2.refs_6_ = bf16[464,128]{1,0:T(8,128)(2,1)S(1)} collective-permute-done((bf16[464,128]{1,0:T(8,128)(2,1)S(1)}, bf16[464,128]{1,0:T(8,128)(2,1)S(1)}, u32[]{:S(2)}, u32[]{:S(2)}) %collective-permute-start.2) | collective-permute-done | bytes 118816 | tf_op jit(solution)/shard_map/ppermute | solution.py:390
  11.3 0.1 fusion.1
  11.4 3.1 %collective-permute-start.8 = (bf16[448,128]{1,0:T(8,128)(2,1)S(1)}, bf16[448,128]{1,0:T(8,128)(2,1)S(1)}, u32[]{:S(2)}, u32[]{:S(2)}) collective-permute-start(bf16[448,128]{1,0:T(8,128)(2,1)S(1)} %fusion.1), channel_id=1, source_target_pairs={{0,2},{2,0},{1,3},{3,1},{4,6},{6,4},{5,7},{7,5},{8,10},{10,8},{9,1... | collective-permute-start | bytes 344072 | tf_op jit(solution)/shard_map/ppermute | solution.py:485
  14.5 0.0 collective-permute-done.3.refs_0_
  14.5 0.0 collective-permute-done.4.refs_1_
  14.5 0.0 collective-permute-done.halo_ref
  14.5 1.0 %shard_map.48 = (f32[2,8,64,128]{3,2,1,0:T(8,128)S(1)}, f32[2,192,128]{2,1,0:T(8,128)S(1)}, bf16[176,128]{1,0:T(8,128)(2,1)S(1)}) custom-call(bf16[8,2,64,128]{3,2,1,0:T(8,128)(2,1)S(1)} %get-tuple-element.26.own_ref, f32[8,128]{1,0:T(8,128)S(1)} %get-tuple-element.23.dec_ref.refs_3_, bf16[3,3,128,128]{3,2,1,0:T(8,128)(2,1)S(1)} %get-tuple-element.24.w_ref, ...), custom_call_target="tpu_custom_call" | custom-call | flops 301989888 | bytes 4194304 | tf_op jit(solution)/shard_map/pallas_call | solution.py:371
  15.6 1.4 %collective-permute-start.7 = (bf16[176,128]{1,0:T(8,128)(2,1)S(1)}, bf16[176,128]{1,0:T(8,128)(2,1)S(1)}, u32[]{:S(2)}, u32[]{:S(2)}) collective-permute-start(bf16[176,128]{1,0:T(8,128)(2,1)S(1)} %get-tuple-element.38.after_ref), channel_id=1, source_target_pairs={{1,2},{3,0},{2,1},{0,3},{5,6},{7,4},{6,5},{4,7},{9,10},{11,8},{10,... | collective-permute-start | bytes 135176 | tf_op jit(solution)/shard_map/ppermute | solution.py:390
  17.0 1.7 %collective-permute-start.6 = (bf16[176,128]{1,0:T(8,128)(2,1)S(1)}, bf16[176,128]{1,0:T(8,128)(2,1)S(1)}, u32[]{:S(2)}, u32[]{:S(2)}) collective-permute-start(bf16[176,128]{1,0:T(8,128)(2,1)S(1)} %get-tuple-element.38.after_ref), channel_id=1, source_target_pairs={{0,2},{2,0},{1,3},{3,1},{4,6},{6,4},{5,7},{7,5},{8,10},{10,8},{9,1... | collective-permute-start | bytes 135176 | tf_op jit(solution)/shard_map/ppermute | solution.py:504
  18.7 1.4 %collective-permute-start.5 = (bf16[176,128]{1,0:T(8,128)(2,1)S(1)}, bf16[176,128]{1,0:T(8,128)(2,1)S(1)}, u32[]{:S(2)}, u32[]{:S(2)}) collective-permute-start(bf16[176,128]{1,0:T(8,128)(2,1)S(1)} %get-tuple-element.38.after_ref), channel_id=1, source_target_pairs={{0,1},{2,3},{1,0},{3,2},{4,5},{6,7},{5,4},{7,6},{8,9},{10,11},{9,8... | collective-permute-start | bytes 135176 | tf_op jit(solution)/shard_map/ppermute | solution.py:390
  20.0 1.1 %shard_map.49.refs_4_ = bf16[1536,256]{1,0:T(8,128)(2,1)S(1)} custom-call(bf16[176,128]{1,0:T(8,128)(2,1)S(1)} %get-tuple-element.38.after_ref, bf16[3,3,128,128]{3,2,1,0:T(8,128)(2,1)} %w_hbm.3), custom_call_target="tpu_custom_call" | custom-call | bytes 4194304 | tf_op jit(solution)/shard_map/pallas_call | solution.py:371
  21.1 3.3 %shard_map.50.refs_11_ = bf16[8,8,64,128]{3,2,1,0:T(8,128)(2,1)} custom-call(bf16[7,8,64,128]{3,2,1,0:T(8,128)(2,1)S(1)} %get-tuple-element.25.refs_0_, f32[2,8,64,128]{3,2,1,0:T(8,128)S(1)} %get-tuple-element.36.refs_1_, f32[2,192,128]{2,1,0:T(8,128)S(1)} %get-tuple-element.37.refs_2_, f32[8,128]{1,0:T(8,128)S(1)} %get-tuple-element.23.dec_ref.refs_3_, ...), custom_call_target="tpu_custom_call" | custom-call | flops 1207959552 | bytes 4194304 | tf_op jit(solution)/shard_map/pallas_call | solution.py:371
  24.4 0.0 collective-permute-done.8.refs_10_
  24.4 0.0 collective-permute-done.7.refs_9_
  24.4 0.0 collective-permute-done.6.refs_8_
  24.4 0.0 collective-permute-done.5.refs_7_
  24.4 0.1 shard_map.51
  (5 shorter events, 0.1 us)
Async XLA Ops:
  1.3 5.0 %collective-permute-start.1 = (bf16[2,32,128]{2,1,0:T(8,128)(2,1)S(1)}, bf16[2,32,128]{2,1,0:T(8,128)(2,1)S(1)}, u32[]{:S(2)}, u32[]{:S(2)}) collective-permute-start(bf16[2,32,128]{2,1,0:T(8,128)(2,1)S(1)} %get-tuple-element.29), channel_id=1, source_target_pairs={{0,16},{16,0},{1,17},{17,1},{2,18},{18,2},{3,19},{19,3},{4,20},{20... | collective-permute-start | bytes 49160 | tf_op jit(solution)/shard_map/ppermute | solution.py:444
  4.3 10.2 %collective-permute-start = (bf16[8,2,64,128]{3,2,1,0:T(8,128)(2,1)S(1)}, bf16[8,2,64,128]{3,2,1,0:T(8,128)(2,1)S(1)}, u32[]{:S(2)}, u32[]{:S(2)}) collective-permute-start(bf16[8,2,64,128]{3,2,1,0:T(8,128)(2,1)S(1)} %get-tuple-element.26.own_ref), channel_id=1, source_target_pairs={{0,16},{16,0},{1,17},{17,1},{2,18},{18,2},{3,19},{19,3},{4,20},{20... | collective-permute-start | bytes 786440 | tf_op jit(solution)/shard_map/ppermute | solution.py:445
  6.4 4.9 %collective-permute-start.2 = (bf16[464,128]{1,0:T(8,128)(2,1)S(1)}, bf16[464,128]{1,0:T(8,128)(2,1)S(1)}, u32[]{:S(2)}, u32[]{:S(2)}) collective-permute-start(bf16[464,128]{1,0:T(8,128)(2,1)S(1)} %get-tuple-element.31), channel_id=1, source_target_pairs={{0,1},{2,3},{1,0},{3,2},{4,5},{6,7},{5,4},{7,6},{8,9},{10,11},{9,8... | collective-permute-start | bytes 356360 | tf_op jit(solution)/shard_map/ppermute | solution.py:390
  8.5 6.0 %collective-permute-start.3 = (bf16[12,16,128]{2,1,0:T(8,128)(2,1)S(1)}, bf16[12,16,128]{2,1,0:T(8,128)(2,1)S(1)}, u32[]{:S(2)}, u32[]{:S(2)}) collective-permute-start(bf16[12,16,128]{2,1,0:T(8,128)(2,1)S(1)} %pad_maximum_fusion), channel_id=1, source_target_pairs={{0,4},{8,12},{4,0},{12,8},{1,5},{9,13},{5,1},{13,9},{2,6},{10,14},... | collective-permute-start | bytes 147464 | tf_op jit(solution)/shard_map/ppermute | solution.py:390
  8.6 5.9 %collective-permute-start.4 = (bf16[12,16,128]{2,1,0:T(8,128)(2,1)S(1)}, bf16[12,16,128]{2,1,0:T(8,128)(2,1)S(1)}, u32[]{:S(2)}, u32[]{:S(2)}) collective-permute-start(bf16[12,16,128]{2,1,0:T(8,128)(2,1)S(1)} %pad_maximum_fusion.1), channel_id=1, source_target_pairs={{4,8},{12,0},{8,4},{0,12},{5,9},{13,1},{9,5},{1,13},{6,10},{14,2},... | collective-permute-start | bytes 147464 | tf_op jit(solution)/shard_map/ppermute | solution.py:390
  11.4 13.0 %collective-permute-start.8 = (bf16[448,128]{1,0:T(8,128)(2,1)S(1)}, bf16[448,128]{1,0:T(8,128)(2,1)S(1)}, u32[]{:S(2)}, u32[]{:S(2)}) collective-permute-start(bf16[448,128]{1,0:T(8,128)(2,1)S(1)} %fusion.1), channel_id=1, source_target_pairs={{0,2},{2,0},{1,3},{3,1},{4,6},{6,4},{5,7},{7,5},{8,10},{10,8},{9,1... | collective-permute-start | bytes 344072 | tf_op jit(solution)/shard_map/ppermute | solution.py:485
  15.6 8.9 %collective-permute-start.7 = (bf16[176,128]{1,0:T(8,128)(2,1)S(1)}, bf16[176,128]{1,0:T(8,128)(2,1)S(1)}, u32[]{:S(2)}, u32[]{:S(2)}) collective-permute-start(bf16[176,128]{1,0:T(8,128)(2,1)S(1)} %get-tuple-element.38.after_ref), channel_id=1, source_target_pairs={{1,2},{3,0},{2,1},{0,3},{5,6},{7,4},{6,5},{4,7},{9,10},{11,8},{10,... | collective-permute-start | bytes 135176 | tf_op jit(solution)/shard_map/ppermute | solution.py:390
  17.0 7.4 %collective-permute-start.6 = (bf16[176,128]{1,0:T(8,128)(2,1)S(1)}, bf16[176,128]{1,0:T(8,128)(2,1)S(1)}, u32[]{:S(2)}, u32[]{:S(2)}) collective-permute-start(bf16[176,128]{1,0:T(8,128)(2,1)S(1)} %get-tuple-element.38.after_ref), channel_id=1, source_target_pairs={{0,2},{2,0},{1,3},{3,1},{4,6},{6,4},{5,7},{7,5},{8,10},{10,8},{9,1... | collective-permute-start | bytes 135176 | tf_op jit(solution)/shard_map/ppermute | solution.py:504
  18.7 5.8 %collective-permute-start.5 = (bf16[176,128]{1,0:T(8,128)(2,1)S(1)}, bf16[176,128]{1,0:T(8,128)(2,1)S(1)}, u32[]{:S(2)}, u32[]{:S(2)}) collective-permute-start(bf16[176,128]{1,0:T(8,128)(2,1)S(1)} %get-tuple-element.38.after_ref), channel_id=1, source_target_pairs={{0,1},{2,3},{1,0},{3,2},{4,5},{6,7},{5,4},{7,6},{8,9},{10,11},{9,8... | collective-permute-start | bytes 135176 | tf_op jit(solution)/shard_map/ppermute | solution.py:390
